TPU v7x, 32 devices: a whole 2x2x4 slice. The times are simulated.
32 devices in a mesh: pair: 8 (over z, y), aux: 4 (over x, core).
Axes of the slice: x: 2, y: 2, z: 4, core: 2. Of those that a mesh axis runs over, the one named last changes fastest.
Arguments:
- factors: bfloat16 [8, 8192, 8, 128], P('pair', 'aux'), may hold values from -0.0625 to 0.0625
- amplitudes: bfloat16 [48, 128, 128], P('pair'), may hold values from -20 to 20
- block_list: int32 [48, 3], P('pair'), may hold values from 0 to 7, as said below
- owner_map: int32 [8], replicated, may hold values from 0 to 7, as said below
Outputs:
- residual_blocks: bfloat16 [48, 128, 128], P('pair')
Inputs may be any that keep to these rules, and one draw needn't show every extreme that they name: `block_list`: each row (k, A, C) names an occupied orbital below 8 and two virtual blocks below 8; no row repeats. Among the 6 rows of one device at most 2 have orbitals with the same owner_map entry, and exactly 2 for some entry on every device. `owner_map`: A permutation: entry k is the row of factors that holds orbital k.
All inputs are finite; a program needn't handle non-finite values.
Results may differ from a plain program's by a relative error of at most 0.0046.
Values may be sent and summed in bfloat16 or wider, within the bound.
No kernel may reach another device: no remote copies, remote signals or barrier semaphores. Data moves between devices by JAX's collectives and lax.ppermute only.
A program may use at most 64 MiB of HBM per device.

v0:
```python
import jax
import jax.numpy as jnp
from jax import lax
from jax.sharding import PartitionSpec as P

CAP = 2


def on_device(factors, amplitudes, block_list, owner_map):
    pair_count = lax.axis_size("pair")
    slot_total = pair_count * CAP
    block_count = amplitudes.shape[0]
    block_width = amplitudes.shape[1]
    virt_blocks = factors.shape[2]
    share_rows = factors.shape[1]
    orbital_total = owner_map.shape[0]
    orbitals = block_list[:, 0]
    block_a = block_list[:, 1]
    block_c = block_list[:, 2]
    matches = orbitals[:, None] == lax.iota(jnp.int32, orbital_total)[None, :]
    owners = jnp.sum(jnp.where(matches, owner_map[None, :], 0), axis=1)
    owner_hits = (owners[:, None] == lax.iota(jnp.int32, pair_count)[None, :]).astype(jnp.int32)
    earlier = jnp.cumsum(owner_hits, axis=0) - owner_hits
    slot_rank = jnp.sum(earlier * owner_hits, axis=1)
    slots = owners * CAP + slot_rank
    placing = slots[:, None] == lax.iota(jnp.int32, slot_total)[None, :]
    place_matrix = placing.astype(jnp.bfloat16)
    flat_blocks = amplitudes.reshape(block_count, block_width * block_width)
    send_blocks = jnp.einsum(
        "js,jm->sm", place_matrix, flat_blocks, preferred_element_type=jnp.float32
    )
    send_blocks = send_blocks.astype(jnp.bfloat16).reshape(
        pair_count, CAP, block_width, block_width
    )
    send_a = jnp.sum(jnp.where(placing, block_a[:, None] + 1, 0), axis=0)
    send_c = jnp.sum(jnp.where(placing, block_c[:, None] + 1, 0), axis=0)
    send_index = (
        jnp.stack([send_a, send_c], axis=-1).astype(jnp.bfloat16).reshape(pair_count, CAP, 2)
    )
    recv_blocks, recv_index = (
        lax.all_to_all(send_blocks, "pair", split_axis=0, concat_axis=0, tiled=True),
        lax.all_to_all(send_index, "pair", split_axis=0, concat_axis=0, tiled=True),
    )
    recv_index = recv_index.reshape(slot_total, 2).astype(jnp.int32) - 1
    slot_a = recv_index[:, 0]
    slot_c = recv_index[:, 1]
    onehot_a = (slot_a[:, None] == lax.iota(jnp.int32, virt_blocks)[None, :]).astype(jnp.bfloat16)
    onehot_c = (slot_c[:, None] == lax.iota(jnp.int32, virt_blocks)[None, :]).astype(jnp.bfloat16)
    combined = (onehot_c[:, :, None] * onehot_a[:, None, :]).reshape(
        slot_total, virt_blocks * virt_blocks
    )
    recv_flat = recv_blocks.reshape(slot_total, block_width * block_width)
    weights = jnp.einsum("sm,sn->mn", combined, recv_flat, preferred_element_type=jnp.float32)
    weights = weights.reshape(virt_blocks, virt_blocks, block_width, block_width)
    weights = jnp.transpose(weights, (0, 3, 1, 2)).reshape(
        virt_blocks * block_width, virt_blocks * block_width
    )
    weights = weights.astype(jnp.bfloat16)
    factor_flat = factors.reshape(share_rows, virt_blocks * block_width)
    factor_rows = factor_flat
    inter_share = lax.psum_scatter(
        jnp.dot(factor_rows, weights, preferred_element_type=jnp.float32),
        "pair",
        scatter_dimension=0,
        tiled=True,
    )
    inter_share = inter_share.astype(jnp.bfloat16)
    shard_rows = lax.all_gather(inter_share, "pair", axis=0, tiled=True)
    height = shard_rows.shape[0]
    factor_rows = factor_flat
    left = shard_rows.reshape(height, virt_blocks, block_width)
    right = factor_rows.reshape(height, virt_blocks, block_width)
    projected = jnp.einsum("qAa,qCc->ACac", left, right, preferred_element_type=jnp.float32)
    safe_a = jnp.maximum(slot_a, 0)
    safe_c = jnp.maximum(slot_c, 0)
    summed = lax.psum(projected, "aux")
    picked = summed[safe_a, safe_c].astype(jnp.bfloat16)
    picked = picked.reshape(pair_count, CAP, block_width, block_width)
    returned = lax.all_to_all(picked, "pair", split_axis=0, concat_axis=0, tiled=True)
    returned = returned.reshape(slot_total, block_width * block_width)
    result = jnp.einsum("js,sm->jm", place_matrix, returned, preferred_element_type=jnp.float32)
    return result.astype(jnp.bfloat16).reshape(block_count, block_width, block_width)


def solution(mesh):
    placed = (P("pair", "aux", None, None), P("pair", None, None), P("pair", None), P())
    return jax.shard_map(
        on_device, mesh=mesh, in_specs=placed, out_specs=P("pair", None, None), check_vma=False
    )
```

profile of v0, /device:TPU:0, one launch (start us, length us, event | category | flops | bytes accessed | tf_op | source)
XLA Modules:
  0.0 392.5 jit_solution(6788591746998717793)
XLA Ops:
  6.5 0.8 add_bitcast_fusion
  7.3 0.8 select_reduce_fusion.3
  8.3 0.2 select_reduce_fusion.2
  8.8 0.6 copy.21
  9.4 7.3 %all-to-all-start = ((bf16[8,2,2]{1,2,0:T(2,128)(2,1)}), bf16[8,2,2]{1,2,0:T(2,128)(2,1)S(1)}, u32[]{:S(2)}, u32[]{:S(2)}) async-start(bf16[8,2,2]{1,2,0:T(2,128)(2,1)} %copy.21), calls=%async_computation | async-start | bytes 8192 | tf_op jit(solution)/shard_map/all_to_all | solution.py:42
  16.6 1.4 fusion.10
  18.0 0.9 copy.31
  18.9 4.1 %all-to-all-done = bf16[8,2,2]{1,2,0:T(2,128)(2,1)S(1)} async-done(((bf16[8,2,2]{1,2,0:T(2,128)(2,1)}), bf16[8,2,2]{1,2,0:T(2,128)(2,1)S(1)}, u32[]{:S(2)}, u32[]{:S(2)}) %all-to-all-start) | async-done | bytes 96 | tf_op jit(solution)/shard_map/all_to_all | solution.py:42
  23.0 3.5 all-to-all-start.1
  26.6 0.1 copy.22
  26.7 0.1 copy.23
  26.9 12.9 %all-to-all-done.1 = bf16[8,2,128,128]{3,2,1,0:T(8,128)(2,1)S(1)} async-done(((bf16[8,2,128,128]{3,2,1,0:T(8,128)(2,1)}), bf16[8,2,128,128]{3,2,1,0:T(8,128)(2,1)S(1)}, u32[]{:S(2)}, u32[]{:S(2)}) %all-to-all-start.1) | async-done | bytes 524320 | tf_op jit(solution)/shard_map/all_to_all | solution.py:41
  39.8 0.7 convert_bitcast_fusion
  40.5 3.3 copy.25
  43.8 10.6 %convolution_bitcast_fusion = f32[2048,1024]{0,1:T(8,128)} fusion(bf16[256,8,8,128]{3,2,1,0:T(8,128)(2,1)} %bitcast.94, bf16[128,8,8,128]{3,2,1,0:T(8,128)(2,1)} %bitcast.90), kind=kOutput, calls=%fused_computation.3 | convolution fusion | flops 4294967296 | bytes 14680064 | tf_op jit(solution)/shard_map/dot_general | solution.py:62
  54.4 148.6 %reduce-scatter.2.cloned.1.call-done = f32[256,1024]{0,1:T(8,128)} async-done(((f32[2048,1024]{0,1:T(8,128)}), f32[256,1024]{0,1:T(8,128)}) %reduce-scatter.2.cloned.1.call-update) | async-done | bytes 1048592 | tf_op jit(solution)/shard_map/reduce_scatter | solution.py:61
  203.0 2.1 convert_element_type.57
  205.1 74.2 %all-gather.2.cloned.1.call-done = bf16[2048,1024]{0,1:T(8,128)(2,1)} async-done(((bf16[256,1024]{0,1:T(8,128)(2,1)}), bf16[2048,1024]{0,1:T(8,128)(2,1)}) %all-gather.2.cloned.1.call-update) | async-done | bytes 4194320 | tf_op jit(solution)/shard_map/all_gather | solution.py:68
  279.3 9.9 %fusion.5 = f32[8,8,128,128]{3,2,1,0:T(8,128)} fusion(bf16[2048,8,128,1]{0,2,3,1:T(8,128)(2,1)} %bitcast.96, bf16[2048,8,128]{2,1,0:T(8,128)(2,1)} %bitcast.95), kind=kOutput, calls=%fused_computation.9 | convolution fusion | flops 4294967296 | bytes 12582912 | tf_op jit(solution)/shard_map/qAa,qCc->ACac/dot_general | solution.py:73
  289.2 76.3 %all-reduce.1 = bf16[8,8,128,128]{3,2,1,0:T(8,128)(2,1)S(1)} all-reduce(f32[8,8,128,128]{3,2,1,0:T(8,128)} %fusion.5), channel_id=1, replica_groups=mesh['pair'=8,'aux'=4] {'aux'}, use_global_device_ids=true, to_apply=%region_6.7 | all-reduce | flops 1048576 | bytes 6291456 | tf_op jit(solution)/shard_map/psum | solution.py:76
  365.5 0.7 gather_fusion
  366.2 18.4 %all_to_all.15 = bf16[8,2,128,128]{3,2,1,0:T(8,128)(2,1)S(1)} all-to-all(bf16[8,2,128,128]{3,2,1,0:T(8,128)(2,1)S(1)} %bitcast.91), channel_id=1, replica_groups=mesh['pair'=8,'aux'=4] {'pair'}, dimensions={0} | all-to-all | bytes 1048576 | tf_op jit(solution)/shard_map/all_to_all | solution.py:79
  384.6 0.4 fusion.11
  385.0 0.7 copy.67
  (17 shorter events, 0.6 us)
Async XLA Ops:
  9.4 13.7 %all-to-all-start = ((bf16[8,2,2]{1,2,0:T(2,128)(2,1)}), bf16[8,2,2]{1,2,0:T(2,128)(2,1)S(1)}, u32[]{:S(2)}, u32[]{:S(2)}) async-start(bf16[8,2,2]{1,2,0:T(2,128)(2,1)} %copy.21), calls=%async_computation | async-start | bytes 8192 | tf_op jit(solution)/shard_map/all_to_all | solution.py:42
  23.0 16.8 %all-to-all-start.1 = ((bf16[8,2,128,128]{3,2,1,0:T(8,128)(2,1)}), bf16[8,2,128,128]{3,2,1,0:T(8,128)(2,1)S(1)}, u32[]{:S(2)}, u32[]{:S(2)}) async-start(bf16[8,2,128,128]{3,2,1,0:T(8,128)(2,1)} %bitcast.35), calls=%async_computation.1 | async-start | bytes 1048576 | tf_op jit(solution)/shard_map/all_to_all | solution.py:41
  26.5 176.5 %reduce-scatter.2.cloned.1.call-start = ((), (), s32[]{:S(2)}) async-start(), calls=%async_computation.4 | async-start | bytes 9437184 | tf_op jit(solution)/shard_map/reduce_scatter | solution.py:61
  54.4 224.9 %all-gather.2.cloned.1.call-start = ((), (), s32[]{:S(2)}) async-start(), calls=%async_computation.5 | async-start | bytes 4718592 | tf_op jit(solution)/shard_map/all_gather | solution.py:68
Sparse Core Ops, SparseCore 0:
  54.5 148.4 reduce-scatter.1
  205.3 73.9 all-gather.1
where the time goes:
time: 393 us
  waiting for transfers between devices  240 us (61%)
  blocking collectives  94.7 us (24%)
  matrix products  23 us (6%)
  between operations  13.5 us (3%)
  starting transfers between devices  10.9 us (3%)
  local copies, waits for them, and re-layouts  6.56 us (2%)
  other arithmetic  4.13 us (1%)
    reduce_scatter x1, waiting for transfers between devices, on_device(): lax.psum_scatter(jnp.dot(factor_rows, weights, preferred_element_type=jnp...  149 us
    psum x1, blocking collectives, on_device(): summed = lax.psum(projected, 'aux')  76.3 us
    all_gather x1, waiting for transfers between devices, on_device(): shard_rows = lax.all_gather(inter_share, 'pair', axis=0, tiled=True)  74.2 us
    all_to_all x1, blocking collectives, on_device(): lax.all_to_all(picked, 'pair', split_axis=0, concat_axis=0, tiled=True)  18.4 us
    all_to_all x1, waiting for transfers between devices, on_device(): lax.all_to_all(send_blocks, 'pair', split_axis=0, concat_axis=0, tiled=True)  12.9 us
    dot_general x1, matrix products, on_device(): jnp.dot(factor_rows, weights, preferred_element_type=jnp.float32)  10.6 us
    dot_general x1, matrix products, on_device(): jnp.einsum('qAa,qCc->ACac', left, right, preferred_element_type=jnp.float32)  9.92 us
  transfers between devices with their start and end apart: 4, of which 4 were waited for; matrix products, arithmetic and copies ran while one was open for 1% of the time, Pallas kernels for 0%

commit v1 on v0

v1 whole, which is shorter than its diff:
```python
import jax
import jax.numpy as jnp
from jax import lax
from jax.experimental import pallas as pl
from jax.experimental.pallas import tpu as pltpu
from jax.sharding import PartitionSpec as P

RANKS = 2
GROUP = 48
META = 16
SMALL = 16
VMEM_BYTES = 40 * 1024 * 1024

SMEM_SPEC = pl.BlockSpec(memory_space=pltpu.SMEM)
VMEM_SPEC = pl.BlockSpec(memory_space=pltpu.VMEM)
PARAMS = pltpu.CompilerParams(vmem_limit_bytes=VMEM_BYTES)


def pack_kernel(slots, bits, place_ref, list_ref, owner_ref, blocks_ref, out_ref, pos_ref, meta_ref):
    group = place_ref[0]
    half = place_ref[1]
    count, width, depth = blocks_ref.shape
    rows = width // 2
    out_ref[...] = jnp.zeros_like(out_ref)
    meta_ref[...] = jnp.zeros_like(meta_ref)
    line = lax.broadcasted_iota(jnp.int32, meta_ref.shape[1:], 0)
    lane = lax.broadcasted_iota(jnp.int32, meta_ref.shape[1:], 1)

    def place(j, carry):
        owner = owner_ref[list_ref[j, 0]]

        def earlier(i, total):
            same = (owner_ref[list_ref[i, 0]] >> bits) == (owner >> bits)
            return total + same.astype(jnp.int32)

        slot = lax.fori_loop(0, j, earlier, jnp.int32(0))
        hop = (owner >> bits) ^ group
        pos_ref[j] = hop * slots + slot
        start = pl.multiple_of(slot * rows, rows)
        taken = pl.ds(pl.multiple_of(half * rows, rows), rows)
        out_ref[hop, pl.ds(start, rows), :] = blocks_ref[j, taken, :]
        is_line = line == slot
        old = meta_ref[hop]
        local = owner & ((1 << bits) - 1)
        for k, value in enumerate((list_ref[j, 1], list_ref[j, 2], local)):
            old = jnp.where(is_line & (lane == k), (value + 1).astype(jnp.float32), old)
        meta_ref[hop] = old
        return carry

    lax.fori_loop(0, count, place, 0)
    out_ref[:, pl.ds(slots * rows, META), :] = meta_ref[...].astype(out_ref.dtype)


def pack(place, block_list, owner_map, blocks, slots, bits, groups):
    count, width, depth = blocks.shape
    height = slots * (width // 2) + META
    return pl.pallas_call(
        lambda *refs: pack_kernel(slots, bits, *refs),
        out_shape=(
            jax.ShapeDtypeStruct((groups, height, depth), blocks.dtype),
            jax.ShapeDtypeStruct((count,), jnp.int32),
        ),
        in_specs=[SMEM_SPEC, SMEM_SPEC, SMEM_SPEC, VMEM_SPEC],
        out_specs=(VMEM_SPEC, SMEM_SPEC),
        scratch_shapes=[pltpu.VMEM((groups, META, depth), jnp.float32)],
        compiler_params=PARAMS,
        name="pack",
    )(place, block_list, owner_map, blocks)


def unpack_kernel(slots, where_ref, mine_ref, out_ref):
    step = pl.program_id(0)
    rows = out_ref.shape[1] // 2
    out_ref[...] = jnp.zeros_like(out_ref)
    for slot in range(slots):
        odd = where_ref[0, step * slots + slot] & 1
        there = pl.ds(pl.multiple_of(odd * rows, rows), rows)
        out_ref[slot, there, :] = mine_ref[0, slot * rows : (slot + 1) * rows, :]


def unpack(where, mine, slots):
    pairs, height, depth = mine.shape
    width = (height - META) // slots * 2
    return pl.pallas_call(
        lambda *refs: unpack_kernel(slots, *refs),
        grid=(pairs,),
        out_shape=jax.ShapeDtypeStruct((pairs * slots, width, depth), mine.dtype),
        in_specs=[SMEM_SPEC, pl.BlockSpec((1, height, depth), lambda i: (i, 0, 0))],
        out_specs=pl.BlockSpec((slots, width, depth), lambda i: (i, 0, 0)),
        compiler_params=PARAMS,
        name="unpack",
    )(where, mine)


def contract_kernel(group, where_ref, blocks_ref, factors_ref, out_ref, sent_ref):
    step = pl.program_id(0)

    @pl.when(step == 0)
    def _():
        out_ref[...] = jnp.zeros_like(out_ref)

    def one(i, carry):
        a = where_ref[0, step * group + i]

        @pl.when(a >= 0)
        def _():
            f = where_ref[1, step * group + i]
            out_ref[a >> 1] += lax.dot_general(
                factors_ref[f],
                blocks_ref[i],
                (((1,), (1,)), ((), ())),
                preferred_element_type=jnp.float32,
            )

        return carry

    lax.fori_loop(0, group, one, 0)

    @pl.when(step == pl.num_programs(0) - 1)
    def _():
        sent_ref[...] = out_ref[...].astype(sent_ref.dtype)


def contract(where, blocks, factors, virt):
    slots, width, depth = blocks.shape
    height = factors.shape[1]
    group = min(GROUP, slots)
    shape = (virt // 2, height, width)
    whole = pl.BlockSpec(shape, lambda i: (0, 0, 0))
    return pl.pallas_call(
        lambda *refs: contract_kernel(group, *refs),
        grid=(slots // group,),
        out_shape=(
            jax.ShapeDtypeStruct(shape, jnp.float32),
            jax.ShapeDtypeStruct(shape, jnp.bfloat16),
        ),
        in_specs=[
            SMEM_SPEC,
            pl.BlockSpec((group, width, depth), lambda i: (i, 0, 0)),
            pl.BlockSpec(factors.shape, lambda i: (0, 0, 0)),
        ],
        out_specs=(whole, whole),
        compiler_params=PARAMS,
        name="contract",
    )(where, blocks, factors)


def project_kernel(group, first, where_ref, own_ref, got_ref, factors_ref, *refs):
    out_ref, inter_ref = refs[-2:]
    step = pl.program_id(0)
    rows = out_ref.shape[1]

    @pl.when(step == 0)
    def _():
        whole = own_ref[...] + got_ref[...].astype(jnp.float32)
        inter_ref[...] = whole.astype(inter_ref.dtype)

    if first:
        out_ref[...] = jnp.zeros_like(out_ref)
    else:
        out_ref[...] = refs[0][...]

    def one(i, carry):
        a = where_ref[0, step * group + i]

        @pl.when(a >= 0)
        def _():
            f = where_ref[1, step * group + i]
            term = lax.dot_general(
                inter_ref[a >> 1],
                factors_ref[f],
                (((0,), (0,)), ((), ())),
                preferred_element_type=jnp.float32,
            )
            out_ref[i] += jnp.where((a & 1) == 0, term[:rows], term[rows:])

        return carry

    lax.fori_loop(0, group, one, 0)


def project(where, own, got, factors, so_far):
    slots = where.shape[1]
    width, depth = own.shape[2], factors.shape[2]
    group = min(GROUP, slots)
    first = so_far is None
    block = pl.BlockSpec((group, width // 2, depth), lambda i: (i, 0, 0))
    whole = pl.BlockSpec(own.shape, lambda i: (0, 0, 0))
    return pl.pallas_call(
        lambda *refs: project_kernel(group, first, *refs),
        grid=(slots // group,),
        out_shape=jax.ShapeDtypeStruct((slots, width // 2, depth), jnp.float32),
        in_specs=[SMEM_SPEC, whole, whole, pl.BlockSpec(factors.shape, lambda i: (0, 0, 0))]
        + ([] if first else [block]),
        out_specs=block,
        scratch_shapes=[pltpu.VMEM(own.shape, jnp.bfloat16)],
        input_output_aliases={} if first else {4: 0},
        compiler_params=PARAMS,
        name="project",
    )(where, own, got, factors, *([] if first else [so_far]))


def on_device(factors, amplitudes, block_list, owner_map):
    pairs = lax.axis_size("pair")
    shares = lax.axis_size("aux")
    small = pairs <= SMALL
    members = 4 if small else 2
    chunks = 4 if small else 1
    bits = members.bit_length() - 1
    groups = pairs // members
    wide = shares // 2
    me = lax.axis_index("pair")
    share = lax.axis_index("aux")
    local, team = me & (members - 1), me >> bits
    half, part = share & 1, share >> 1
    place = jnp.stack([team, half]).astype(jnp.int32)
    count, width, depth = amplitudes.shape
    virt = factors.shape[2]
    slots = min(RANKS * members, count)
    factors = factors[0]
    held_rows = factors.shape[0] // members
    chunk = held_rows // chunks

    def over_pair(value, distance):
        if distance == 0:
            return value
        return lax.ppermute(value, "pair", [(i, i ^ distance) for i in range(pairs)])

    def over_aux(value, distance):
        return lax.ppermute(value, "aux", [(i, i ^ distance) for i in range(shares)])

    def over_both(value, far, near):
        if (far, near) == (0, 0):
            return value
        route = [
            (i * shares + k, (i ^ far) * shares + (k ^ near))
            for i in range(pairs)
            for k in range(shares)
        ]
        return lax.ppermute(value, ("pair", "aux"), route)

    def trade(values, stride):
        if small:
            return jnp.stack([over_pair(values[i], i * stride) for i in range(pairs // stride)])
        order = lax.iota(jnp.int32, pairs // stride) ^ (me // stride)
        teams = [list(range(s, pairs, stride)) for s in range(stride)]
        got = lax.all_to_all(values[order], "pair", 0, 0, axis_index_groups=teams, tiled=True)
        return got[order]

    packed, positions = pack(place, block_list, owner_map, amplitudes, slots, bits, groups)
    if small:
        mine = jnp.stack([over_pair(packed[d >> bits], d) for d in range(pairs)])
    else:
        mine = trade(jnp.repeat(packed, members, axis=0), 1)
    rows = width // 2
    meta = mine[:, slots * rows : (slots + 0) * rows + slots, :3].astype(jnp.int32) - 1
    meta = meta.reshape(pairs * slots, 3)
    where = jnp.stack([meta[:, 0], (meta[:, 2] ^ local) * virt + meta[:, 1]])
    blocks = unpack(where, mine, slots)

    held = []
    for j in range(chunks):
        got = []
        for d in range(members):
            start = (local ^ d) * held_rows + j * chunk
            got.append(over_pair(lax.dynamic_slice_in_dim(factors, start, chunk, 0), d))
        got = jnp.stack(got)
        both = jnp.stack([got, over_aux(got, 1)], axis=1)
        both = jnp.transpose(both, (0, 3, 1, 2, 4))
        held.append(both.reshape(members * virt, 2 * chunk, depth))

    total = None
    for j in range(chunks):
        own, sent = contract(where, blocks, held[j], virt)
        got = over_pair(sent, members)
        stride = members * 2
        while stride < pairs:
            own = own + got.astype(jnp.float32)
            got = over_pair(own.astype(jnp.bfloat16), stride)
            stride *= 2
        total = project(where, own, got, held[j], total)

    quarter = rows // wide
    total = total.reshape(pairs // 2, 2, slots, wide, quarter, depth)
    summed = None
    for h in range(wide):
        piece = lax.dynamic_index_in_dim(total, part ^ h, 3, False)
        for y in range(2):
            value = piece[:, y]
            if (y, h) != (0, 0):
                value = over_both(value.astype(jnp.bfloat16), y, 2 * h).astype(jnp.float32)
            summed = value if summed is None else summed + value
    home = trade(summed.astype(jnp.bfloat16), 2).astype(jnp.float32)
    home = home.reshape(groups, members // 2, slots, quarter, depth)
    home = jnp.sum(home, axis=1).reshape(groups * slots, quarter, depth)
    result = home[positions].astype(jnp.bfloat16)
    pieces = jnp.stack([result] + [over_aux(result, a) for a in range(1, shares)])
    order = lax.iota(jnp.int32, shares)
    order = ((order % wide) * 2 + order // wide) ^ share
    return jnp.transpose(pieces[order], (1, 0, 2, 3)).reshape(count, width, depth)


def solution(mesh):
    placed = (P("pair", "aux", None, None), P("pair", None, None), P("pair", None), P())
    return jax.shard_map(
        on_device, mesh=mesh, in_specs=placed, out_specs=P("pair", None, None), check_vma=False
    )
```

time: 393 us -> 167 us (0.42)
  waiting for transfers between devices: 240 us -> 45.9 us
  blocking collectives: 94.7 us -> 0 us
  Pallas kernels: 0 us -> 50.6 us
  starting transfers between devices: 10.9 us -> 47.4 us
  matrix products: 23 us -> 0 us
  between operations: 13.5 us -> 0.48 us
  other arithmetic: 4.13 us -> 10.8 us
  local copies, waits for them, and re-layouts: 6.56 us -> 11.5 us
    reduce_scatter x1 -> x0, waiting for transfers between devices: 149 us -> none  [on_device(): lax.psum_scatter(jnp.dot(factor_rows, weights, preferred_element_type=jnp...]
    psum x1 -> x0, blocking collectives: 76.3 us -> none  [on_device(): summed = lax.psum(projected, 'aux')]
    all_gather x1 -> x0, waiting for transfers between devices: 74.2 us -> none  [on_device(): shard_rows = lax.all_gather(inter_share, 'pair', axis=0, tiled=True)]
    pallas_call x0 -> x10, Pallas kernels: none -> 50.6 us  [the longest x4 25.3 us: project(): pl.pallas_call(lambda *refs: project_kernel(group, first, *refs), grid=(s...]
    ppermute x0 -> x36, starting transfers between devices: none -> 47.4 us  [the longest x26 41.3 us: over_pair(): lax.ppermute(value, 'pair', [(i, i ^ distance) for i in range(pairs)])]
    ppermute x0 -> x36, waiting for transfers between devices: none -> 45.9 us  [the longest x26 34 us: over_pair(): lax.ppermute(value, 'pair', [(i, i ^ distance) for i in range(pairs)])]
    dot_general x5 -> x0, matrix products: 23 us -> none  [the longest x1 10.6 us: on_device(): jnp.dot(factor_rows, weights, preferred_element_type=jnp.float32)]
    all_to_all x1 -> x0, blocking collectives: 18.4 us -> none  [on_device(): lax.all_to_all(picked, 'pair', split_axis=0, concat_axis=0, tiled=True)]
  transfers between devices with their start and end apart: 4 -> 36, of which waited for: 4 -> 18; matrix products, arithmetic and copies ran while one was open for 1% -> 10% of each run, Pallas kernels for 0% -> 26%
where the time goes in v1:
time: 167 us
  Pallas kernels  50.6 us (30%)
  starting transfers between devices  47.4 us (28%)
  waiting for transfers between devices  45.9 us (27%)
  local copies, waits for them, and re-layouts  11.5 us (7%)
  other arithmetic  10.8 us (6%)
    ppermute x26, starting transfers between devices, over_pair(): lax.ppermute(value, 'pair', [(i, i ^ distance) for i in range(pairs)])  41.3 us
    ppermute x26, waiting for transfers between devices, over_pair(): lax.ppermute(value, 'pair', [(i, i ^ distance) for i in range(pairs)])  34 us
    pallas_call x4, Pallas kernels, project(): pl.pallas_call(lambda *refs: project_kernel(group, first, *refs), grid=(s...  25.3 us
    pallas_call x4, Pallas kernels, contract(): pl.pallas_call(lambda *refs: contract_kernel(group, *refs), grid=(slots /...  22.9 us
    ppermute x3, waiting for transfers between devices, over_both(): return lax.ppermute(value, ('pair', 'aux'), route)  8.49 us
    transpose x4, other arithmetic, on_device(): both = jnp.transpose(both, (0, 3, 1, 2, 4))  5.67 us
    another operation x4, other arithmetic, on_device(): both = jnp.stack([got, over_aux(got, 1)], axis=1)  4.77 us
    unnamed x37, local copies, waits for them, and re-layouts  4.13 us
  transfers between devices with their start and end apart: 36, of which 18 were waited for; matrix products, arithmetic and copies ran while one was open for 10% of the time, Pallas kernels for 26%

profile of v1, /device:TPU:0, one launch (start us, length us, event | category | flops | bytes accessed | tf_op | source)
XLA Modules:
  0.0 166.6 jit_solution(7419854479220791771)
XLA Ops:
  4.0 3.0 %collective-permute-start = (bf16[400,128]{1,0:T(8,128)(2,1)S(1)}, bf16[400,128]{1,0:T(8,128)(2,1)S(1)}, u32[]{:S(2)}, u32[]{:S(2)}) collective-permute-start(bf16[400,128]{1,0:T(8,128)(2,1)S(1)} %get-tuple-element.53), channel_id=1, source_target_pairs={{0,4},{4,0},{8,12},{12,8},{16,20},{20,16},{24,28},{28,24},{1,5},{5... | collective-permute-start | bytes 307208 | tf_op jit(solution)/shard_map/ppermute | solution.py:227
  8.6 3.0 %collective-permute-start.3 = (bf16[400,128]{1,0:T(8,128)(2,1)S(1)}, bf16[400,128]{1,0:T(8,128)(2,1)S(1)}, u32[]{:S(2)}, u32[]{:S(2)}) collective-permute-start(bf16[400,128]{1,0:T(8,128)(2,1)S(1)} %get-tuple-element.51), channel_id=1, source_target_pairs={{0,16},{4,20},{8,24},{12,28},{16,0},{20,4},{24,8},{28,12},{1,17},{... | collective-permute-start | bytes 307208 | tf_op jit(solution)/shard_map/ppermute | solution.py:227
  12.9 3.0 %constant_dynamic-slice_fusion.1 = (bf16[1,128,8,128]{3,2,1,0:T(8,128)(2,1)S(1)}, bf16[128,8,128]{2,1,0:T(8,128)(2,1)S(1)}, bf16[128,8,128]{2,1,0:T(8,128)(2,1)S...) fusion(bf16[1,2048,8,128]{3,2,1,0:T(8,128)(2,1)} %param.4, ...), kind=kLoop, calls=%fused_computation.52 | loop fusion | bytes 8388672 | tf_op jit(solution)/shard_map/dynamic_slice | solution.py:266
  15.8 3.7 %collective-permute-start.5 = (bf16[400,128]{1,0:T(8,128)(2,1)S(1)}, bf16[400,128]{1,0:T(8,128)(2,1)S(1)}, u32[]{:S(2)}, u32[]{:S(2)}) collective-permute-start(bf16[400,128]{1,0:T(8,128)(2,1)S(1)} %get-tuple-element.51), channel_id=1, source_target_pairs={{0,24},{4,28},{8,16},{12,20},{16,8},{20,12},{24,0},{28,4},{1,25},{... | collective-permute-start | bytes 307208 | tf_op jit(solution)/shard_map/ppermute | solution.py:227
  20.3 3.0 %collective-permute-start.24 = (bf16[128,8,128]{2,1,0:T(8,128)(2,1)S(1)}, bf16[128,8,128]{2,1,0:T(8,128)(2,1)S(1)}, u32[]{:S(2)}, u32[]{:S(2)}) collective-permute-start(bf16[128,8,128]{2,1,0:T(8,128)(2,1)S(1)} %get-tuple-element.39), channel_id=1, source_target_pairs={{0,12},{4,8},{8,4},{12,0},{16,28},{20,24},{24,20},{28,16},{1,13},{... | collective-permute-start | bytes 786440 | tf_op jit(solution)/shard_map/ppermute | solution.py:227
  26.2 3.2 %collective-permute-done.22 = bf16[128,8,128]{2,1,0:T(8,128)(2,1)S(1)} collective-permute-done((bf16[128,8,128]{2,1,0:T(8,128)(2,1)S(1)}, bf16[128,8,128]{2,1,0:T(8,128)(2,1)S(1)}, u32[]{:S(2)}, u32[]{:S(2)}) %collective-permute-start.22) | collective-permute-done | bytes 262176 | tf_op jit(solution)/shard_map/ppermute | solution.py:227
  31.9 4.3 %collective-permute-done.24 = bf16[128,8,128]{2,1,0:T(8,128)(2,1)S(1)} collective-permute-done((bf16[128,8,128]{2,1,0:T(8,128)(2,1)S(1)}, bf16[128,8,128]{2,1,0:T(8,128)(2,1)S(1)}, u32[]{:S(2)}, u32[]{:S(2)}) %collective-permute-start.24) | collective-permute-done | bytes 262176 | tf_op jit(solution)/shard_map/ppermute | solution.py:227
  36.5 4.0 %collective-permute-done.17 = bf16[128,8,128]{2,1,0:T(8,128)(2,1)S(1)} collective-permute-done((bf16[128,8,128]{2,1,0:T(8,128)(2,1)S(1)}, bf16[128,8,128]{2,1,0:T(8,128)(2,1)S(1)}, u32[]{:S(2)}, u32[]{:S(2)}) %collective-permute-start.17) | collective-permute-done | bytes 262176 | tf_op jit(solution)/shard_map/ppermute | solution.py:227
  44.0 3.6 %collective-permute-done.19 = bf16[128,8,128]{2,1,0:T(8,128)(2,1)S(1)} collective-permute-done((bf16[128,8,128]{2,1,0:T(8,128)(2,1)S(1)}, bf16[128,8,128]{2,1,0:T(8,128)(2,1)S(1)}, u32[]{:S(2)}, u32[]{:S(2)}) %collective-permute-start.19) | collective-permute-done | bytes 262176 | tf_op jit(solution)/shard_map/ppermute | solution.py:227
  51.2 7.1 %collective-permute-start.8 = (bf16[128,8,128]{2,1,0:T(8,128)(2,1)S(1)}, bf16[128,8,128]{2,1,0:T(8,128)(2,1)S(1)}, u32[]{:S(2)}, u32[]{:S(2)}) collective-permute-start(bf16[128,8,128]{2,1,0:T(8,128)(2,1)S(1)} %get-tuple-element.36), channel_id=1, source_target_pairs={{0,8},{4,12},{8,0},{12,4},{16,24},{20,28},{24,16},{28,20},{1,9},{5... | collective-permute-start | bytes 786440 | tf_op jit(solution)/shard_map/ppermute | solution.py:227
  65.8 5.7 %collective-permute-done.9 = bf16[128,8,128]{2,1,0:T(8,128)(2,1)S(1)} collective-permute-done((bf16[128,8,128]{2,1,0:T(8,128)(2,1)S(1)}, bf16[128,8,128]{2,1,0:T(8,128)(2,1)S(1)}, u32[]{:S(2)}, u32[]{:S(2)}) %collective-permute-start.9) | collective-permute-done | bytes 262176 | tf_op jit(solution)/shard_map/ppermute | solution.py:227
  76.3 5.7 %contract.7 = (f32[4,256,128]{2,1,0:T(8,128)S(1)}, bf16[4,256,128]{2,1,0:T(8,128)(2,1)}) custom-call(s32[2,48]{1,0:T(2,128)S(1)} %pad_add_fusion.refs_0_, bf16[48,128,128]{2,1,0:T(8,128)(2,1)S(1)} %unpack.1.refs_1_, bf16[32,256,128]{2,1,0:T(8,128)(2,1)S(1)} %bitcast.132), custom_call_target="tpu_custom_call" | custom-call | tf_op jit(solution)/shard_map/contract/pallas_call | solution.py:130
  84.0 5.7 %contract.6 = (f32[4,256,128]{2,1,0:T(8,128)S(1)}, bf16[4,256,128]{2,1,0:T(8,128)(2,1)}) custom-call(s32[2,48]{1,0:T(2,128)S(1)} %pad_add_fusion.refs_0_, bf16[48,128,128]{2,1,0:T(8,128)(2,1)S(1)} %unpack.1.refs_1_, bf16[32,256,128]{2,1,0:T(8,128)(2,1)S(1)} %bitcast.134), custom_call_target="tpu_custom_call" | custom-call | tf_op jit(solution)/shard_map/contract/pallas_call | solution.py:130
  89.7 2.9 %collective-permute-start.21 = (bf16[4,256,128]{2,1,0:T(8,128)(2,1)}, bf16[4,256,128]{2,1,0:T(8,128)(2,1)}, u32[]{:S(2)}, u32[]{:S(2)}) collective-permute-start(bf16[4,256,128]{2,1,0:T(8,128)(2,1)} %get-tuple-element.21), channel_id=1, source_target_pairs={{0,16},{4,20},{8,24},{12,28},{16,0},{20,4},{24,8},{28,12},{1,17},{... | collective-permute-start | bytes 786440 | tf_op jit(solution)/shard_map/ppermute | solution.py:227
  94.6 5.7 %contract.5 = (f32[4,256,128]{2,1,0:T(8,128)S(1)}, bf16[4,256,128]{2,1,0:T(8,128)(2,1)}) custom-call(s32[2,48]{1,0:T(2,128)S(1)} %pad_add_fusion.refs_0_, bf16[48,128,128]{2,1,0:T(8,128)(2,1)S(1)} %unpack.1.refs_1_, bf16[32,256,128]{2,1,0:T(8,128)(2,1)S(1)} %bitcast.136), custom_call_target="tpu_custom_call" | custom-call | tf_op jit(solution)/shard_map/contract/pallas_call | solution.py:130
  103.1 5.7 %contract.4 = (f32[4,256,128]{2,1,0:T(8,128)S(1)}, bf16[4,256,128]{2,1,0:T(8,128)(2,1)}) custom-call(s32[2,48]{1,0:T(2,128)S(1)} %pad_add_fusion.refs_0_, bf16[48,128,128]{2,1,0:T(8,128)(2,1)S(1)} %unpack.1.refs_1_, bf16[32,256,128]{2,1,0:T(8,128)(2,1)S(1)} %bitcast.138), custom_call_target="tpu_custom_call" | custom-call | tf_op jit(solution)/shard_map/contract/pallas_call | solution.py:130
  109.6 2.9 %collective-permute-start.11 = (bf16[4,256,128]{2,1,0:T(8,128)(2,1)}, bf16[4,256,128]{2,1,0:T(8,128)(2,1)}, u32[]{:S(2)}, u32[]{:S(2)}) collective-permute-start(bf16[4,256,128]{2,1,0:T(8,128)(2,1)} %get-tuple-element.17), channel_id=1, source_target_pairs={{0,16},{4,20},{8,24},{12,28},{16,0},{20,4},{24,8},{28,12},{1,17},{... | collective-permute-start | bytes 786440 | tf_op jit(solution)/shard_map/ppermute | solution.py:227
  112.6 5.8 %project.4.refs_4_ = f32[48,64,128]{2,1,0:T(8,128)S(1)} custom-call(s32[2,48]{1,0:T(2,128)S(1)} %pad_add_fusion.refs_0_, f32[4,256,128]{2,1,0:T(8,128)S(1)} %get-tuple-element.22.refs_1_, bf16[4,256,128]{2,1,0:T(8,128)(2,1)S(1)} %collective-permute-done.26.refs_2_, bf16[32,256,128]{2,1,0:T(8,128)(2,1)S(1)} %bitcast.133), custom_call_target="tpu_custom_call" | custom-call | tf_op jit(solution)/shard_map/project/pallas_call | solution.py:189
  118.5 6.5 %project.5.refs_4_ = f32[48,64,128]{2,1,0:T(8,128)S(1)} custom-call(s32[2,48]{1,0:T(2,128)S(1)} %pad_add_fusion.refs_0_, f32[4,256,128]{2,1,0:T(8,128)S(1)} %get-tuple-element.20.refs_1_, bf16[4,256,128]{2,1,0:T(8,128)(2,1)} %collective-permute-done.21.refs_2_, bf16[32,256,128]{2,1,0:T(8,128)(2,1)S(1)} %bitcast.135, ...), custom_call_target="tpu_custom_call", output_to_operand_aliasing={{}: (4, {})} | custom-call | tf_op jit(solution)/shard_map/project/pallas_call | solution.py:189
  125.8 6.5 %project.6.refs_4_ = f32[48,64,128]{2,1,0:T(8,128)S(1)} custom-call(s32[2,48]{1,0:T(2,128)S(1)} %pad_add_fusion.refs_0_, f32[4,256,128]{2,1,0:T(8,128)S(1)} %copy-done.7, bf16[4,256,128]{2,1,0:T(8,128)(2,1)} %collective-permute-done.16.refs_2_, bf16[32,256,128]{2,1,0:T(8,128)(2,1)S(1)} %bitcast.137, ...), custom_call_target="tpu_custom_call", output_to_operand_aliasing={{}: (4, {})} | custom-call | tf_op jit(solution)/shard_map/project/pallas_call | solution.py:189
  132.4 6.4 %project.7 = f32[48,64,128]{2,1,0:T(8,128)S(1)} custom-call(s32[2,48]{1,0:T(2,128)S(1)} %pad_add_fusion.refs_0_, f32[4,256,128]{2,1,0:T(8,128)S(1)} %copy-done.9, bf16[4,256,128]{2,1,0:T(8,128)(2,1)} %collective-permute-done.11.refs_2_, bf16[32,256,128]{2,1,0:T(8,128)(2,1)S(1)} %bitcast.139, ...), custom_call_target="tpu_custom_call", output_to_operand_aliasing={{}: (4, {})} | custom-call | tf_op jit(solution)/shard_map/project/pallas_call | solution.py:189
  142.6 3.1 %collective-permute-done.27 = bf16[4,6,32,128]{3,2,1,0:T(8,128)(2,1)S(1)} collective-permute-done((bf16[4,6,32,128]{3,2,1,0:T(8,128)(2,1)S(1)}, bf16[4,6,32,128]{3,2,1,0:T(8,128)(2,1)S(1)}, u32[]{:S(2)}, u32[]{:S(2)}) %collective-permute-start.27) | collective-permute-done | bytes 196640 | tf_op jit(solution)/shard_map/ppermute | solution.py:240
  146.9 4.2 %collective-permute-done.29 = bf16[4,6,32,128]{3,2,1,0:T(8,128)(2,1)S(1)} collective-permute-done((bf16[4,6,32,128]{3,2,1,0:T(8,128)(2,1)S(1)}, bf16[4,6,32,128]{3,2,1,0:T(8,128)(2,1)S(1)}, u32[]{:S(2)}, u32[]{:S(2)}) %collective-permute-start.29) | collective-permute-done | bytes 196640 | tf_op jit(solution)/shard_map/ppermute | solution.py:240
  156.5 2.8 %collective-permute-done.32 = bf16[6,32,128]{2,1,0:T(8,128)(2,1)S(1)} collective-permute-done((bf16[6,32,128]{2,1,0:T(8,128)(2,1)S(1)}, bf16[6,32,128]{2,1,0:T(8,128)(2,1)S(1)}, u32[]{:S(2)}, u32[]{:S(2)}) %collective-permute-start.32) | collective-permute-done | bytes 49184 | tf_op jit(solution)/shard_map/ppermute | solution.py:227
  (131 shorter events, 58.6 us)
Async XLA Ops:
  4.0 11.9 %collective-permute-start = (bf16[400,128]{1,0:T(8,128)(2,1)S(1)}, bf16[400,128]{1,0:T(8,128)(2,1)S(1)}, u32[]{:S(2)}, u32[]{:S(2)}) collective-permute-start(bf16[400,128]{1,0:T(8,128)(2,1)S(1)} %get-tuple-element.53), channel_id=1, source_target_pairs={{0,4},{4,0},{8,12},{12,8},{16,20},{20,16},{24,28},{28,24},{1,5},{5... | collective-permute-start | bytes 307208 | tf_op jit(solution)/shard_map/ppermute | solution.py:227
  7.0 12.5 %collective-permute-start.1 = (bf16[400,128]{1,0:T(8,128)(2,1)S(1)}, bf16[400,128]{1,0:T(8,128)(2,1)S(1)}, u32[]{:S(2)}, u32[]{:S(2)}) collective-permute-start(bf16[400,128]{1,0:T(8,128)(2,1)S(1)} %get-tuple-element.53), channel_id=1, source_target_pairs={{0,8},{4,12},{8,0},{12,4},{16,24},{20,28},{24,16},{28,20},{1,9},{5... | collective-permute-start | bytes 307208 | tf_op jit(solution)/shard_map/ppermute | solution.py:227
  8.6 11.5 %collective-permute-start.2 = (bf16[400,128]{1,0:T(8,128)(2,1)S(1)}, bf16[400,128]{1,0:T(8,128)(2,1)S(1)}, u32[]{:S(2)}, u32[]{:S(2)}) collective-permute-start(bf16[400,128]{1,0:T(8,128)(2,1)S(1)} %get-tuple-element.53), channel_id=1, source_target_pairs={{0,12},{4,8},{8,4},{12,0},{16,28},{20,24},{24,20},{28,16},{1,13},{... | collective-permute-start | bytes 307208 | tf_op jit(solution)/shard_map/ppermute | solution.py:227
  8.6 11.7 %collective-permute-start.3 = (bf16[400,128]{1,0:T(8,128)(2,1)S(1)}, bf16[400,128]{1,0:T(8,128)(2,1)S(1)}, u32[]{:S(2)}, u32[]{:S(2)}) collective-permute-start(bf16[400,128]{1,0:T(8,128)(2,1)S(1)} %get-tuple-element.51), channel_id=1, source_target_pairs={{0,16},{4,20},{8,24},{12,28},{16,0},{20,4},{24,8},{28,12},{1,17},{... | collective-permute-start | bytes 307208 | tf_op jit(solution)/shard_map/ppermute | solution.py:227
  11.6 13.6 %collective-permute-start.4 = (bf16[400,128]{1,0:T(8,128)(2,1)S(1)}, bf16[400,128]{1,0:T(8,128)(2,1)S(1)}, u32[]{:S(2)}, u32[]{:S(2)}) collective-permute-start(bf16[400,128]{1,0:T(8,128)(2,1)S(1)} %get-tuple-element.51), channel_id=1, source_target_pairs={{0,20},{4,16},{8,28},{12,24},{16,4},{20,0},{24,12},{28,8},{1,21},{... | collective-permute-start | bytes 307208 | tf_op jit(solution)/shard_map/ppermute | solution.py:227
  20.3 16.0 %collective-permute-start.24 = (bf16[128,8,128]{2,1,0:T(8,128)(2,1)S(1)}, bf16[128,8,128]{2,1,0:T(8,128)(2,1)S(1)}, u32[]{:S(2)}, u32[]{:S(2)}) collective-permute-start(bf16[128,8,128]{2,1,0:T(8,128)(2,1)S(1)} %get-tuple-element.39), channel_id=1, source_target_pairs={{0,12},{4,8},{8,4},{12,0},{16,28},{20,24},{24,20},{28,16},{1,13},{... | collective-permute-start | bytes 786440 | tf_op jit(solution)/shard_map/ppermute | solution.py:227
  25.1 15.4 %collective-permute-start.17 = (bf16[128,8,128]{2,1,0:T(8,128)(2,1)S(1)}, bf16[128,8,128]{2,1,0:T(8,128)(2,1)S(1)}, u32[]{:S(2)}, u32[]{:S(2)}) collective-permute-start(bf16[128,8,128]{2,1,0:T(8,128)(2,1)S(1)} %get-tuple-element.29), channel_id=1, source_target_pairs={{0,4},{4,0},{8,12},{12,8},{16,20},{20,16},{24,28},{28,24},{1,5},{5... | collective-permute-start | bytes 786440 | tf_op jit(solution)/shard_map/ppermute | solution.py:227
  25.9 15.8 %collective-permute-start.18 = (bf16[128,8,128]{2,1,0:T(8,128)(2,1)S(1)}, bf16[128,8,128]{2,1,0:T(8,128)(2,1)S(1)}, u32[]{:S(2)}, u32[]{:S(2)}) collective-permute-start(bf16[128,8,128]{2,1,0:T(8,128)(2,1)S(1)} %get-tuple-element.28), channel_id=1, source_target_pairs={{0,8},{4,12},{8,0},{12,4},{16,24},{20,28},{24,16},{28,20},{1,9},{5... | collective-permute-start | bytes 786440 | tf_op jit(solution)/shard_map/ppermute | solution.py:227
  29.3 18.2 %collective-permute-start.19 = (bf16[128,8,128]{2,1,0:T(8,128)(2,1)S(1)}, bf16[128,8,128]{2,1,0:T(8,128)(2,1)S(1)}, u32[]{:S(2)}, u32[]{:S(2)}) collective-permute-start(bf16[128,8,128]{2,1,0:T(8,128)(2,1)S(1)} %get-tuple-element.27), channel_id=1, source_target_pairs={{0,12},{4,8},{8,4},{12,0},{16,28},{20,24},{24,20},{28,16},{1,13},{... | collective-permute-start | bytes 786440 | tf_op jit(solution)/shard_map/ppermute | solution.py:227
  30.3 20.9 %collective-permute-start.12 = (bf16[128,8,128]{2,1,0:T(8,128)(2,1)S(1)}, bf16[128,8,128]{2,1,0:T(8,128)(2,1)S(1)}, u32[]{:S(2)}, u32[]{:S(2)}) collective-permute-start(bf16[128,8,128]{2,1,0:T(8,128)(2,1)S(1)} %get-tuple-element.33), channel_id=1, source_target_pairs={{0,4},{4,0},{8,12},{12,8},{16,20},{20,16},{24,28},{28,24},{1,5},{5... | collective-permute-start | bytes 786440 | tf_op jit(solution)/shard_map/ppermute | solution.py:227
  36.3 22.0 %collective-permute-start.13 = (bf16[128,8,128]{2,1,0:T(8,128)(2,1)S(1)}, bf16[128,8,128]{2,1,0:T(8,128)(2,1)S(1)}, u32[]{:S(2)}, u32[]{:S(2)}) collective-permute-start(bf16[128,8,128]{2,1,0:T(8,128)(2,1)S(1)} %get-tuple-element.32), channel_id=1, source_target_pairs={{0,8},{4,12},{8,0},{12,4},{16,24},{20,28},{24,16},{28,20},{1,9},{5... | collective-permute-start | bytes 786440 | tf_op jit(solution)/shard_map/ppermute | solution.py:227
  40.5 20.5 %collective-permute-start.14 = (bf16[128,8,128]{2,1,0:T(8,128)(2,1)S(1)}, bf16[128,8,128]{2,1,0:T(8,128)(2,1)S(1)}, u32[]{:S(2)}, u32[]{:S(2)}) collective-permute-start(bf16[128,8,128]{2,1,0:T(8,128)(2,1)S(1)} %get-tuple-element.31), channel_id=1, source_target_pairs={{0,12},{4,8},{8,4},{12,0},{16,28},{20,24},{24,20},{28,16},{1,13},{... | collective-permute-start | bytes 786440 | tf_op jit(solution)/shard_map/ppermute | solution.py:227
  41.7 20.9 %collective-permute-start.6 = (bf16[400,128]{1,0:T(8,128)(2,1)S(1)}, bf16[400,128]{1,0:T(8,128)(2,1)S(1)}, u32[]{:S(2)}, u32[]{:S(2)}) collective-permute-start(bf16[400,128]{1,0:T(8,128)(2,1)S(1)} %get-tuple-element.51), channel_id=1, source_target_pairs={{0,28},{4,24},{8,20},{12,16},{16,12},{20,8},{24,4},{28,0},{1,29},{... | collective-permute-start | bytes 307208 | tf_op jit(solution)/shard_map/ppermute | solution.py:227
  47.6 15.9 %collective-permute-start.7 = (bf16[128,8,128]{2,1,0:T(8,128)(2,1)S(1)}, bf16[128,8,128]{2,1,0:T(8,128)(2,1)S(1)}, u32[]{:S(2)}, u32[]{:S(2)}) collective-permute-start(bf16[128,8,128]{2,1,0:T(8,128)(2,1)S(1)} %get-tuple-element.37), channel_id=1, source_target_pairs={{0,4},{4,0},{8,12},{12,8},{16,20},{20,16},{24,28},{28,24},{1,5},{5... | collective-permute-start | bytes 786440 | tf_op jit(solution)/shard_map/ppermute | solution.py:227
  51.2 14.6 %collective-permute-start.8 = (bf16[128,8,128]{2,1,0:T(8,128)(2,1)S(1)}, bf16[128,8,128]{2,1,0:T(8,128)(2,1)S(1)}, u32[]{:S(2)}, u32[]{:S(2)}) collective-permute-start(bf16[128,8,128]{2,1,0:T(8,128)(2,1)S(1)} %get-tuple-element.36), channel_id=1, source_target_pairs={{0,8},{4,12},{8,0},{12,4},{16,24},{20,28},{24,16},{28,20},{1,9},{5... | collective-permute-start | bytes 786440 | tf_op jit(solution)/shard_map/ppermute | solution.py:227
  58.3 13.2 %collective-permute-start.9 = (bf16[128,8,128]{2,1,0:T(8,128)(2,1)S(1)}, bf16[128,8,128]{2,1,0:T(8,128)(2,1)S(1)}, u32[]{:S(2)}, u32[]{:S(2)}) collective-permute-start(bf16[128,8,128]{2,1,0:T(8,128)(2,1)S(1)} %get-tuple-element.35), channel_id=1, source_target_pairs={{0,12},{4,8},{8,4},{12,0},{16,28},{20,24},{24,20},{28,16},{1,13},{... | collective-permute-start | bytes 786440 | tf_op jit(solution)/shard_map/ppermute | solution.py:227
  61.0 13.3 %collective-permute-start.25 = (bf16[4,128,8,128]{3,2,1,0:T(8,128)(2,1)S(1)}, bf16[4,128,8,128]{3,2,1,0:T(8,128)(2,1)}, u32[]{:S(2)}, u32[]{:S(2)}) collective-permute-start(bf16[4,128,8,128]{3,2,1,0:T(8,128)(2,1)S(1)} %get-tuple-element.42), channel_id=1, source_target_pairs={{0,1},{1,0},{2,3},{3,2},{4,5},{5,4},{6,7},{7,6},{8,9},{9,8},{10,11... | collective-permute-start | bytes 3145736 | tf_op jit(solution)/shard_map/ppermute | solution.py:230
  62.6 19.4 %collective-permute-start.20 = (bf16[4,128,8,128]{3,2,1,0:T(8,128)(2,1)}, bf16[4,128,8,128]{3,2,1,0:T(8,128)(2,1)}, u32[]{:S(2)}, u32[]{:S(2)}) collective-permute-start(bf16[4,128,8,128]{3,2,1,0:T(8,128)(2,1)} %get-tuple-element.44), channel_id=1, source_target_pairs={{0,1},{1,0},{2,3},{3,2},{4,5},{5,4},{6,7},{7,6},{8,9},{9,8},{10,11... | collective-permute-start | bytes 3145736 | tf_op jit(solution)/shard_map/ppermute | solution.py:230
  63.5 29.1 %collective-permute-start.15 = (bf16[4,128,8,128]{3,2,1,0:T(8,128)(2,1)}, bf16[4,128,8,128]{3,2,1,0:T(8,128)(2,1)}, u32[]{:S(2)}, u32[]{:S(2)}) collective-permute-start(bf16[4,128,8,128]{3,2,1,0:T(8,128)(2,1)} %get-tuple-element.46), channel_id=1, source_target_pairs={{0,1},{1,0},{2,3},{3,2},{4,5},{5,4},{6,7},{7,6},{8,9},{9,8},{10,11... | collective-permute-start | bytes 3145736 | tf_op jit(solution)/shard_map/ppermute | solution.py:230
  73.0 28.1 %collective-permute-start.10 = (bf16[4,128,8,128]{3,2,1,0:T(8,128)(2,1)}, bf16[4,128,8,128]{3,2,1,0:T(8,128)(2,1)}, u32[]{:S(2)}, u32[]{:S(2)}) collective-permute-start(bf16[4,128,8,128]{3,2,1,0:T(8,128)(2,1)} %get-tuple-element.48), channel_id=1, source_target_pairs={{0,1},{1,0},{2,3},{3,2},{4,5},{5,4},{6,7},{7,6},{8,9},{9,8},{10,11... | collective-permute-start | bytes 3145736 | tf_op jit(solution)/shard_map/ppermute | solution.py:230
  82.0 30.6 %collective-permute-start.26 = (bf16[4,256,128]{2,1,0:T(8,128)(2,1)}, bf16[4,256,128]{2,1,0:T(8,128)(2,1)S(1)}, u32[]{:S(2)}, u32[]{:S(2)}) collective-permute-start(bf16[4,256,128]{2,1,0:T(8,128)(2,1)} %get-tuple-element.23), channel_id=1, source_target_pairs={{0,16},{4,20},{8,24},{12,28},{16,0},{20,4},{24,8},{28,12},{1,17},{... | collective-permute-start | bytes 786440 | tf_op jit(solution)/shard_map/ppermute | solution.py:227
  89.7 28.8 %collective-permute-start.21 = (bf16[4,256,128]{2,1,0:T(8,128)(2,1)}, bf16[4,256,128]{2,1,0:T(8,128)(2,1)}, u32[]{:S(2)}, u32[]{:S(2)}) collective-permute-start(bf16[4,256,128]{2,1,0:T(8,128)(2,1)} %get-tuple-element.21), channel_id=1, source_target_pairs={{0,16},{4,20},{8,24},{12,28},{16,0},{20,4},{24,8},{28,12},{1,17},{... | collective-permute-start | bytes 786440 | tf_op jit(solution)/shard_map/ppermute | solution.py:227
  101.2 24.6 %collective-permute-start.16 = (bf16[4,256,128]{2,1,0:T(8,128)(2,1)}, bf16[4,256,128]{2,1,0:T(8,128)(2,1)}, u32[]{:S(2)}, u32[]{:S(2)}) collective-permute-start(bf16[4,256,128]{2,1,0:T(8,128)(2,1)} %get-tuple-element.19), channel_id=1, source_target_pairs={{0,16},{4,20},{8,24},{12,28},{16,0},{20,4},{24,8},{28,12},{1,17},{... | collective-permute-start | bytes 786440 | tf_op jit(solution)/shard_map/ppermute | solution.py:227
  109.6 22.7 %collective-permute-start.11 = (bf16[4,256,128]{2,1,0:T(8,128)(2,1)}, bf16[4,256,128]{2,1,0:T(8,128)(2,1)}, u32[]{:S(2)}, u32[]{:S(2)}) collective-permute-start(bf16[4,256,128]{2,1,0:T(8,128)(2,1)} %get-tuple-element.17), channel_id=1, source_target_pairs={{0,16},{4,20},{8,24},{12,28},{16,0},{20,4},{24,8},{28,12},{1,17},{... | collective-permute-start | bytes 786440 | tf_op jit(solution)/shard_map/ppermute | solution.py:227
  (27 other events, 162.2 us)

commit v2 on v0

--- a/solution.py
+++ b/solution.py
@@ -1,12 +1,306 @@
 import jax
 import jax.numpy as jnp
 from jax import lax
+from jax.experimental import pallas as pl
+from jax.experimental.pallas import tpu as pltpu
 from jax.sharding import PartitionSpec as P
 
 CAP = 2
-
-
-def on_device(factors, amplitudes, block_list, owner_map):
+BATCH = 8
+META = 16
+MEMBERS = 4
+FULL = 2
+VMEM_BYTES = 48 * 1024 * 1024
+
+SMEM_SPEC = pl.BlockSpec(memory_space=pltpu.SMEM)
+VMEM_SPEC = pl.BlockSpec(memory_space=pltpu.VMEM)
+PARAMS = pltpu.CompilerParams(vmem_limit_bytes=VMEM_BYTES)
+COSTS = dict(pack=0, plan=10**13, contract=10**13, whole=0, project=0)
+
+
+def cost(name):
+    return pl.CostEstimate(flops=COSTS[name], bytes_accessed=0, transcendentals=0)
+
+
+def pack_kernel(place_ref, list_ref, owner_ref, blocks_ref, out_ref):
+    half = place_ref[1]
+    count, width, depth = blocks_ref.shape
+    rows = width // 2
+    line = lax.broadcasted_iota(jnp.int32, (META, depth), 0)
+    lane = lax.broadcasted_iota(jnp.int32, (META, depth), 1)
+    meta = jnp.zeros((META, depth), jnp.float32)
+    taken = pl.ds(pl.multiple_of(half * rows, rows), rows)
+    for j in range(count):
+        out_ref[j * rows : (j + 1) * rows, :] = blocks_ref[j, taken, :]
+        owner = owner_ref[list_ref[j, 0]]
+        for k, value in enumerate((list_ref[j, 1], list_ref[j, 2], owner)):
+            meta = jnp.where((line == j) & (lane == k), value.astype(jnp.float32), meta)
+    out_ref[pl.ds(count * rows, META), :] = meta.astype(out_ref.dtype)
+
+
+def pack(place, block_list, owner_map, blocks):
+    count, width, depth = blocks.shape
+    return pl.pallas_call(
+        pack_kernel,
+        out_shape=jax.ShapeDtypeStruct((count * (width // 2) + META, depth), blocks.dtype),
+        in_specs=[SMEM_SPEC, SMEM_SPEC, SMEM_SPEC, VMEM_SPEC],
+        out_specs=VMEM_SPEC,
+        compiler_params=PARAMS,
+        cost_estimate=cost("pack"),
+        name="pack",
+    )(place, block_list, owner_map, blocks)
+
+
+def plan_kernel(slots, owners, virt, meta_ref, out_ref):
+    total = meta_ref.shape[0]
+    room = total + BATCH
+
+    def one(s, filled):
+        owner = meta_ref[s, 2]
+        sender = lax.div(s, slots)
+        at = filled[0]
+        for m in range(1, owners):
+            at = jnp.where(owner == m, filled[m] + m * room, at)
+        out_ref[0, at] = sender
+        out_ref[1, at] = s - sender * slots
+        out_ref[2, at] = meta_ref[s, 0]
+        out_ref[3, at] = meta_ref[s, 1]
+        out_ref[4, at] = s
+        return tuple(n + (owner == m).astype(jnp.int32) for m, n in enumerate(filled))
+
+    filled = lax.fori_loop(0, total, one, (jnp.int32(0),) * owners)
+    for m, n in enumerate(filled):
+        for u in range(BATCH):
+            for k, value in enumerate((0, 0, virt, 0, total)):
+                out_ref[k, m * room + n + u] = jnp.int32(value)
+        out_ref[5, m] = lax.div(n + BATCH - 1, BATCH)
+
+
+def plan(meta, slots, owners, virt):
+    room = meta.shape[0] + BATCH
+    return pl.pallas_call(
+        lambda *refs: plan_kernel(slots, owners, virt, *refs),
+        out_shape=jax.ShapeDtypeStruct((6, owners * room), jnp.int32),
+        in_specs=[SMEM_SPEC],
+        out_specs=SMEM_SPEC,
+        cost_estimate=cost("plan"),
+        name="plan",
+    )(meta)
+
+
+def over_slots(plan_ref, owners, picks, step):
+    room = plan_ref.shape[1] // owners
+    for owner, ref in picks:
+
+        def batch(b, carry, owner=owner, ref=ref):
+            step(ref, owner * room + b * BATCH)
+            return carry
+
+        lax.fori_loop(0, plan_ref[5, owner], batch, 0)
+
+
+def add_blocks(plan_ref, blocks_ref, rows, sum_ref):
+    def step(factors_ref, first):
+        terms = []
+        for i in range(BATCH):
+            start = pl.multiple_of(plan_ref[1, first + i] * rows, rows)
+            terms.append(
+                lax.dot_general(
+                    blocks_ref[plan_ref[0, first + i], pl.ds(start, rows), :],
+                    factors_ref[plan_ref[3, first + i]],
+                    (((1,), (1,)), ((), ())),
+                    preferred_element_type=jnp.float32,
+                )
+            )
+        for i in range(BATCH):
+            sum_ref[plan_ref[2, first + i]] += terms[i]
+
+    return step
+
+
+def add_products(plan_ref, inter_ref, out_ref):
+    def step(factors_ref, first):
+        terms = []
+        for i in range(BATCH):
+            terms.append(
+                jnp.dot(
+                    inter_ref[plan_ref[2, first + i]],
+                    factors_ref[plan_ref[3, first + i]],
+                    preferred_element_type=jnp.float32,
+                )
+            )
+        for i in range(BATCH):
+            out_ref[plan_ref[4, first + i]] += terms[i]
+
+    return step
+
+
+def contract_kernel(owners, rows, place_ref, plan_ref, blocks_ref, *refs):
+    own_ref, sent_ref = refs[-2:]
+    own_ref[...] = jnp.zeros_like(own_ref)
+    picks = [(place_ref[0] ^ d, ref) for d, ref in enumerate(refs[:-2])]
+    over_slots(plan_ref, owners, picks, add_blocks(plan_ref, blocks_ref, rows, own_ref))
+    sent_ref[...] = own_ref[pl.ds(0, sent_ref.shape[0])].astype(sent_ref.dtype)
+
+
+def contract(place, listed, blocks, factors, owners, virt, rows):
+    chunk = factors[0].shape[1]
+    return pl.pallas_call(
+        lambda *refs: contract_kernel(owners, rows, *refs),
+        out_shape=(
+            jax.ShapeDtypeStruct((virt + 1, rows, chunk), jnp.float32),
+            jax.ShapeDtypeStruct((virt, rows, chunk), jnp.bfloat16),
+        ),
+        in_specs=[SMEM_SPEC] * 2 + [VMEM_SPEC] * (1 + len(factors)),
+        out_specs=(VMEM_SPEC, VMEM_SPEC),
+        compiler_params=PARAMS,
+        cost_estimate=cost("contract"),
+        name="contract",
+    )(place, listed, blocks, *factors)
+
+
+def whole_kernel(owners, rows, virt, plan_ref, blocks_ref, *refs):
+    out_ref, sum_ref, inter_ref = refs[-3:]
+    factors_ref = refs[0]
+    so_far = refs[1:-3]
+    out_ref[...] = so_far[0][...] if so_far else jnp.zeros_like(out_ref)
+    sum_ref[...] = jnp.zeros_like(sum_ref)
+    picks = [(k, factors_ref.at[pl.ds(k * virt, virt)]) for k in range(owners)]
+    over_slots(plan_ref, owners, picks, add_blocks(plan_ref, blocks_ref, rows, sum_ref))
+    inter_ref[...] = sum_ref[...].astype(inter_ref.dtype)
+    over_slots(plan_ref, owners, picks, add_products(plan_ref, inter_ref, out_ref))
+
+
+def whole(listed, blocks, factors, so_far, owners, virt, rows, total):
+    chunk, depth = factors.shape[1:]
+    so_far = [] if so_far is None else [so_far]
+    return pl.pallas_call(
+        lambda *refs: whole_kernel(owners, rows, virt, *refs),
+        out_shape=jax.ShapeDtypeStruct((total + 1, rows, depth), jnp.float32),
+        in_specs=[SMEM_SPEC] + [VMEM_SPEC] * (2 + len(so_far)),
+        out_specs=VMEM_SPEC,
+        scratch_shapes=[
+            pltpu.VMEM((virt + 1, rows, chunk), jnp.float32),
+            pltpu.VMEM((virt + 1, rows, chunk), jnp.bfloat16),
+        ],
+        compiler_params=PARAMS,
+        cost_estimate=cost("whole"),
+        name="whole",
+    )(listed, blocks, factors, *so_far)
+
+
+def project_kernel(owners, members, place_ref, plan_ref, own_ref, got_ref, so_far_ref, *refs):
+    out_ref, inter_ref = refs[-2:]
+    virt = got_ref.shape[0]
+    summed = own_ref[pl.ds(0, virt)] + got_ref[...].astype(jnp.float32)
+    inter_ref[pl.ds(0, virt)] = summed.astype(inter_ref.dtype)
+    inter_ref[virt] = jnp.zeros(inter_ref.shape[1:], inter_ref.dtype)
+    out_ref[...] = so_far_ref[...]
+    picks = [(place_ref[0] ^ d, ref) for d, ref in enumerate(refs[:members])]
+    over_slots(plan_ref, owners, picks, add_products(plan_ref, inter_ref, out_ref))
+
+
+def project(place, listed, own, got, factors, so_far, owners):
+    return pl.pallas_call(
+        lambda *refs: project_kernel(owners, len(factors), *refs),
+        out_shape=jax.ShapeDtypeStruct(so_far.shape, jnp.float32),
+        in_specs=[SMEM_SPEC] * 2 + [VMEM_SPEC] * (3 + len(factors)),
+        out_specs=VMEM_SPEC,
+        scratch_shapes=[pltpu.VMEM(own.shape, jnp.bfloat16)],
+        compiler_params=PARAMS,
+        cost_estimate=cost("project"),
+        name="project",
+    )(place, listed, own, got, so_far, *factors)
+
+
+def after(value, *others):
+    return lax.optimization_barrier((value, *others))[0]
+
+
+def near_plan(factors, amplitudes, block_list, owner_map):
+    pairs = lax.axis_size("pair")
+    shares = lax.axis_size("aux")
+    wide = shares // 2
+    me = lax.axis_index("pair")
+    share = lax.axis_index("aux")
+    half, part = share & 1, share >> 1
+    place = jnp.stack([me, half]).astype(jnp.int32)
+    slots, width, depth = amplitudes.shape
+    rows = width // 2
+    total = pairs * slots
+    virt = factors.shape[2]
+    factors = factors[0]
+    full_rows = factors.shape[0] // FULL
+    full_chunk = full_rows // pairs
+    chunk = (factors.shape[0] - full_rows) // MEMBERS
+
+    def over_pair(value, distance):
+        if distance == 0:
+            return value
+        return lax.ppermute(value, "pair", [(i, i ^ distance) for i in range(pairs)])
+
+    def over_aux(value, distance):
+        return lax.ppermute(value, "aux", [(i, i ^ distance) for i in range(shares)])
+
+    def over_both(value, far, near):
+        route = [
+            (i * shares + k, (i ^ far) * shares + (k ^ near))
+            for i in range(pairs)
+            for k in range(shares)
+        ]
+        return lax.ppermute(value, ("pair", "aux"), route)
+
+    full = factors[:full_rows].reshape(pairs, full_chunk, virt, depth)
+    full, turn = lax.optimization_barrier((full, me))
+    starts = [full_rows + ((turn & (MEMBERS - 1)) ^ d) * chunk for d in range(MEMBERS)]
+    pieces = [lax.dynamic_slice_in_dim(factors, start, chunk, 0) for start in starts]
+    pieces = [jnp.transpose(piece, (1, 0, 2)) for piece in pieces]
+    full = lax.all_to_all(full, "pair", 0, 0, tiled=True)
+
+    packed = pack(place, block_list, owner_map, after(amplitudes, turn))
+    near = jnp.stack([over_pair(packed, 2 * i) for i in range(pairs // 2)])
+    blocks = jnp.concatenate([near, over_pair(near, 1)])
+    meta = blocks[:, slots * rows : slots * rows + slots, :3].astype(jnp.int32)
+    listed = plan(meta.reshape(total, 3), slots, pairs, virt)
+
+    mine = [pieces[0]]
+    for d in range(1, MEMBERS):
+        mine.append(after(over_pair(pieces[d], d), blocks))
+    other = [over_aux(piece, 1) for piece in mine]
+    work = []
+    for held in (mine, other):
+        own, sent = contract(place, listed, blocks, held, pairs, virt, rows)
+        work.append((own, over_pair(sent, MEMBERS), held))
+    full = jnp.transpose(after(full, sent), (0, 2, 1, 3)).reshape(pairs * virt, full_chunk, depth)
+    out = None
+    for held in (full, over_aux(full, 1)):
+        out = whole(listed, blocks, held, out, pairs, virt, rows, total)
+    for own, got, held in work:
+        out = project(place, listed, own, got, held, out, pairs)
+
+    quarter = rows // wide
+    out = out[:total].reshape(2, pairs // 2, slots, wide, quarter, depth)
+    summed = None
+    for h in range(wide):
+        piece = lax.dynamic_index_in_dim(out, part ^ h, 3, False)
+        for y in range(2):
+            value = piece[y]
+            if (y, h) != (0, 0):
+                value = over_both(value.astype(jnp.bfloat16), y, 2 * h).astype(jnp.float32)
+            summed = value if summed is None else summed + value
+    summed = summed.astype(jnp.bfloat16)
+    home = None
+    for i in range(pairs // 2):
+        value = over_pair(summed[i], 2 * i).astype(jnp.float32)
+        home = value if home is None else home + value
+    result = home.astype(jnp.bfloat16)
+    quarters = jnp.stack([result] + [over_aux(result, a) for a in range(1, shares)])
+    order = lax.iota(jnp.int32, shares)
+    order = ((order % wide) * 2 + order // wide) ^ share
+    return jnp.transpose(quarters[order], (1, 0, 2, 3)).reshape(slots, width, depth)
+
+
+def far_plan(factors, amplitudes, block_list, owner_map):
     pair_count = lax.axis_size("pair")
     slot_total = pair_count * CAP
     block_count = amplitudes.shape[0]
@@ -84,6 +378,7 @@
 
 def solution(mesh):
     placed = (P("pair", "aux", None, None), P("pair", None, None), P("pair", None), P())
+    on_device = near_plan if mesh.shape["pair"] == 2 * MEMBERS else far_plan
     return jax.shard_map(
         on_device, mesh=mesh, in_specs=placed, out_specs=P("pair", None, None), check_vma=False
     )

time: 393 us -> 137 us (0.35)
  waiting for transfers between devices: 240 us -> 69.2 us
  blocking collectives: 94.7 us -> 0 us
  Pallas kernels: 0 us -> 26.7 us
  matrix products: 23 us -> 0 us
  starting transfers between devices: 10.9 us -> 30.7 us
  between operations: 13.5 us -> 0.35 us
    reduce_scatter x1 -> x0, waiting for transfers between devices: 149 us -> none  [on_device(): lax.psum_scatter(jnp.dot(factor_rows, weights, preferred_element_type=jnp...]
    psum x1 -> x0, blocking collectives: 76.3 us -> none  [on_device(): summed = lax.psum(projected, 'aux')]
    all_gather x1 -> x0, waiting for transfers between devices: 74.2 us -> none  [on_device(): shard_rows = lax.all_gather(inter_share, 'pair', axis=0, tiled=True)]
    ppermute x0 -> x23, waiting for transfers between devices: none -> 69.2 us  [the longest x12 57 us: over_pair(): lax.ppermute(value, 'pair', [(i, i ^ distance) for i in range(pairs)])]
    pallas_call x0 -> x8, Pallas kernels: none -> 26.7 us  [the longest x2 11.5 us: whole(): pl.pallas_call(lambda *refs: whole_kernel(owners, rows, virt, *refs), out...]
    ppermute x0 -> x23, starting transfers between devices: none -> 25.8 us  [the longest x12 18.6 us: over_pair(): lax.ppermute(value, 'pair', [(i, i ^ distance) for i in range(pairs)])]
    dot_general x5 -> x0, matrix products: 23 us -> none  [the longest x1 10.6 us: on_device(): jnp.dot(factor_rows, weights, preferred_element_type=jnp.float32)]
    all_to_all x1 -> x0, blocking collectives: 18.4 us -> none  [on_device(): lax.all_to_all(picked, 'pair', split_axis=0, concat_axis=0, tiled=True)]
  transfers between devices with their start and end apart: 4 -> 24, of which waited for: 4 -> 10; matrix products, arithmetic and copies ran while one was open for 1% -> 4% of each run, Pallas kernels for 0% -> 17%
where the time goes in v2:
time: 137 us
  waiting for transfers between devices  69.2 us (51%)
  starting transfers between devices  30.7 us (22%)
  Pallas kernels  26.7 us (19%)
  local copies, waits for them, and re-layouts  9.58 us (7%)
    ppermute x12, waiting for transfers between devices, over_pair(): lax.ppermute(value, 'pair', [(i, i ^ distance) for i in range(pairs)])  57 us
    ppermute x12, starting transfers between devices, over_pair(): lax.ppermute(value, 'pair', [(i, i ^ distance) for i in range(pairs)])  18.6 us
    pallas_call x2, Pallas kernels, whole(): pl.pallas_call(lambda *refs: whole_kernel(owners, rows, virt, *refs), out...  11.5 us
    ppermute x3, waiting for transfers between devices, over_both(): return lax.ppermute(value, ('pair', 'aux'), route)  8.8 us
    pallas_call x2, Pallas kernels, contract(): pl.pallas_call(lambda *refs: contract_kernel(owners, rows, *refs), out_sh...  5.75 us
    pallas_call x2, Pallas kernels, project(): pl.pallas_call(lambda *refs: project_kernel(owners, len(factors), *refs),...  5.28 us
    all_to_all x1, starting transfers between devices, near_plan(): full = lax.all_to_all(full, 'pair', 0, 0, tiled=True)  4.88 us
    ppermute x3, starting transfers between devices, over_both(): return lax.ppermute(value, ('pair', 'aux'), route)  4.19 us
  transfers between devices with their start and end apart: 24, of which 10 were waited for; matrix products, arithmetic and copies ran while one was open for 4% of the time, Pallas kernels for 17%

profile of v2, /device:TPU:0, one launch (start us, length us, event | category | flops | bytes accessed | tf_op | source)
XLA Modules:
  0.0 136.9 jit_solution(13388590027579815849)
XLA Ops:
  1.6 3.1 %collective-permute-start = (bf16[400,128]{1,0:T(8,128)(2,1)S(1)}, bf16[400,128]{1,0:T(8,128)(2,1)S(1)}, u32[]{:S(2)}, u32[]{:S(2)}) collective-permute-start(bf16[400,128]{1,0:T(8,128)(2,1)S(1)} %pack.1), channel_id=1, source_target_pairs={{0,8},{4,12},{8,0},{12,4},{16,24},{20,28},{24,16},{28,20},{1,9},{5... | collective-permute-start | bytes 307208 | tf_op jit(solution)/shard_map/ppermute | solution.py:240
  4.7 2.6 %collective-permute-start.1 = (bf16[400,128]{1,0:T(8,128)(2,1)S(1)}, bf16[400,128]{1,0:T(8,128)(2,1)S(1)}, u32[]{:S(2)}, u32[]{:S(2)}) collective-permute-start(bf16[400,128]{1,0:T(8,128)(2,1)S(1)} %pack.1), channel_id=1, source_target_pairs={{0,16},{4,20},{8,24},{12,28},{16,0},{20,4},{24,8},{28,12},{1,17},{... | collective-permute-start | bytes 307208 | tf_op jit(solution)/shard_map/ppermute | solution.py:240
  9.0 1.9 %collective-permute-start.9 = (bf16[8,256,128]{2,1,0:T(8,128)(2,1)S(1)}, bf16[8,256,128]{2,1,0:T(8,128)(2,1)}, u32[]{:S(2)}, u32[]{:S(2)}) collective-permute-start(bf16[8,256,128]{2,1,0:T(8,128)(2,1)S(1)} %bitcast.81), channel_id=1, source_target_pairs={{0,12},{4,8},{8,4},{12,0},{16,28},{20,24},{24,20},{28,16},{1,13},{... | collective-permute-start | bytes 1572872 | tf_op jit(solution)/shard_map/ppermute | solution.py:240
  14.3 4.9 %all-to-all-start = ((bf16[8,128,8,128]{3,1,2,0:T(8,128)(2,1)}), bf16[8,128,8,128]{3,1,2,0:T(8,128)(2,1)}, u32[]{:S(2)}, u32[]{:S(2)}) async-start(bf16[8,128,8,128]{3,1,2,0:T(8,128)(2,1)} %copy.32), calls=%async_computation | async-start | bytes 4194304 | tf_op jit(solution)/shard_map/all_to_all | solution.py:258
  20.2 2.0 %collective-permute-start.5 = (bf16[8,256,128]{2,1,0:T(8,128)(2,1)S(1)}, bf16[8,256,128]{2,1,0:T(8,128)(2,1)}, u32[]{:S(2)}, u32[]{:S(2)}) collective-permute-start(bf16[8,256,128]{2,1,0:T(8,128)(2,1)S(1)} %bitcast.82), channel_id=1, source_target_pairs={{0,4},{4,0},{8,12},{12,8},{16,20},{20,16},{24,28},{28,24},{1,5},{5... | collective-permute-start | bytes 1572872 | tf_op jit(solution)/shard_map/ppermute | solution.py:240
  22.5 44.5 %collective-permute-done.3 = bf16[4,400,128]{2,1,0:T(8,128)(2,1)S(1)} collective-permute-done((bf16[4,400,128]{2,1,0:T(8,128)(2,1)S(1)}, bf16[4,400,128]{2,1,0:T(8,128)(2,1)S(1)}, u32[]{:S(2)}, u32[]{:S(2)}) %collective-permute-start.3) | collective-permute-done | bytes 409632 | tf_op jit(solution)/shard_map/ppermute | solution.py:240
  69.3 3.5 %plan.1.refs_1_.refs_0_ = s32[6,448]{1,0:T(8,128)} custom-call(s32[48,3]{1,0:T(8,128)} %reshape.120.refs_0_), custom_call_target="tpu_custom_call" | custom-call | flops 9999999827968 | tf_op jit(solution)/shard_map/plan/pallas_call | solution.py:81
  73.6 2.9 %contract.2 = (f32[9,64,256]{2,1,0:T(8,128)S(1)}, bf16[8,64,256]{2,1,0:T(8,128)(2,1)S(1)}) custom-call(s32[2]{0:T(128)S(1)} %copy-done.6, s32[6,448]{1,0:T(8,128)S(1)} %copy-done.2, bf16[8,400,128]{2,1,0:T(8,128)(2,1)S(1)} %copy-done.1, bf16[8,256,128]{2,1,0:T(8,128)(2,1)} %collective-permute-done.4.refs_3_.refs_5_, ...), custom_call_target="tpu_custom_call" | custom-call | flops 9999999827968 | tf_op jit(solution)/shard_map/contract/pallas_call | solution.py:148
  77.0 2.9 %contract.3 = (f32[9,64,256]{2,1,0:T(8,128)S(1)}, bf16[8,64,256]{2,1,0:T(8,128)(2,1)S(1)}) custom-call(s32[2]{0:T(128)S(1)} %copy-done.6, s32[6,448]{1,0:T(8,128)S(1)} %copy-done.3, bf16[8,400,128]{2,1,0:T(8,128)(2,1)S(1)} %copy-done.1, bf16[8,256,128]{2,1,0:T(8,128)(2,1)} %bitcast.73.refs_3_.refs_5_, ...), custom_call_target="tpu_custom_call" | custom-call | flops 9999999827968 | tf_op jit(solution)/shard_map/contract/pallas_call | solution.py:148
  79.9 2.4 %collective-permute-start.12 = (bf16[8,64,256]{2,1,0:T(8,128)(2,1)S(1)}, bf16[8,64,256]{2,1,0:T(8,128)(2,1)S(1)}, u32[]{:S(2)}, u32[]{:S(2)}) collective-permute-start(bf16[8,64,256]{2,1,0:T(8,128)(2,1)S(1)} %get-tuple-element.24), channel_id=1, source_target_pairs={{0,16},{4,20},{8,24},{12,28},{16,0},{20,4},{24,8},{28,12},{1,17},{... | collective-permute-start | bytes 786440 | tf_op jit(solution)/shard_map/ppermute | solution.py:240
  82.9 5.8 %whole.2.refs_3_ = f32[49,64,128]{2,1,0:T(8,128)S(1)} custom-call(s32[6,448]{1,0:T(8,128)S(1)} %copy-done.3, bf16[8,400,128]{2,1,0:T(8,128)(2,1)S(1)} %copy-done.1, bf16[64,128,128]{2,1,0:T(8,128)(2,1)} %bitcast.17.refs_2_), custom_call_target="tpu_custom_call" | custom-call | tf_op jit(solution)/shard_map/whole/pallas_call | solution.py:177
  88.6 5.8 %whole.3.refs_4_ = f32[49,64,128]{2,1,0:T(8,128)S(1)} custom-call(s32[6,448]{1,0:T(8,128)S(1)} %copy-done.3, bf16[8,400,128]{2,1,0:T(8,128)(2,1)S(1)} %copy-done.1, bf16[64,128,128]{2,1,0:T(8,128)(2,1)} %collective-permute-done.13.refs_2_, f32[49,64,128]{2,1,0:T(8,128)S(1)} %whole.2.refs_3_), custom_call_target="tpu_custom_call" | custom-call | tf_op jit(solution)/shard_map/whole/pallas_call | solution.py:177
  94.4 6.8 %collective-permute-done.12.refs_3_ = bf16[8,64,256]{2,1,0:T(8,128)(2,1)S(1)} collective-permute-done((bf16[8,64,256]{2,1,0:T(8,128)(2,1)S(1)}, bf16[8,64,256]{2,1,0:T(8,128)(2,1)S(1)}, u32[]{:S(2)}, u32[]{:S(2)}) %collective-permute-start.12) | collective-permute-done | bytes 262176 | tf_op jit(solution)/shard_map/ppermute | solution.py:240
  101.2 2.6 %project.2.refs_4_ = f32[49,64,128]{2,1,0:T(8,128)S(1)} custom-call(s32[2]{0:T(128)S(1)} %copy-done.6, s32[6,448]{1,0:T(8,128)S(1)} %copy-done.3, f32[9,64,256]{2,1,0:T(8,128)S(1)} %get-tuple-element.23.refs_2_, bf16[8,64,256]{2,1,0:T(8,128)(2,1)S(1)} %collective-permute-done.12.refs_3_, f32[49,64,128]{2,1,0:T(8,128)S(1)} %whole.3.refs_4_, ...), custom_call_target="tpu_custom_call" | custom-call | tf_op jit(solution)/shard_map/project/pallas_call | solution.py:204
  103.9 2.1 %collective-permute-done.11.refs_3_ = bf16[8,64,256]{2,1,0:T(8,128)(2,1)S(1)} collective-permute-done((bf16[8,64,256]{2,1,0:T(8,128)(2,1)S(1)}, bf16[8,64,256]{2,1,0:T(8,128)(2,1)S(1)}, u32[]{:S(2)}, u32[]{:S(2)}) %collective-permute-start.11) | collective-permute-done | bytes 262176 | tf_op jit(solution)/shard_map/ppermute | solution.py:240
  106.0 2.6 %project.3 = f32[49,64,128]{2,1,0:T(8,128)S(1)} custom-call(s32[2]{0:T(128)S(1)} %copy-done.6, s32[6,448]{1,0:T(8,128)S(1)} %copy-done.3, f32[9,64,256]{2,1,0:T(8,128)S(1)} %get-tuple-element.21.refs_2_, bf16[8,64,256]{2,1,0:T(8,128)(2,1)S(1)} %collective-permute-done.11.refs_3_, f32[49,64,128]{2,1,0:T(8,128)S(1)} %project.2.refs_4_, ...), custom_call_target="tpu_custom_call" | custom-call | tf_op jit(solution)/shard_map/project/pallas_call | solution.py:204
  109.0 2.5 %collective-permute-start.14 = (bf16[4,6,32,128]{3,2,1,0:T(8,128)(2,1)S(1)}, bf16[4,6,32,128]{3,2,1,0:T(8,128)(2,1)S(1)}, u32[]{:S(2)}, u32[]{:S(2)}) collective-permute-start(bf16[4,6,32,128]{3,2,1,0:T(8,128)(2,1)S(1)} %fusion.4), channel_id=1, source_target_pairs={{0,4},{1,5},{2,6},{3,7},{4,0},{5,1},{6,2},{7,3},{8,12},{9,13},{10,... | collective-permute-start | bytes 589832 | tf_op jit(solution)/shard_map/ppermute | solution.py:251
  113.2 3.3 %collective-permute-done.14 = bf16[4,6,32,128]{3,2,1,0:T(8,128)(2,1)S(1)} collective-permute-done((bf16[4,6,32,128]{3,2,1,0:T(8,128)(2,1)S(1)}, bf16[4,6,32,128]{3,2,1,0:T(8,128)(2,1)S(1)}, u32[]{:S(2)}, u32[]{:S(2)}) %collective-permute-start.14) | collective-permute-done | bytes 196640 | tf_op jit(solution)/shard_map/ppermute | solution.py:251
  116.5 2.9 %collective-permute-done.15 = bf16[4,6,32,128]{3,2,1,0:T(8,128)(2,1)S(1)} collective-permute-done((bf16[4,6,32,128]{3,2,1,0:T(8,128)(2,1)S(1)}, bf16[4,6,32,128]{3,2,1,0:T(8,128)(2,1)S(1)}, u32[]{:S(2)}, u32[]{:S(2)}) %collective-permute-start.15) | collective-permute-done | bytes 196640 | tf_op jit(solution)/shard_map/ppermute | solution.py:251
  119.4 2.6 %collective-permute-done.16 = bf16[4,6,32,128]{3,2,1,0:T(8,128)(2,1)S(1)} collective-permute-done((bf16[4,6,32,128]{3,2,1,0:T(8,128)(2,1)S(1)}, bf16[4,6,32,128]{3,2,1,0:T(8,128)(2,1)S(1)}, u32[]{:S(2)}, u32[]{:S(2)}) %collective-permute-start.16) | collective-permute-done | bytes 196640 | tf_op jit(solution)/shard_map/ppermute | solution.py:251
  122.2 2.1 %collective-permute-start.18 = (bf16[6,32,128]{2,1,0:T(8,128)(2,1)S(1)}, bf16[6,32,128]{2,1,0:T(8,128)(2,1)S(1)}, u32[]{:S(2)}, u32[]{:S(2)}) collective-permute-start(bf16[6,32,128]{2,1,0:T(8,128)(2,1)S(1)} %get-tuple-element.33), channel_id=1, source_target_pairs={{0,16},{4,20},{8,24},{12,28},{16,0},{20,4},{24,8},{28,12},{1,17},{... | collective-permute-start | bytes 147464 | tf_op jit(solution)/shard_map/ppermute | solution.py:240
  124.3 2.3 %collective-permute-start.19 = (bf16[6,32,128]{2,1,0:T(8,128)(2,1)S(1)}, bf16[6,32,128]{2,1,0:T(8,128)(2,1)S(1)}, u32[]{:S(2)}, u32[]{:S(2)}) collective-permute-start(bf16[6,32,128]{2,1,0:T(8,128)(2,1)S(1)} %get-tuple-element.32), channel_id=1, source_target_pairs={{0,24},{4,28},{8,16},{12,20},{16,8},{20,12},{24,0},{28,4},{1,25},{... | collective-permute-start | bytes 147464 | tf_op jit(solution)/shard_map/ppermute | solution.py:240
  127.5 2.7 %collective-permute-done.19 = bf16[6,32,128]{2,1,0:T(8,128)(2,1)S(1)} collective-permute-done((bf16[6,32,128]{2,1,0:T(8,128)(2,1)S(1)}, bf16[6,32,128]{2,1,0:T(8,128)(2,1)S(1)}, u32[]{:S(2)}, u32[]{:S(2)}) %collective-permute-start.19) | collective-permute-done | bytes 49184 | tf_op jit(solution)/shard_map/ppermute | solution.py:240
  132.2 2.3 %collective-permute-done.21 = bf16[6,32,128]{2,1,0:T(8,128)(2,1)S(1)} collective-permute-done((bf16[6,32,128]{2,1,0:T(8,128)(2,1)S(1)}, bf16[6,32,128]{2,1,0:T(8,128)(2,1)S(1)}, u32[]{:S(2)}, u32[]{:S(2)}) %collective-permute-start.21) | collective-permute-done | bytes 49184 | tf_op jit(solution)/shard_map/ppermute | solution.py:243
  (83 shorter events, 19.5 us)
Async XLA Ops:
  1.6 18.6 %collective-permute-start = (bf16[400,128]{1,0:T(8,128)(2,1)S(1)}, bf16[400,128]{1,0:T(8,128)(2,1)S(1)}, u32[]{:S(2)}, u32[]{:S(2)}) collective-permute-start(bf16[400,128]{1,0:T(8,128)(2,1)S(1)} %pack.1), channel_id=1, source_target_pairs={{0,8},{4,12},{8,0},{12,4},{16,24},{20,28},{24,16},{28,20},{1,9},{5... | collective-permute-start | bytes 307208 | tf_op jit(solution)/shard_map/ppermute | solution.py:240
  4.7 17.5 %collective-permute-start.1 = (bf16[400,128]{1,0:T(8,128)(2,1)S(1)}, bf16[400,128]{1,0:T(8,128)(2,1)S(1)}, u32[]{:S(2)}, u32[]{:S(2)}) collective-permute-start(bf16[400,128]{1,0:T(8,128)(2,1)S(1)} %pack.1), channel_id=1, source_target_pairs={{0,16},{4,20},{8,24},{12,28},{16,0},{20,4},{24,8},{28,12},{1,17},{... | collective-permute-start | bytes 307208 | tf_op jit(solution)/shard_map/ppermute | solution.py:240
  7.3 15.0 %collective-permute-start.2 = (bf16[400,128]{1,0:T(8,128)(2,1)S(1)}, bf16[400,128]{1,0:T(8,128)(2,1)S(1)}, u32[]{:S(2)}, u32[]{:S(2)}) collective-permute-start(bf16[400,128]{1,0:T(8,128)(2,1)S(1)} %pack.1), channel_id=1, source_target_pairs={{0,24},{4,28},{8,16},{12,20},{16,8},{20,12},{24,0},{28,4},{1,25},{... | collective-permute-start | bytes 307208 | tf_op jit(solution)/shard_map/ppermute | solution.py:240
  9.0 59.6 %collective-permute-start.9 = (bf16[8,256,128]{2,1,0:T(8,128)(2,1)S(1)}, bf16[8,256,128]{2,1,0:T(8,128)(2,1)}, u32[]{:S(2)}, u32[]{:S(2)}) collective-permute-start(bf16[8,256,128]{2,1,0:T(8,128)(2,1)S(1)} %bitcast.81), channel_id=1, source_target_pairs={{0,12},{4,8},{8,4},{12,0},{16,28},{20,24},{24,20},{28,16},{1,13},{... | collective-permute-start | bytes 1572872 | tf_op jit(solution)/shard_map/ppermute | solution.py:240
  11.0 57.7 %collective-permute-start.7 = (bf16[8,256,128]{2,1,0:T(8,128)(2,1)S(1)}, bf16[8,256,128]{2,1,0:T(8,128)(2,1)}, u32[]{:S(2)}, u32[]{:S(2)}) collective-permute-start(bf16[8,256,128]{2,1,0:T(8,128)(2,1)S(1)} %bitcast.80), channel_id=1, source_target_pairs={{0,8},{4,12},{8,0},{12,4},{16,24},{20,28},{24,16},{28,20},{1,9},{5... | collective-permute-start | bytes 1572872 | tf_op jit(solution)/shard_map/ppermute | solution.py:240
  14.3 62.1 %all-to-all-start = ((bf16[8,128,8,128]{3,1,2,0:T(8,128)(2,1)}), bf16[8,128,8,128]{3,1,2,0:T(8,128)(2,1)}, u32[]{:S(2)}, u32[]{:S(2)}) async-start(bf16[8,128,8,128]{3,1,2,0:T(8,128)(2,1)} %copy.32), calls=%async_computation | async-start | bytes 4194304 | tf_op jit(solution)/shard_map/all_to_all | solution.py:258
  20.2 49.0 %collective-permute-start.5 = (bf16[8,256,128]{2,1,0:T(8,128)(2,1)S(1)}, bf16[8,256,128]{2,1,0:T(8,128)(2,1)}, u32[]{:S(2)}, u32[]{:S(2)}) collective-permute-start(bf16[8,256,128]{2,1,0:T(8,128)(2,1)S(1)} %bitcast.82), channel_id=1, source_target_pairs={{0,4},{4,0},{8,12},{12,8},{16,20},{20,16},{24,28},{28,24},{1,5},{5... | collective-permute-start | bytes 1572872 | tf_op jit(solution)/shard_map/ppermute | solution.py:240
  22.2 50.6 %collective-permute-start.4 = (bf16[8,256,128]{2,1,0:T(8,128)(2,1)}, bf16[8,256,128]{2,1,0:T(8,128)(2,1)}, u32[]{:S(2)}, u32[]{:S(2)}) collective-permute-start(bf16[8,256,128]{2,1,0:T(8,128)(2,1)} %bitcast.73.refs_3_.refs_5_), channel_id=1, source_target_pairs={{0,1},{1,0},{2,3},{3,2},{4,5},{5,4},{6,7},{7,6},{8,9},{9,8},{10,11... | collective-permute-start | bytes 1572872 | tf_op jit(solution)/shard_map/ppermute | solution.py:243
  22.3 44.7 %collective-permute-start.3 = (bf16[4,400,128]{2,1,0:T(8,128)(2,1)S(1)}, bf16[4,400,128]{2,1,0:T(8,128)(2,1)S(1)}, u32[]{:S(2)}, u32[]{:S(2)}) collective-permute-start(bf16[4,400,128]{2,1,0:T(8,128)(2,1)S(1)} %pad_maximum_fusion), channel_id=1, source_target_pairs={{0,4},{4,0},{8,12},{12,8},{16,20},{20,16},{24,28},{28,24},{1,5},{5... | collective-permute-start | bytes 1228808 | tf_op jit(solution)/shard_map/ppermute | solution.py:240
  68.7 4.1 %collective-permute-start.10 = (bf16[8,256,128]{2,1,0:T(8,128)(2,1)}, bf16[8,256,128]{2,1,0:T(8,128)(2,1)}, u32[]{:S(2)}, u32[]{:S(2)}) collective-permute-start(bf16[8,256,128]{2,1,0:T(8,128)(2,1)} %collective-permute-done.9.refs_6_.refs_8_), channel_id=1, source_target_pairs={{0,1},{1,0},{2,3},{3,2},{4,5},{5,4},{6,7},{7,6},{8,9},{9,8},{10,11... | collective-permute-start | bytes 1572872 | tf_op jit(solution)/shard_map/ppermute | solution.py:243
  68.7 4.1 %collective-permute-start.8 = (bf16[8,256,128]{2,1,0:T(8,128)(2,1)}, bf16[8,256,128]{2,1,0:T(8,128)(2,1)}, u32[]{:S(2)}, u32[]{:S(2)}) collective-permute-start(bf16[8,256,128]{2,1,0:T(8,128)(2,1)} %collective-permute-done.7.refs_5_.refs_7_), channel_id=1, source_target_pairs={{0,1},{1,0},{2,3},{3,2},{4,5},{5,4},{6,7},{7,6},{8,9},{9,8},{10,11... | collective-permute-start | bytes 1572872 | tf_op jit(solution)/shard_map/ppermute | solution.py:243
  69.2 3.6 %collective-permute-start.6 = (bf16[8,256,128]{2,1,0:T(8,128)(2,1)}, bf16[8,256,128]{2,1,0:T(8,128)(2,1)}, u32[]{:S(2)}, u32[]{:S(2)}) collective-permute-start(bf16[8,256,128]{2,1,0:T(8,128)(2,1)} %collective-permute-done.5.refs_4_.refs_6_), channel_id=1, source_target_pairs={{0,1},{1,0},{2,3},{3,2},{4,5},{5,4},{6,7},{7,6},{8,9},{9,8},{10,11... | collective-permute-start | bytes 1572872 | tf_op jit(solution)/shard_map/ppermute | solution.py:243
  76.5 12.2 %collective-permute-start.13 = (bf16[64,128,128]{2,1,0:T(8,128)(2,1)}, bf16[64,128,128]{2,1,0:T(8,128)(2,1)}, u32[]{:S(2)}, u32[]{:S(2)}) collective-permute-start(bf16[64,128,128]{2,1,0:T(8,128)(2,1)} %bitcast.17.refs_2_), channel_id=1, source_target_pairs={{0,1},{1,0},{2,3},{3,2},{4,5},{5,4},{6,7},{7,6},{8,9},{9,8},{10,11... | collective-permute-start | bytes 6291464 | tf_op jit(solution)/shard_map/ppermute | solution.py:243
  79.9 21.4 %collective-permute-start.12 = (bf16[8,64,256]{2,1,0:T(8,128)(2,1)S(1)}, bf16[8,64,256]{2,1,0:T(8,128)(2,1)S(1)}, u32[]{:S(2)}, u32[]{:S(2)}) collective-permute-start(bf16[8,64,256]{2,1,0:T(8,128)(2,1)S(1)} %get-tuple-element.24), channel_id=1, source_target_pairs={{0,16},{4,20},{8,24},{12,28},{16,0},{20,4},{24,8},{28,12},{1,17},{... | collective-permute-start | bytes 786440 | tf_op jit(solution)/shard_map/ppermute | solution.py:240
  82.3 23.7 %collective-permute-start.11 = (bf16[8,64,256]{2,1,0:T(8,128)(2,1)S(1)}, bf16[8,64,256]{2,1,0:T(8,128)(2,1)S(1)}, u32[]{:S(2)}, u32[]{:S(2)}) collective-permute-start(bf16[8,64,256]{2,1,0:T(8,128)(2,1)S(1)} %get-tuple-element.22), channel_id=1, source_target_pairs={{0,16},{4,20},{8,24},{12,28},{16,0},{20,4},{24,8},{28,12},{1,17},{... | collective-permute-start | bytes 786440 | tf_op jit(solution)/shard_map/ppermute | solution.py:240
  109.0 7.5 %collective-permute-start.14 = (bf16[4,6,32,128]{3,2,1,0:T(8,128)(2,1)S(1)}, bf16[4,6,32,128]{3,2,1,0:T(8,128)(2,1)S(1)}, u32[]{:S(2)}, u32[]{:S(2)}) collective-permute-start(bf16[4,6,32,128]{3,2,1,0:T(8,128)(2,1)S(1)} %fusion.4), channel_id=1, source_target_pairs={{0,4},{1,5},{2,6},{3,7},{4,0},{5,1},{6,2},{7,3},{8,12},{9,13},{10,... | collective-permute-start | bytes 589832 | tf_op jit(solution)/shard_map/ppermute | solution.py:251
  111.6 7.9 %collective-permute-start.15 = (bf16[4,6,32,128]{3,2,1,0:T(8,128)(2,1)S(1)}, bf16[4,6,32,128]{3,2,1,0:T(8,128)(2,1)S(1)}, u32[]{:S(2)}, u32[]{:S(2)}) collective-permute-start(bf16[4,6,32,128]{3,2,1,0:T(8,128)(2,1)S(1)} %slice_bitcast_fusion.2), channel_id=1, source_target_pairs={{0,2},{1,3},{2,0},{3,1},{4,6},{5,7},{6,4},{7,5},{8,10},{9,11},{10,... | collective-permute-start | bytes 589832 | tf_op jit(solution)/shard_map/ppermute | solution.py:251
  113.2 8.9 %collective-permute-start.16 = (bf16[4,6,32,128]{3,2,1,0:T(8,128)(2,1)S(1)}, bf16[4,6,32,128]{3,2,1,0:T(8,128)(2,1)S(1)}, u32[]{:S(2)}, u32[]{:S(2)}) collective-permute-start(bf16[4,6,32,128]{3,2,1,0:T(8,128)(2,1)S(1)} %slice_bitcast_fusion.1), channel_id=1, source_target_pairs={{0,6},{1,7},{2,4},{3,5},{4,2},{5,3},{6,0},{7,1},{8,14},{9,15},{10,... | collective-permute-start | bytes 589832 | tf_op jit(solution)/shard_map/ppermute | solution.py:251
  122.2 4.5 %collective-permute-start.17 = (bf16[6,32,128]{2,1,0:T(8,128)(2,1)S(1)}, bf16[6,32,128]{2,1,0:T(8,128)(2,1)S(1)}, u32[]{:S(2)}, u32[]{:S(2)}) collective-permute-start(bf16[6,32,128]{2,1,0:T(8,128)(2,1)S(1)} %get-tuple-element.31), channel_id=1, source_target_pairs={{0,8},{4,12},{8,0},{12,4},{16,24},{20,28},{24,16},{28,20},{1,9},{5... | collective-permute-start | bytes 147464 | tf_op jit(solution)/shard_map/ppermute | solution.py:240
  122.2 5.3 %collective-permute-start.18 = (bf16[6,32,128]{2,1,0:T(8,128)(2,1)S(1)}, bf16[6,32,128]{2,1,0:T(8,128)(2,1)S(1)}, u32[]{:S(2)}, u32[]{:S(2)}) collective-permute-start(bf16[6,32,128]{2,1,0:T(8,128)(2,1)S(1)} %get-tuple-element.33), channel_id=1, source_target_pairs={{0,16},{4,20},{8,24},{12,28},{16,0},{20,4},{24,8},{28,12},{1,17},{... | collective-permute-start | bytes 147464 | tf_op jit(solution)/shard_map/ppermute | solution.py:240
  124.3 5.9 %collective-permute-start.19 = (bf16[6,32,128]{2,1,0:T(8,128)(2,1)S(1)}, bf16[6,32,128]{2,1,0:T(8,128)(2,1)S(1)}, u32[]{:S(2)}, u32[]{:S(2)}) collective-permute-start(bf16[6,32,128]{2,1,0:T(8,128)(2,1)S(1)} %get-tuple-element.32), channel_id=1, source_target_pairs={{0,24},{4,28},{8,16},{12,20},{16,8},{20,12},{24,0},{28,4},{1,25},{... | collective-permute-start | bytes 147464 | tf_op jit(solution)/shard_map/ppermute | solution.py:240
  130.3 1.9 %collective-permute-start.20 = (bf16[6,32,128]{2,1,0:T(8,128)(2,1)S(1)}, bf16[6,32,128]{2,1,0:T(8,128)(2,1)S(1)}, u32[]{:S(2)}, u32[]{:S(2)}) collective-permute-start(bf16[6,32,128]{2,1,0:T(8,128)(2,1)S(1)} %fusion.7), channel_id=1, source_target_pairs={{0,1},{1,0},{2,3},{3,2},{4,5},{5,4},{6,7},{7,6},{8,9},{9,8},{10,11... | collective-permute-start | bytes 147464 | tf_op jit(solution)/shard_map/ppermute | solution.py:243
  130.3 4.2 %collective-permute-start.21 = (bf16[6,32,128]{2,1,0:T(8,128)(2,1)S(1)}, bf16[6,32,128]{2,1,0:T(8,128)(2,1)S(1)}, u32[]{:S(2)}, u32[]{:S(2)}) collective-permute-start(bf16[6,32,128]{2,1,0:T(8,128)(2,1)S(1)} %fusion.7), channel_id=1, source_target_pairs={{0,2},{1,3},{2,0},{3,1},{4,6},{5,7},{6,4},{7,5},{8,10},{9,11},{10,... | collective-permute-start | bytes 147464 | tf_op jit(solution)/shard_map/ppermute | solution.py:243
  131.9 3.7 %collective-permute-start.22 = (bf16[6,32,128]{2,1,0:T(8,128)(2,1)S(1)}, bf16[6,32,128]{2,1,0:T(8,128)(2,1)S(1)}, u32[]{:S(2)}, u32[]{:S(2)}) collective-permute-start(bf16[6,32,128]{2,1,0:T(8,128)(2,1)S(1)} %fusion.7), channel_id=1, source_target_pairs={{0,3},{1,2},{2,1},{3,0},{4,7},{5,6},{6,5},{7,4},{8,11},{9,10},{10,... | collective-permute-start | bytes 147464 | tf_op jit(solution)/shard_map/ppermute | solution.py:243
  (10 other events, 22.0 us)

commit v3 on v2

--- a/solution.py
+++ b/solution.py
@@ -10,7 +10,7 @@
 META = 16
 MEMBERS = 4
 FULL = 2
-VMEM_BYTES = 48 * 1024 * 1024
+VMEM_BYTES = 16 * 1024 * 1024
 
 SMEM_SPEC = pl.BlockSpec(memory_space=pltpu.SMEM)
 VMEM_SPEC = pl.BlockSpec(memory_space=pltpu.VMEM)
@@ -51,112 +51,148 @@
     )(place, block_list, owner_map, blocks)
 
 
-def plan_kernel(slots, owners, virt, meta_ref, out_ref):
+def plan_kernel(slots, owners, virt, meta_ref, out_ref, filled_ref):
     total = meta_ref.shape[0]
     room = total + BATCH
-
-    def one(s, filled):
+    for m in range(owners):
+        filled_ref[m] = m * room
+
+    def one(s, place):
         owner = meta_ref[s, 2]
-        sender = lax.div(s, slots)
-        at = filled[0]
-        for m in range(1, owners):
-            at = jnp.where(owner == m, filled[m] + m * room, at)
-        out_ref[0, at] = sender
-        out_ref[1, at] = s - sender * slots
-        out_ref[2, at] = meta_ref[s, 0]
-        out_ref[3, at] = meta_ref[s, 1]
-        out_ref[4, at] = s
-        return tuple(n + (owner == m).astype(jnp.int32) for m, n in enumerate(filled))
-
-    filled = lax.fori_loop(0, total, one, (jnp.int32(0),) * owners)
-    for m, n in enumerate(filled):
+        sender, first = place
+        where = meta_ref[s, 0] * 16 + meta_ref[s, 1]
+        at = filled_ref[owner]
+        out_ref[at] = ((s * 16 + sender) * 16 + s - first) * 256 + where
+        filled_ref[owner] = at + 1
+        over = s + 1 - first == slots
+        return sender + over.astype(jnp.int32), jnp.where(over, s + 1, first)
+
+    lax.fori_loop(0, total, one, (jnp.int32(0), jnp.int32(0)))
+    for m in range(owners):
+        n = filled_ref[m]
         for u in range(BATCH):
-            for k, value in enumerate((0, 0, virt, 0, total)):
-                out_ref[k, m * room + n + u] = jnp.int32(value)
-        out_ref[5, m] = lax.div(n + BATCH - 1, BATCH)
+            out_ref[n + u] = jnp.int32(total * 65536 + virt * 16)
+        out_ref[owners * room + m] = lax.div(n - m * room + BATCH - 1, BATCH)
 
 
 def plan(meta, slots, owners, virt):
     room = meta.shape[0] + BATCH
     return pl.pallas_call(
         lambda *refs: plan_kernel(slots, owners, virt, *refs),
-        out_shape=jax.ShapeDtypeStruct((6, owners * room), jnp.int32),
+        out_shape=jax.ShapeDtypeStruct((owners * room + owners,), jnp.int32),
         in_specs=[SMEM_SPEC],
         out_specs=SMEM_SPEC,
+        scratch_shapes=[pltpu.SMEM((owners,), jnp.int32)],
         cost_estimate=cost("plan"),
         name="plan",
     )(meta)
 
 
 def over_slots(plan_ref, owners, picks, step):
-    room = plan_ref.shape[1] // owners
+    room = plan_ref.shape[0] // owners - 1
     for owner, ref in picks:
 
         def batch(b, carry, owner=owner, ref=ref):
             step(ref, owner * room + b * BATCH)
             return carry
 
-        lax.fori_loop(0, plan_ref[5, owner], batch, 0)
+        lax.fori_loop(0, plan_ref[owners * room + owner], batch, 0)
 
 
 def add_blocks(plan_ref, blocks_ref, rows, sum_ref):
     def step(factors_ref, first):
+        words = [plan_ref[first + i] for i in range(BATCH)]
         terms = []
-        for i in range(BATCH):
-            start = pl.multiple_of(plan_ref[1, first + i] * rows, rows)
+        for word in words:
+            start = pl.multiple_of(((word >> 8) & 15) * rows, rows)
             terms.append(
                 lax.dot_general(
-                    blocks_ref[plan_ref[0, first + i], pl.ds(start, rows), :],
-                    factors_ref[plan_ref[3, first + i]],
+                    blocks_ref[(word >> 12) & 15, pl.ds(start, rows), :],
+                    factors_ref[word & 15],
                     (((1,), (1,)), ((), ())),
                     preferred_element_type=jnp.float32,
                 )
             )
-        for i in range(BATCH):
-            sum_ref[plan_ref[2, first + i]] += terms[i]
+        for word, term in zip(words, terms):
+            sum_ref[(word >> 4) & 15] += term
 
     return step
 
 
 def add_products(plan_ref, inter_ref, out_ref):
     def step(factors_ref, first):
+        words = [plan_ref[first + i] for i in range(BATCH)]
         terms = []
-        for i in range(BATCH):
+        for word in words:
             terms.append(
                 jnp.dot(
-                    inter_ref[plan_ref[2, first + i]],
-                    factors_ref[plan_ref[3, first + i]],
+                    inter_ref[(word >> 4) & 15],
+                    factors_ref[word & 15],
                     preferred_element_type=jnp.float32,
                 )
             )
-        for i in range(BATCH):
-            out_ref[plan_ref[4, first + i]] += terms[i]
+        for word, term in zip(words, terms):
+            out_ref[word >> 16] += term
 
     return step
 
 
-def contract_kernel(owners, rows, place_ref, plan_ref, blocks_ref, *refs):
-    own_ref, sent_ref = refs[-2:]
-    own_ref[...] = jnp.zeros_like(own_ref)
-    picks = [(place_ref[0] ^ d, ref) for d, ref in enumerate(refs[:-2])]
-    over_slots(plan_ref, owners, picks, add_blocks(plan_ref, blocks_ref, rows, own_ref))
-    sent_ref[...] = own_ref[pl.ds(0, sent_ref.shape[0])].astype(sent_ref.dtype)
-
-
-def contract(place, listed, blocks, factors, owners, virt, rows):
-    chunk = factors[0].shape[1]
+def contract_kernel(owners, rows, place_ref, plan_ref, blocks_ref, others_ref, *refs):
+    pieces = refs[:MEMBERS]
+    own_ref, same_ref, cross_ref, stack_ref, sum_ref, sems = refs[MEMBERS:]
+    virt = own_ref.shape[0]
+    copies = [
+        pltpu.make_async_copy(ref, stack_ref.at[pl.ds(d * virt, virt)], sems.at[d])
+        for d, ref in enumerate(pieces)
+    ]
+    for copy in copies:
+        copy.start()
+    sum_ref[...] = jnp.zeros_like(sum_ref)
+
+    def step(factors_ref, first):
+        words = [plan_ref[first + i] for i in range(BATCH)]
+        terms = []
+        for word in words:
+            start = pl.multiple_of(((word >> 8) & 15) * rows, rows)
+            halves = [ref[(word >> 12) & 15, pl.ds(start, rows), :] for ref in (blocks_ref, others_ref)]
+            terms.append(
+                lax.dot_general(
+                    jnp.concatenate(halves),
+                    factors_ref[word & 15],
+                    (((1,), (1,)), ((), ())),
+                    preferred_element_type=jnp.float32,
+                )
+            )
+        for word, term in zip(words, terms):
+            sum_ref[(word >> 4) & 15] += term
+
+    picks = [(place_ref[0] ^ d, ref) for d, ref in enumerate(pieces)]
+    over_slots(plan_ref, owners, picks, step)
+    own = sum_ref[pl.ds(0, virt), pl.ds(0, rows), :]
+    own_ref[...] = own
+    same_ref[...] = own.astype(same_ref.dtype)
+    cross_ref[...] = sum_ref[pl.ds(0, virt), pl.ds(rows, rows), :].astype(cross_ref.dtype)
+    for copy in copies:
+        copy.wait()
+
+
+def contract(place, listed, blocks, others, factors, owners, virt, rows):
+    chunk, depth = factors[0].shape[1:]
+    sent = jax.ShapeDtypeStruct((virt, rows, chunk), jnp.bfloat16)
+    stack = jax.ShapeDtypeStruct((MEMBERS * virt, chunk, depth), jnp.bfloat16)
     return pl.pallas_call(
         lambda *refs: contract_kernel(owners, rows, *refs),
-        out_shape=(
-            jax.ShapeDtypeStruct((virt + 1, rows, chunk), jnp.float32),
-            jax.ShapeDtypeStruct((virt, rows, chunk), jnp.bfloat16),
-        ),
-        in_specs=[SMEM_SPEC] * 2 + [VMEM_SPEC] * (1 + len(factors)),
-        out_specs=(VMEM_SPEC, VMEM_SPEC),
+        out_shape=(jax.ShapeDtypeStruct((virt, rows, chunk), jnp.float32), sent, sent, stack),
+        in_specs=[SMEM_SPEC] * 2 + [VMEM_SPEC] * (2 + len(factors)),
+        out_specs=(VMEM_SPEC,) * 3 + (pl.BlockSpec(memory_space=pl.ANY),),
+        scratch_shapes=[
+            pltpu.VMEM((virt + 1, 2 * rows, chunk), jnp.float32),
+            pltpu.SemaphoreType.DMA((MEMBERS,)),
+        ],
         compiler_params=PARAMS,
         cost_estimate=cost("contract"),
         name="contract",
-    )(place, listed, blocks, *factors)
+    )(place, listed, blocks, others, *factors)
 
 
 def whole_kernel(owners, rows, virt, plan_ref, blocks_ref, *refs):
@@ -189,28 +225,45 @@
     )(listed, blocks, factors, *so_far)
 
 
-def project_kernel(owners, members, place_ref, plan_ref, own_ref, got_ref, so_far_ref, *refs):
+def project_kernel(owners, place_ref, plan_ref, own_ref, got_ref, so_far_ref, *refs):
     out_ref, inter_ref = refs[-2:]
     virt = got_ref.shape[0]
-    summed = own_ref[pl.ds(0, virt)] + got_ref[...].astype(jnp.float32)
+    summed = own_ref[...].astype(jnp.float32) + got_ref[...].astype(jnp.float32)
     inter_ref[pl.ds(0, virt)] = summed.astype(inter_ref.dtype)
     inter_ref[virt] = jnp.zeros(inter_ref.shape[1:], inter_ref.dtype)
     out_ref[...] = so_far_ref[...]
-    picks = [(place_ref[0] ^ d, ref) for d, ref in enumerate(refs[:members])]
+    pieces = refs[:-2]
+    if len(pieces) == 1:
+        pieces = [refs[0].at[pl.ds(d * virt, virt)] for d in range(MEMBERS)]
+    picks = [(place_ref[0] ^ d, ref) for d, ref in enumerate(pieces)]
     over_slots(plan_ref, owners, picks, add_products(plan_ref, inter_ref, out_ref))
 
 
 def project(place, listed, own, got, factors, so_far, owners):
-    return pl.pallas_call(
-        lambda *refs: project_kernel(owners, len(factors), *refs),
+    virt, rows, chunk = got.shape
+    return pl.pallas_call(
+        lambda *refs: project_kernel(owners, *refs),
         out_shape=jax.ShapeDtypeStruct(so_far.shape, jnp.float32),
         in_specs=[SMEM_SPEC] * 2 + [VMEM_SPEC] * (3 + len(factors)),
         out_specs=VMEM_SPEC,
-        scratch_shapes=[pltpu.VMEM(own.shape, jnp.bfloat16)],
+        scratch_shapes=[pltpu.VMEM((virt + 1, rows, chunk), jnp.bfloat16)],
         compiler_params=PARAMS,
         cost_estimate=cost("project"),
         name="project",
     )(place, listed, own, got, so_far, *factors)
+
+
+def touch(values, *others):
+    values = list(values)
+    anywhere = pl.BlockSpec(memory_space=pl.ANY)
+    return pl.pallas_call(
+        lambda *refs: None,
+        out_shape=[jax.ShapeDtypeStruct(value.shape, value.dtype) for value in values],
+        in_specs=[anywhere] * (len(values) + len(others)),
+        out_specs=[anywhere] * len(values),
+        input_output_aliases={i: i for i in range(len(values))},
+        name="touch",
+    )(*values, *others)
 
 
 def after(value, *others):
@@ -255,7 +308,6 @@
     starts = [full_rows + ((turn & (MEMBERS - 1)) ^ d) * chunk for d in range(MEMBERS)]
     pieces = [lax.dynamic_slice_in_dim(factors, start, chunk, 0) for start in starts]
     pieces = [jnp.transpose(piece, (1, 0, 2)) for piece in pieces]
-    full = lax.all_to_all(full, "pair", 0, 0, tiled=True)
 
     packed = pack(place, block_list, owner_map, after(amplitudes, turn))
     near = jnp.stack([over_pair(packed, 2 * i) for i in range(pairs // 2)])
@@ -263,15 +315,18 @@
     meta = blocks[:, slots * rows : slots * rows + slots, :3].astype(jnp.int32)
     listed = plan(meta.reshape(total, 3), slots, pairs, virt)
 
-    mine = [pieces[0]]
-    for d in range(1, MEMBERS):
-        mine.append(after(over_pair(pieces[d], d), blocks))
-    other = [over_aux(piece, 1) for piece in mine]
-    work = []
-    for held in (mine, other):
-        own, sent = contract(place, listed, blocks, held, pairs, virt, rows)
-        work.append((own, over_pair(sent, MEMBERS), held))
-    full = jnp.transpose(after(full, sent), (0, 2, 1, 3)).reshape(pairs * virt, full_chunk, depth)
+    full = lax.all_to_all(after(full, near), "pair", 0, 0, tiled=True)
+    for d in (1, 3):
+        pieces[d] = after(pieces[d], near)
+
+    others = over_aux(blocks, 1)
+    mine = [over_pair(pieces[d], d) for d in range(1, MEMBERS)]
+    mine = [pieces[0], *touch(mine, listed, others)]
+    own, same, cross, stack = contract(place, listed, blocks, others, mine, pairs, virt, rows)
+    got = over_pair(same, MEMBERS), over_both(cross, MEMBERS, 1)
+    own = own, over_aux(cross, 1)
+    work = list(zip(own, got, (mine, [over_aux(stack, 1)])))
+    full = jnp.transpose(after(full, same), (0, 2, 1, 3)).reshape(pairs * virt, full_chunk, depth)
     out = None
     for held in (full, over_aux(full, 1)):
         out = whole(listed, blocks, held, out, pairs, virt, rows, total)

time: 137 us -> 132 us (0.964)
  waiting for transfers between devices: 69.2 us -> 62.3 us
  local copies, waits for them, and re-layouts: 9.58 us -> 14.3 us
  Pallas kernels: 26.7 us -> 23.7 us
    ppermute x12 -> x11, waiting for transfers between devices: 57 us -> 47.2 us  [over_pair(): lax.ppermute(value, 'pair', [(i, i ^ distance) for i in range(pairs)])]
    unnamed x24 -> x22, local copies, waits for them, and re-layouts: 2.64 us -> 5.6 us
    ppermute x3 -> x4, waiting for transfers between devices: 8.8 us -> 10.9 us  [over_both(): return lax.ppermute(value, ('pair', 'aux'), route)]
    pallas_call x2 -> x1, Pallas kernels: 5.75 us -> 4.2 us  [contract(): pl.pallas_call(lambda *refs: contract_kernel(owners, rows, *refs), out_sh...]
    pallas_call x2 -> x3, Pallas kernels: 5.28 us -> 4.6 us  [the longest x2 4.6 us: project(): pl.pallas_call(lambda *refs: project_kernel(owners, *refs), out_shape=jax...]
    ppermute x8 -> x7, starting transfers between devices: 3.03 us -> 2.45 us  [over_aux(): lax.ppermute(value, 'aux', [(i, i ^ distance) for i in range(shares)])]
    ppermute x12 -> x11, starting transfers between devices: 18.6 us -> 19.1 us  [over_pair(): lax.ppermute(value, 'pair', [(i, i ^ distance) for i in range(pairs)])]
    ppermute x3 -> x4, starting transfers between devices: 4.19 us -> 3.8 us  [over_both(): return lax.ppermute(value, ('pair', 'aux'), route)]
  transfers between devices with their start and end apart: 24 -> 23, of which waited for: 10 -> 13; matrix products, arithmetic and copies ran while one was open for 4% -> 8% of each run, Pallas kernels for 17% -> 16%
where the time goes in v3:
time: 132 us; the launch traced here: 131 us
  waiting for transfers between devices  62.3 us (47%)
  starting transfers between devices  29.7 us (22%)
  Pallas kernels  23.7 us (18%)
  local copies, waits for them, and re-layouts  14.3 us (11%)
    ppermute x11, waiting for transfers between devices, over_pair(): lax.ppermute(value, 'pair', [(i, i ^ distance) for i in range(pairs)])  47.2 us
    ppermute x11, starting transfers between devices, over_pair(): lax.ppermute(value, 'pair', [(i, i ^ distance) for i in range(pairs)])  19.1 us
    pallas_call x2, Pallas kernels, whole(): pl.pallas_call(lambda *refs: whole_kernel(owners, rows, virt, *refs), out...  12 us
    ppermute x4, waiting for transfers between devices, over_both(): return lax.ppermute(value, ('pair', 'aux'), route)  10.9 us
    unnamed x22, local copies, waits for them, and re-layouts  5.6 us
    pallas_call x2, Pallas kernels, project(): pl.pallas_call(lambda *refs: project_kernel(owners, *refs), out_shape=jax...  4.6 us
    all_to_all x1, starting transfers between devices, near_plan(): full = lax.all_to_all(after(full, near), 'pair', 0, 0, tiled=True)  4.35 us
    pallas_call x1, Pallas kernels, contract(): pl.pallas_call(lambda *refs: contract_kernel(owners, rows, *refs), out_sh...  4.2 us
  transfers between devices with their start and end apart: 23, of which 13 were waited for; matrix products, arithmetic and copies ran while one was open for 8% of the time, Pallas kernels for 16%

profile of v3, /device:TPU:0, one launch (start us, length us, event | category | flops | bytes accessed | tf_op | source)
XLA Modules:
  0.0 131.2 jit_solution(5128947316509331558)
XLA Ops:
  1.6 3.1 %collective-permute-start = (bf16[400,128]{1,0:T(8,128)(2,1)S(1)}, bf16[400,128]{1,0:T(8,128)(2,1)S(1)}, u32[]{:S(2)}, u32[]{:S(2)}) collective-permute-start(bf16[400,128]{1,0:T(8,128)(2,1)S(1)} %pack.1), channel_id=1, source_target_pairs={{0,8},{4,12},{8,0},{12,4},{16,24},{20,28},{24,16},{28,20},{1,9},{5... | collective-permute-start | bytes 307208 | tf_op jit(solution)/shard_map/ppermute | solution.py:293
  4.7 2.6 %collective-permute-start.1 = (bf16[400,128]{1,0:T(8,128)(2,1)S(1)}, bf16[400,128]{1,0:T(8,128)(2,1)S(1)}, u32[]{:S(2)}, u32[]{:S(2)}) collective-permute-start(bf16[400,128]{1,0:T(8,128)(2,1)S(1)} %pack.1), channel_id=1, source_target_pairs={{0,16},{4,20},{8,24},{12,28},{16,0},{20,4},{24,8},{28,12},{1,17},{... | collective-permute-start | bytes 307208 | tf_op jit(solution)/shard_map/ppermute | solution.py:293
  7.3 1.7 %constant_dynamic-slice_fusion = (bf16[1,256,8,128]{3,2,1,0:T(8,128)(2,1)S(1)}, bf16[1,256,8,128]{3,2,1,0:T(8,128)(2,1)S(1)}, bf16[1,256,8,128]{3,2,1,0:T(8,128)(2,1)S(1)}, bf16[1,256,8,128]{3,2,1,0:T(8,128)(2,1)S(1)}) fusion(bf16[1,2048,8,128]{3,2,1,0:T(8,128)(2,1)} %param.4, s32[]{:T(128)S(6)} %select_n.58, s32[]{:T(128)S(6)} %select_n.56, ...), kind=kLoop, calls=%fused_computation.36 | loop fusion | bytes 4194320 | tf_op jit(solution)/shard_map/dynamic_slice | solution.py:309
  12.6 2.8 %collective-permute-done.1 = bf16[400,128]{1,0:T(8,128)(2,1)S(1)} collective-permute-done((bf16[400,128]{1,0:T(8,128)(2,1)S(1)}, bf16[400,128]{1,0:T(8,128)(2,1)S(1)}, u32[]{:S(2)}, u32[]{:S(2)}) %collective-permute-start.1) | collective-permute-done | bytes 102432 | tf_op jit(solution)/shard_map/ppermute | solution.py:293
  15.5 1.6 %collective-permute-start.3 = (bf16[4,400,128]{2,1,0:T(8,128)(2,1)S(1)}, bf16[4,400,128]{2,1,0:T(8,128)(2,1)S(1)}, u32[]{:S(2)}, u32[]{:S(2)}) collective-permute-start(bf16[4,400,128]{2,1,0:T(8,128)(2,1)S(1)} %pad_maximum_fusion), channel_id=1, source_target_pairs={{0,4},{4,0},{8,12},{12,8},{16,20},{20,16},{24,28},{28,24},{1,5},{5... | collective-permute-start | bytes 1228808 | tf_op jit(solution)/shard_map/ppermute | solution.py:293
  17.1 1.6 %collective-permute-start.7 = (bf16[8,256,128]{2,1,0:T(8,128)(2,1)}, bf16[8,256,128]{2,1,0:T(8,128)(2,1)}, u32[]{:S(2)}, u32[]{:S(2)}) collective-permute-start(bf16[8,256,128]{2,1,0:T(8,128)(2,1)} %get-tuple-element.22), channel_id=1, source_target_pairs={{0,12},{4,8},{8,4},{12,0},{16,28},{20,24},{24,20},{28,16},{1,13},{... | collective-permute-start | bytes 1572872 | tf_op jit(solution)/shard_map/ppermute | solution.py:293
  20.2 1.9 %copy.35 = bf16[8,128,8,128]{3,1,2,0:T(8,128)(2,1)} copy(bf16[8,128,8,128]{3,2,1,0:T(8,128)(2,1)S(1)} %bitcast.75) | data formatting | bytes 4194304 | tf_op jit(solution)/shard_map/optimization_barrier | solution.py:270
  22.1 4.3 %all-to-all-start = ((bf16[8,128,8,128]{3,1,2,0:T(8,128)(2,1)}), bf16[8,128,8,128]{3,1,2,0:T(8,128)(2,1)}, u32[]{:S(2)}, u32[]{:S(2)}) async-start(bf16[8,128,8,128]{3,1,2,0:T(8,128)(2,1)} %copy.35), calls=%async_computation | async-start | bytes 4194304 | tf_op jit(solution)/shard_map/all_to_all | solution.py:318
  28.4 26.0 %collective-permute-done.3 = bf16[4,400,128]{2,1,0:T(8,128)(2,1)S(1)} collective-permute-done((bf16[4,400,128]{2,1,0:T(8,128)(2,1)S(1)}, bf16[4,400,128]{2,1,0:T(8,128)(2,1)S(1)}, u32[]{:S(2)}, u32[]{:S(2)}) %collective-permute-start.3) | collective-permute-done | bytes 409632 | tf_op jit(solution)/shard_map/ppermute | solution.py:293
  56.5 2.2 %plan.1.refs_3_.refs_1_.refs_0_ = s32[456]{0:T(512)} custom-call(s32[48,3]{1,0:T(8,128)} %reshape.120.refs_0_), custom_call_target="tpu_custom_call" | custom-call | flops 9999999827968 | tf_op jit(solution)/shard_map/plan/pallas_call | solution.py:80
  58.7 7.3 %collective-permute-done.5.refs_0_ = bf16[8,256,128]{2,1,0:T(8,128)(2,1)} collective-permute-done((bf16[8,256,128]{2,1,0:T(8,128)(2,1)}, bf16[8,256,128]{2,1,0:T(8,128)(2,1)}, u32[]{:S(2)}, u32[]{:S(2)}) %collective-permute-start.5) | collective-permute-done | bytes 524320 | tf_op jit(solution)/shard_map/ppermute | solution.py:293
  66.1 4.2 %contract.1 = (f32[8,64,256]{2,1,0:T(8,128)S(1)}, bf16[8,64,256]{2,1,0:T(8,128)(2,1)}, bf16[8,64,256]{2,1,0:T(8,128)(2,1)S(1)}, bf16[32,256,128]{2,1,0:T(8,128)(2,1)S(1)}) custom-call(s32[2]{0:T(128)S(1)} %copy-done.3, s32[456]{0:T(512)S(1)} %copy-done.1, bf16[8,400,128]{2,1,0:T(8,128)(2,1)} %constant_dynamic-update-slice_fusion.refs_2_.refs_1_, ...), custom_call_target="tpu_custom_call" | custom-call | flops 9999999827968 | tf_op jit(solution)/shard_map/contract/pallas_call | solution.py:183
  73.7 3.4 %collective-permute-start.10 = (bf16[8,64,256]{2,1,0:T(8,128)(2,1)}, bf16[8,64,256]{2,1,0:T(8,128)(2,1)}, u32[]{:S(2)}, u32[]{:S(2)}) collective-permute-start(bf16[8,64,256]{2,1,0:T(8,128)(2,1)} %get-tuple-element.28), channel_id=1, source_target_pairs={{0,16},{4,20},{8,24},{12,28},{16,0},{20,4},{24,8},{28,12},{1,17},{... | collective-permute-start | bytes 786440 | tf_op jit(solution)/shard_map/ppermute | solution.py:293
  77.3 6.0 %whole.2.refs_3_ = f32[49,64,128]{2,1,0:T(8,128)S(1)} custom-call(s32[456]{0:T(512)S(1)} %copy-done.1, bf16[8,400,128]{2,1,0:T(8,128)(2,1)} %constant_dynamic-update-slice_fusion.refs_2_.refs_1_, bf16[64,128,128]{2,1,0:T(8,128)(2,1)} %bitcast.16.refs_2_), custom_call_target="tpu_custom_call" | custom-call | tf_op jit(solution)/shard_map/whole/pallas_call | solution.py:213
  83.3 6.0 %whole.3.refs_4_ = f32[49,64,128]{2,1,0:T(8,128)S(1)} custom-call(s32[456]{0:T(512)S(1)} %copy-done.1, bf16[8,400,128]{2,1,0:T(8,128)(2,1)} %constant_dynamic-update-slice_fusion.refs_2_.refs_1_, bf16[64,128,128]{2,1,0:T(8,128)(2,1)} %collective-permute-done.11.refs_2_, f32[49,64,128]{2,1,0:T(8,128)S(1)} %whole.2.refs_3_), custom_call_target="tpu_custom_call" | custom-call | tf_op jit(solution)/shard_map/whole/pallas_call | solution.py:213
  89.3 6.5 %collective-permute-done.10.refs_3_ = bf16[8,64,256]{2,1,0:T(8,128)(2,1)} collective-permute-done((bf16[8,64,256]{2,1,0:T(8,128)(2,1)}, bf16[8,64,256]{2,1,0:T(8,128)(2,1)}, u32[]{:S(2)}, u32[]{:S(2)}) %collective-permute-start.10) | collective-permute-done | bytes 262176 | tf_op jit(solution)/shard_map/ppermute | solution.py:293
  95.8 2.5 %project.2.refs_4_ = f32[49,64,128]{2,1,0:T(8,128)S(1)} custom-call(s32[2]{0:T(128)S(1)} %copy-done.3, s32[456]{0:T(512)S(1)} %copy-done.1, f32[8,64,256]{2,1,0:T(8,128)S(1)} %get-tuple-element.27.refs_2_, bf16[8,64,256]{2,1,0:T(8,128)(2,1)} %collective-permute-done.10.refs_3_, f32[49,64,128]{2,1,0:T(8,128)S(1)} %whole.3.refs_4_, ...), custom_call_target="tpu_custom_call" | custom-call | tf_op jit(solution)/shard_map/project/pallas_call | solution.py:244
  98.3 1.8 %collective-permute-done.9.refs_3_ = bf16[8,64,256]{2,1,0:T(8,128)(2,1)} collective-permute-done((bf16[8,64,256]{2,1,0:T(8,128)(2,1)}, bf16[8,64,256]{2,1,0:T(8,128)(2,1)}, u32[]{:S(2)}, u32[]{:S(2)}) %collective-permute-start.9) | collective-permute-done | bytes 262176 | tf_op jit(solution)/shard_map/ppermute | solution.py:304
  100.1 2.1 %project.3 = f32[49,64,128]{2,1,0:T(8,128)S(1)} custom-call(s32[2]{0:T(128)S(1)} %copy-done.3, s32[456]{0:T(512)S(1)} %copy-done.1, bf16[8,64,256]{2,1,0:T(8,128)(2,1)S(1)} %collective-permute-done.8.refs_2_, bf16[8,64,256]{2,1,0:T(8,128)(2,1)} %collective-permute-done.9.refs_3_, f32[49,64,128]{2,1,0:T(8,128)S(1)} %project.2.refs_4_, ...), custom_call_target="tpu_custom_call" | custom-call | tf_op jit(solution)/shard_map/project/pallas_call | solution.py:244
  106.3 3.6 %collective-permute-done.13 = bf16[4,6,32,128]{3,2,1,0:T(8,128)(2,1)S(1)} collective-permute-done((bf16[4,6,32,128]{3,2,1,0:T(8,128)(2,1)S(1)}, bf16[4,6,32,128]{3,2,1,0:T(8,128)(2,1)S(1)}, u32[]{:S(2)}, u32[]{:S(2)}) %collective-permute-start.13) | collective-permute-done | bytes 196640 | tf_op jit(solution)/shard_map/ppermute | solution.py:304
  111.5 4.0 %collective-permute-done.15 = bf16[4,6,32,128]{3,2,1,0:T(8,128)(2,1)S(1)} collective-permute-done((bf16[4,6,32,128]{3,2,1,0:T(8,128)(2,1)S(1)}, bf16[4,6,32,128]{3,2,1,0:T(8,128)(2,1)S(1)}, u32[]{:S(2)}, u32[]{:S(2)}) %collective-permute-start.15) | collective-permute-done | bytes 196640 | tf_op jit(solution)/shard_map/ppermute | solution.py:304
  115.6 3.0 %collective-permute-start.17 = (bf16[6,32,128]{2,1,0:T(8,128)(2,1)S(1)}, bf16[6,32,128]{2,1,0:T(8,128)(2,1)S(1)}, u32[]{:S(2)}, u32[]{:S(2)}) collective-permute-start(bf16[6,32,128]{2,1,0:T(8,128)(2,1)S(1)} %get-tuple-element.39), channel_id=1, source_target_pairs={{0,16},{4,20},{8,24},{12,28},{16,0},{20,4},{24,8},{28,12},{1,17},{... | collective-permute-start | bytes 147464 | tf_op jit(solution)/shard_map/ppermute | solution.py:293
  121.3 3.2 %collective-permute-done.18 = bf16[6,32,128]{2,1,0:T(8,128)(2,1)S(1)} collective-permute-done((bf16[6,32,128]{2,1,0:T(8,128)(2,1)S(1)}, bf16[6,32,128]{2,1,0:T(8,128)(2,1)S(1)}, u32[]{:S(2)}, u32[]{:S(2)}) %collective-permute-start.18) | collective-permute-done | bytes 49184 | tf_op jit(solution)/shard_map/ppermute | solution.py:293
  126.5 2.3 %collective-permute-done.20 = bf16[6,32,128]{2,1,0:T(8,128)(2,1)S(1)} collective-permute-done((bf16[6,32,128]{2,1,0:T(8,128)(2,1)S(1)}, bf16[6,32,128]{2,1,0:T(8,128)(2,1)S(1)}, u32[]{:S(2)}, u32[]{:S(2)}) %collective-permute-start.20) | collective-permute-done | bytes 49184 | tf_op jit(solution)/shard_map/ppermute | solution.py:296
  (78 shorter events, 27.2 us)
Async XLA Ops:
  1.6 11.0 %collective-permute-start = (bf16[400,128]{1,0:T(8,128)(2,1)S(1)}, bf16[400,128]{1,0:T(8,128)(2,1)S(1)}, u32[]{:S(2)}, u32[]{:S(2)}) collective-permute-start(bf16[400,128]{1,0:T(8,128)(2,1)S(1)} %pack.1), channel_id=1, source_target_pairs={{0,8},{4,12},{8,0},{12,4},{16,24},{20,28},{24,16},{28,20},{1,9},{5... | collective-permute-start | bytes 307208 | tf_op jit(solution)/shard_map/ppermute | solution.py:293
  4.7 10.8 %collective-permute-start.1 = (bf16[400,128]{1,0:T(8,128)(2,1)S(1)}, bf16[400,128]{1,0:T(8,128)(2,1)S(1)}, u32[]{:S(2)}, u32[]{:S(2)}) collective-permute-start(bf16[400,128]{1,0:T(8,128)(2,1)S(1)} %pack.1), channel_id=1, source_target_pairs={{0,16},{4,20},{8,24},{12,28},{16,0},{20,4},{24,8},{28,12},{1,17},{... | collective-permute-start | bytes 307208 | tf_op jit(solution)/shard_map/ppermute | solution.py:293
  7.3 8.2 %collective-permute-start.2 = (bf16[400,128]{1,0:T(8,128)(2,1)S(1)}, bf16[400,128]{1,0:T(8,128)(2,1)S(1)}, u32[]{:S(2)}, u32[]{:S(2)}) collective-permute-start(bf16[400,128]{1,0:T(8,128)(2,1)S(1)} %pack.1), channel_id=1, source_target_pairs={{0,24},{4,28},{8,16},{12,20},{16,8},{20,12},{24,0},{28,4},{1,25},{... | collective-permute-start | bytes 307208 | tf_op jit(solution)/shard_map/ppermute | solution.py:293
  9.8 10.4 %slice-start = ((bf16[1,2048,8,128]{3,2,1,0:T(8,128)(2,1)}), bf16[1,1024,8,128]{3,2,1,0:T(8,128)(2,1)S(1)}, s32[]{:S(2)}) async-start(bf16[1,2048,8,128]{3,2,1,0:T(8,128)(2,1)} %param.4), calls=%async_computation.1 | async-start | bytes 4194304 | tf_op jit(solution)/shard_map/slice | solution.py:306
  9.8 48.9 %collective-permute-start.6 = (bf16[8,256,128]{2,1,0:T(8,128)(2,1)}, bf16[8,256,128]{2,1,0:T(8,128)(2,1)}, u32[]{:S(2)}, u32[]{:S(2)}) collective-permute-start(bf16[8,256,128]{2,1,0:T(8,128)(2,1)} %bitcast.70), channel_id=1, source_target_pairs={{0,8},{4,12},{8,0},{12,4},{16,24},{20,28},{24,16},{28,20},{1,9},{5... | collective-permute-start | bytes 1572872 | tf_op jit(solution)/shard_map/ppermute | solution.py:293
  15.5 38.9 %collective-permute-start.3 = (bf16[4,400,128]{2,1,0:T(8,128)(2,1)S(1)}, bf16[4,400,128]{2,1,0:T(8,128)(2,1)S(1)}, u32[]{:S(2)}, u32[]{:S(2)}) collective-permute-start(bf16[4,400,128]{2,1,0:T(8,128)(2,1)S(1)} %pad_maximum_fusion), channel_id=1, source_target_pairs={{0,4},{4,0},{8,12},{12,8},{16,20},{20,16},{24,28},{28,24},{1,5},{5... | collective-permute-start | bytes 1228808 | tf_op jit(solution)/shard_map/ppermute | solution.py:293
  17.1 41.7 %collective-permute-start.7 = (bf16[8,256,128]{2,1,0:T(8,128)(2,1)}, bf16[8,256,128]{2,1,0:T(8,128)(2,1)}, u32[]{:S(2)}, u32[]{:S(2)}) collective-permute-start(bf16[8,256,128]{2,1,0:T(8,128)(2,1)} %get-tuple-element.22), channel_id=1, source_target_pairs={{0,12},{4,8},{8,4},{12,0},{16,28},{20,24},{24,20},{28,16},{1,13},{... | collective-permute-start | bytes 1572872 | tf_op jit(solution)/shard_map/ppermute | solution.py:293
  18.7 47.4 %collective-permute-start.5 = (bf16[8,256,128]{2,1,0:T(8,128)(2,1)}, bf16[8,256,128]{2,1,0:T(8,128)(2,1)}, u32[]{:S(2)}, u32[]{:S(2)}) collective-permute-start(bf16[8,256,128]{2,1,0:T(8,128)(2,1)} %get-tuple-element.21), channel_id=1, source_target_pairs={{0,4},{4,0},{8,12},{12,8},{16,20},{20,16},{24,28},{28,24},{1,5},{5... | collective-permute-start | bytes 1572872 | tf_op jit(solution)/shard_map/ppermute | solution.py:293
  22.1 51.1 %all-to-all-start = ((bf16[8,128,8,128]{3,1,2,0:T(8,128)(2,1)}), bf16[8,128,8,128]{3,1,2,0:T(8,128)(2,1)}, u32[]{:S(2)}, u32[]{:S(2)}) async-start(bf16[8,128,8,128]{3,1,2,0:T(8,128)(2,1)} %copy.35), calls=%async_computation | async-start | bytes 4194304 | tf_op jit(solution)/shard_map/all_to_all | solution.py:318
  55.9 10.2 %collective-permute-start.4 = (bf16[8,400,128]{2,1,0:T(8,128)(2,1)}, bf16[8,400,128]{2,1,0:T(8,128)(2,1)}, u32[]{:S(2)}, u32[]{:S(2)}) collective-permute-start(bf16[8,400,128]{2,1,0:T(8,128)(2,1)} %constant_dynamic-update-slice_fusion.refs_2_.refs_1_), channel_id=1, source_target_pairs={{0,1},{1,0},{2,3},{3,2},{4,5},{5,4},{6,7},{7,6},{8,9},{9,8},{10,11... | collective-permute-start | bytes 2457608 | tf_op jit(solution)/shard_map/ppermute | solution.py:296
  73.2 10.1 %collective-permute-start.11 = (bf16[64,128,128]{2,1,0:T(8,128)(2,1)}, bf16[64,128,128]{2,1,0:T(8,128)(2,1)}, u32[]{:S(2)}, u32[]{:S(2)}) collective-permute-start(bf16[64,128,128]{2,1,0:T(8,128)(2,1)} %bitcast.16.refs_2_), channel_id=1, source_target_pairs={{0,1},{1,0},{2,3},{3,2},{4,5},{5,4},{6,7},{7,6},{8,9},{9,8},{10,11... | collective-permute-start | bytes 6291464 | tf_op jit(solution)/shard_map/ppermute | solution.py:296
  73.2 26.9 %collective-permute-start.12 = (bf16[32,256,128]{2,1,0:T(8,128)(2,1)}, bf16[32,256,128]{2,1,0:T(8,128)(2,1)S(1)}, u32[]{:S(2)}, u32[]{:S(2)}) collective-permute-start(bf16[32,256,128]{2,1,0:T(8,128)(2,1)} %copy-done.5), channel_id=1, source_target_pairs={{0,1},{1,0},{2,3},{3,2},{4,5},{5,4},{6,7},{7,6},{8,9},{9,8},{10,11... | collective-permute-start | bytes 6291464 | tf_op jit(solution)/shard_map/ppermute | solution.py:296
  73.7 22.1 %collective-permute-start.10 = (bf16[8,64,256]{2,1,0:T(8,128)(2,1)}, bf16[8,64,256]{2,1,0:T(8,128)(2,1)}, u32[]{:S(2)}, u32[]{:S(2)}) collective-permute-start(bf16[8,64,256]{2,1,0:T(8,128)(2,1)} %get-tuple-element.28), channel_id=1, source_target_pairs={{0,16},{4,20},{8,24},{12,28},{16,0},{20,4},{24,8},{28,12},{1,17},{... | collective-permute-start | bytes 786440 | tf_op jit(solution)/shard_map/ppermute | solution.py:293
  77.1 21.2 %collective-permute-start.8 = (bf16[8,64,256]{2,1,0:T(8,128)(2,1)}, bf16[8,64,256]{2,1,0:T(8,128)(2,1)S(1)}, u32[]{:S(2)}, u32[]{:S(2)}) collective-permute-start(bf16[8,64,256]{2,1,0:T(8,128)(2,1)} %copy-done.6), channel_id=1, source_target_pairs={{0,1},{1,0},{2,3},{3,2},{4,5},{5,4},{6,7},{7,6},{8,9},{9,8},{10,11... | collective-permute-start | bytes 786440 | tf_op jit(solution)/shard_map/ppermute | solution.py:296
  77.1 23.0 %collective-permute-start.9 = (bf16[8,64,256]{2,1,0:T(8,128)(2,1)}, bf16[8,64,256]{2,1,0:T(8,128)(2,1)}, u32[]{:S(2)}, u32[]{:S(2)}) collective-permute-start(bf16[8,64,256]{2,1,0:T(8,128)(2,1)} %copy-done.6), channel_id=1, source_target_pairs={{0,17},{1,16},{2,19},{3,18},{4,21},{5,20},{6,23},{7,22},{8,25},{9,... | collective-permute-start | bytes 786440 | tf_op jit(solution)/shard_map/ppermute | solution.py:304
  102.6 7.3 %collective-permute-start.13 = (bf16[4,6,32,128]{3,2,1,0:T(8,128)(2,1)S(1)}, bf16[4,6,32,128]{3,2,1,0:T(8,128)(2,1)S(1)}, u32[]{:S(2)}, u32[]{:S(2)}) collective-permute-start(bf16[4,6,32,128]{3,2,1,0:T(8,128)(2,1)S(1)} %fusion.4), channel_id=1, source_target_pairs={{0,4},{1,5},{2,6},{3,7},{4,0},{5,1},{6,2},{7,3},{8,12},{9,13},{10,... | collective-permute-start | bytes 589832 | tf_op jit(solution)/shard_map/ppermute | solution.py:304
  103.6 7.9 %collective-permute-start.14 = (bf16[4,6,32,128]{3,2,1,0:T(8,128)(2,1)S(1)}, bf16[4,6,32,128]{3,2,1,0:T(8,128)(2,1)S(1)}, u32[]{:S(2)}, u32[]{:S(2)}) collective-permute-start(bf16[4,6,32,128]{3,2,1,0:T(8,128)(2,1)S(1)} %slice_bitcast_fusion.2), channel_id=1, source_target_pairs={{0,2},{1,3},{2,0},{3,1},{4,6},{5,7},{6,4},{7,5},{8,10},{9,11},{10,... | collective-permute-start | bytes 589832 | tf_op jit(solution)/shard_map/ppermute | solution.py:304
  105.1 10.3 %collective-permute-start.15 = (bf16[4,6,32,128]{3,2,1,0:T(8,128)(2,1)S(1)}, bf16[4,6,32,128]{3,2,1,0:T(8,128)(2,1)S(1)}, u32[]{:S(2)}, u32[]{:S(2)}) collective-permute-start(bf16[4,6,32,128]{3,2,1,0:T(8,128)(2,1)S(1)} %slice_bitcast_fusion.1), channel_id=1, source_target_pairs={{0,6},{1,7},{2,4},{3,5},{4,2},{5,3},{6,0},{7,1},{8,14},{9,15},{10,... | collective-permute-start | bytes 589832 | tf_op jit(solution)/shard_map/ppermute | solution.py:304
  115.6 4.5 %collective-permute-start.16 = (bf16[6,32,128]{2,1,0:T(8,128)(2,1)S(1)}, bf16[6,32,128]{2,1,0:T(8,128)(2,1)S(1)}, u32[]{:S(2)}, u32[]{:S(2)}) collective-permute-start(bf16[6,32,128]{2,1,0:T(8,128)(2,1)S(1)} %get-tuple-element.37), channel_id=1, source_target_pairs={{0,8},{4,12},{8,0},{12,4},{16,24},{20,28},{24,16},{28,20},{1,9},{5... | collective-permute-start | bytes 147464 | tf_op jit(solution)/shard_map/ppermute | solution.py:293
  115.6 5.7 %collective-permute-start.17 = (bf16[6,32,128]{2,1,0:T(8,128)(2,1)S(1)}, bf16[6,32,128]{2,1,0:T(8,128)(2,1)S(1)}, u32[]{:S(2)}, u32[]{:S(2)}) collective-permute-start(bf16[6,32,128]{2,1,0:T(8,128)(2,1)S(1)} %get-tuple-element.39), channel_id=1, source_target_pairs={{0,16},{4,20},{8,24},{12,28},{16,0},{20,4},{24,8},{28,12},{1,17},{... | collective-permute-start | bytes 147464 | tf_op jit(solution)/shard_map/ppermute | solution.py:293
  118.7 5.9 %collective-permute-start.18 = (bf16[6,32,128]{2,1,0:T(8,128)(2,1)S(1)}, bf16[6,32,128]{2,1,0:T(8,128)(2,1)S(1)}, u32[]{:S(2)}, u32[]{:S(2)}) collective-permute-start(bf16[6,32,128]{2,1,0:T(8,128)(2,1)S(1)} %get-tuple-element.38), channel_id=1, source_target_pairs={{0,24},{4,28},{8,16},{12,20},{16,8},{20,12},{24,0},{28,4},{1,25},{... | collective-permute-start | bytes 147464 | tf_op jit(solution)/shard_map/ppermute | solution.py:293
  124.6 1.9 %collective-permute-start.19 = (bf16[6,32,128]{2,1,0:T(8,128)(2,1)S(1)}, bf16[6,32,128]{2,1,0:T(8,128)(2,1)S(1)}, u32[]{:S(2)}, u32[]{:S(2)}) collective-permute-start(bf16[6,32,128]{2,1,0:T(8,128)(2,1)S(1)} %fusion.7), channel_id=1, source_target_pairs={{0,1},{1,0},{2,3},{3,2},{4,5},{5,4},{6,7},{7,6},{8,9},{9,8},{10,11... | collective-permute-start | bytes 147464 | tf_op jit(solution)/shard_map/ppermute | solution.py:296
  124.7 4.2 %collective-permute-start.20 = (bf16[6,32,128]{2,1,0:T(8,128)(2,1)S(1)}, bf16[6,32,128]{2,1,0:T(8,128)(2,1)S(1)}, u32[]{:S(2)}, u32[]{:S(2)}) collective-permute-start(bf16[6,32,128]{2,1,0:T(8,128)(2,1)S(1)} %fusion.7), channel_id=1, source_target_pairs={{0,2},{1,3},{2,0},{3,1},{4,6},{5,7},{6,4},{7,5},{8,10},{9,11},{10,... | collective-permute-start | bytes 147464 | tf_op jit(solution)/shard_map/ppermute | solution.py:296
  126.2 3.7 %collective-permute-start.21 = (bf16[6,32,128]{2,1,0:T(8,128)(2,1)S(1)}, bf16[6,32,128]{2,1,0:T(8,128)(2,1)S(1)}, u32[]{:S(2)}, u32[]{:S(2)}) collective-permute-start(bf16[6,32,128]{2,1,0:T(8,128)(2,1)S(1)} %fusion.7), channel_id=1, source_target_pairs={{0,3},{1,2},{2,1},{3,0},{4,7},{5,6},{6,5},{7,4},{8,11},{9,10},{10,... | collective-permute-start | bytes 147464 | tf_op jit(solution)/shard_map/ppermute | solution.py:296
  (8 other events, 23.2 us)

commit v4 on v3

--- a/solution.py
+++ b/solution.py
@@ -139,7 +139,7 @@
 
 def contract_kernel(owners, rows, place_ref, plan_ref, blocks_ref, others_ref, *refs):
     pieces = refs[:MEMBERS]
-    own_ref, same_ref, cross_ref, stack_ref, sum_ref, sems = refs[MEMBERS:]
+    own_ref, same_ref, cross_ref, again_ref, stack_ref, sum_ref, sems = refs[MEMBERS:]
     virt = own_ref.shape[0]
     copies = [
         pltpu.make_async_copy(ref, stack_ref.at[pl.ds(d * virt, virt)], sems.at[d])
@@ -171,7 +171,9 @@
     own = sum_ref[pl.ds(0, virt), pl.ds(0, rows), :]
     own_ref[...] = own
     same_ref[...] = own.astype(same_ref.dtype)
-    cross_ref[...] = sum_ref[pl.ds(0, virt), pl.ds(rows, rows), :].astype(cross_ref.dtype)
+    cross = sum_ref[pl.ds(0, virt), pl.ds(rows, rows), :].astype(cross_ref.dtype)
+    cross_ref[...] = cross
+    again_ref[...] = cross
     for copy in copies:
         copy.wait()
 
@@ -182,9 +184,9 @@
     stack = jax.ShapeDtypeStruct((MEMBERS * virt, chunk, depth), jnp.bfloat16)
     return pl.pallas_call(
         lambda *refs: contract_kernel(owners, rows, *refs),
-        out_shape=(jax.ShapeDtypeStruct((virt, rows, chunk), jnp.float32), sent, sent, stack),
+        out_shape=(jax.ShapeDtypeStruct((virt, rows, chunk), jnp.float32), sent, sent, sent, stack),
         in_specs=[SMEM_SPEC] * 2 + [VMEM_SPEC] * (2 + len(factors)),
-        out_specs=(VMEM_SPEC,) * 3 + (pl.BlockSpec(memory_space=pl.ANY),),
+        out_specs=(VMEM_SPEC,) * 4 + (pl.BlockSpec(memory_space=pl.ANY),),
         scratch_shapes=[
             pltpu.VMEM((virt + 1, 2 * rows, chunk), jnp.float32),
             pltpu.SemaphoreType.DMA((MEMBERS,)),
@@ -264,6 +266,28 @@
         input_output_aliases={i: i for i in range(len(values))},
         name="touch",
     )(*values, *others)
+
+
+def gather_kernel(place_ref, *refs):
+    out_ref = refs[-1]
+    shares = len(refs) - 1
+    rows = out_ref.shape[1] // shares
+    for a, ref in enumerate(refs[:-1]):
+        share = place_ref[0] ^ a
+        start = ((share & 1) * (shares // 2) + (share >> 1)) * rows
+        out_ref[:, pl.ds(pl.multiple_of(start, rows), rows), :] = ref[...]
+
+
+def gather(share, pieces):
+    slots, rows, depth = pieces[0].shape
+    return pl.pallas_call(
+        gather_kernel,
+        out_shape=jax.ShapeDtypeStruct((slots, rows * len(pieces), depth), pieces[0].dtype),
+        in_specs=[SMEM_SPEC] + [VMEM_SPEC] * len(pieces),
+        out_specs=VMEM_SPEC,
+        compiler_params=PARAMS,
+        name="gather",
+    )(share.reshape(1).astype(jnp.int32), *pieces)
 
 
 def after(value, *others):
@@ -315,18 +339,18 @@
     meta = blocks[:, slots * rows : slots * rows + slots, :3].astype(jnp.int32)
     listed = plan(meta.reshape(total, 3), slots, pairs, virt)
 
-    full = lax.all_to_all(after(full, near), "pair", 0, 0, tiled=True)
-    for d in (1, 3):
+    full = lax.all_to_all(touch([jnp.transpose(full, (0, 2, 1, 3))], near)[0], "pair", 0, 0, tiled=True)
+    for d in (3,):
         pieces[d] = after(pieces[d], near)
 
     others = over_aux(blocks, 1)
     mine = [over_pair(pieces[d], d) for d in range(1, MEMBERS)]
     mine = [pieces[0], *touch(mine, listed, others)]
-    own, same, cross, stack = contract(place, listed, blocks, others, mine, pairs, virt, rows)
+    own, same, cross, again, stack = contract(place, listed, blocks, others, mine, pairs, virt, rows)
     got = over_pair(same, MEMBERS), over_both(cross, MEMBERS, 1)
-    own = own, over_aux(cross, 1)
+    own = own, over_aux(again, 1)
     work = list(zip(own, got, (mine, [over_aux(stack, 1)])))
-    full = jnp.transpose(after(full, same), (0, 2, 1, 3)).reshape(pairs * virt, full_chunk, depth)
+    full = after(full, same).reshape(pairs * virt, full_chunk, depth)
     out = None
     for held in (full, over_aux(full, 1)):
         out = whole(listed, blocks, held, out, pairs, virt, rows, total)
@@ -349,10 +373,7 @@
         value = over_pair(summed[i], 2 * i).astype(jnp.float32)
         home = value if home is None else home + value
     result = home.astype(jnp.bfloat16)
-    quarters = jnp.stack([result] + [over_aux(result, a) for a in range(1, shares)])
-    order = lax.iota(jnp.int32, shares)
-    order = ((order % wide) * 2 + order // wide) ^ share
-    return jnp.transpose(quarters[order], (1, 0, 2, 3)).reshape(slots, width, depth)
+    return gather(share, [result] + [over_aux(result, a) for a in range(1, shares)])
 
 
 def far_plan(factors, amplitudes, block_list, owner_map):
@@ -431,9 +452,14 @@
     return result.astype(jnp.bfloat16).reshape(block_count, block_width, block_width)
 
 
+def on_device(factors, amplitudes, block_list, owner_map):
+    fits = amplitudes.shape[0] < META and factors.shape[2] < META
+    plan_of = near_plan if lax.axis_size("pair") == 2 * MEMBERS and fits else far_plan
+    return plan_of(factors, amplitudes, block_list, owner_map)
+
+
 def solution(mesh):
     placed = (P("pair", "aux", None, None), P("pair", None, None), P("pair", None), P())
-    on_device = near_plan if mesh.shape["pair"] == 2 * MEMBERS else far_plan
     return jax.shard_map(
         on_device, mesh=mesh, in_specs=placed, out_specs=P("pair", None, None), check_vma=False
     )

time: 132 us -> 130 us (0.985)
  waiting for transfers between devices: 62.3 us -> 58.5 us
    ppermute x11, waiting for transfers between devices: 47.2 us -> 42.8 us  [over_pair(): lax.ppermute(value, 'pair', [(i, i ^ distance) for i in range(pairs)])]
    unnamed x22 -> x24, local copies, waits for them, and re-layouts: 5.6 us -> 7.61 us
    transpose x2 -> x0, local copies, waits for them, and re-layouts: 1.85 us -> none  [the longest x1 1.15 us: near_plan(): pieces = [jnp.transpose(piece, (1, 0, 2)) for piece in pieces]]
    dynamic_slice x3 -> x5, local copies, waits for them, and re-layouts: 2.61 us -> 4.35 us  [near_plan(): lax.dynamic_slice_in_dim(factors, start, chunk, 0)]
  transfers between devices with their start and end apart: 23 -> 23, of which waited for: 13 -> 11; matrix products, arithmetic and copies ran while one was open for 8% -> 9% of each run, Pallas kernels for 16% -> 16%
where the time goes in v4:
time: 130 us
  waiting for transfers between devices  58.5 us (45%)
  starting transfers between devices  29.9 us (23%)
  Pallas kernels  24.4 us (19%)
  local copies, waits for them, and re-layouts  15.6 us (12%)
    ppermute x11, waiting for transfers between devices, over_pair(): lax.ppermute(value, 'pair', [(i, i ^ distance) for i in range(pairs)])  42.8 us
    ppermute x11, starting transfers between devices, over_pair(): lax.ppermute(value, 'pair', [(i, i ^ distance) for i in range(pairs)])  18.8 us
    pallas_call x2, Pallas kernels, whole(): pl.pallas_call(lambda *refs: whole_kernel(owners, rows, virt, *refs), out...  12 us
    ppermute x4, waiting for transfers between devices, over_both(): return lax.ppermute(value, ('pair', 'aux'), route)  10.6 us
    unnamed x24, local copies, waits for them, and re-layouts  7.61 us
    all_to_all x1, starting transfers between devices, near_plan(): lax.all_to_all(touch([jnp.transpose(full, (0, 2, 1, 3))], near)[0], 'pair...  4.88 us
    pallas_call x2, Pallas kernels, project(): pl.pallas_call(lambda *refs: project_kernel(owners, *refs), out_shape=jax...  4.61 us
    dynamic_slice x5, local copies, waits for them, and re-layouts, near_plan(): lax.dynamic_slice_in_dim(factors, start, chunk, 0)  4.35 us
  transfers between devices with their start and end apart: 23, of which 11 were waited for; matrix products, arithmetic and copies ran while one was open for 9% of the time, Pallas kernels for 16%

profile of v4, /device:TPU:0, one launch (start us, length us, event | category | flops | bytes accessed | tf_op | source)
XLA Modules:
  0.0 129.6 jit_solution(10684828098337196360)
XLA Ops:
  2.3 3.1 %collective-permute-start = (bf16[400,128]{1,0:T(8,128)(2,1)S(1)}, bf16[400,128]{1,0:T(8,128)(2,1)S(1)}, u32[]{:S(2)}, u32[]{:S(2)}) collective-permute-start(bf16[400,128]{1,0:T(8,128)(2,1)S(1)} %pack.1), channel_id=1, source_target_pairs={{0,8},{4,12},{8,0},{12,4},{16,24},{20,28},{24,16},{28,20},{1,9},{5... | collective-permute-start | bytes 307208 | tf_op jit(solution)/shard_map/ppermute | solution.py:317
  5.4 2.6 %collective-permute-start.1 = (bf16[400,128]{1,0:T(8,128)(2,1)S(1)}, bf16[400,128]{1,0:T(8,128)(2,1)S(1)}, u32[]{:S(2)}, u32[]{:S(2)}) collective-permute-start(bf16[400,128]{1,0:T(8,128)(2,1)S(1)} %pack.1), channel_id=1, source_target_pairs={{0,16},{4,20},{8,24},{12,28},{16,0},{20,4},{24,8},{28,12},{1,17},{... | collective-permute-start | bytes 307208 | tf_op jit(solution)/shard_map/ppermute | solution.py:317
  8.0 1.7 %constant_dynamic-slice_fusion = (bf16[1,256,8,128]{3,2,1,0:T(8,128)(2,1)S(1)}, bf16[1,256,8,128]{3,2,1,0:T(8,128)(2,1)S(1)}, bf16[1,256,8,128]{3,2,1,0:T(8,128)(2,1)S(1)}, bf16[1,256,8,128]{3,2,1,0:T(8,128)(2,1)S(1)}) fusion(bf16[1,2048,8,128]{3,2,1,0:T(8,128)(2,1)} %param.4, s32[]{:T(128)S(6)} %select_n.22, s32[]{:T(128)S(6)} %select_n.20, ...), kind=kLoop, calls=%fused_computation.31 | loop fusion | bytes 4194320 | tf_op jit(solution)/shard_map/dynamic_slice | solution.py:333
  10.6 1.7 %collective-permute-start.5 = (bf16[8,256,128]{2,1,0:T(8,128)(2,1)}, bf16[8,256,128]{2,1,0:T(8,128)(2,1)}, u32[]{:S(2)}, u32[]{:S(2)}) collective-permute-start(bf16[8,256,128]{2,1,0:T(8,128)(2,1)} %bitcast.66), channel_id=1, source_target_pairs={{0,4},{4,0},{8,12},{12,8},{16,20},{20,16},{24,28},{28,24},{1,5},{5... | collective-permute-start | bytes 1572872 | tf_op jit(solution)/shard_map/ppermute | solution.py:317
  15.5 2.0 %copy.41 = bf16[8,128,8,128]{3,1,2,0:T(8,128)(2,1)} copy(bf16[8,128,8,128]{3,2,1,0:T(8,128)(2,1)S(1)} %bitcast.72) | data formatting | bytes 4194304 | tf_op jit(solution)/shard_map/optimization_barrier | solution.py:331
  18.1 2.3 %collective-permute-start.7 = (bf16[8,256,128]{2,1,0:T(8,128)(2,1)}, bf16[8,256,128]{2,1,0:T(8,128)(2,1)}, u32[]{:S(2)}, u32[]{:S(2)}) collective-permute-start(bf16[8,256,128]{2,1,0:T(8,128)(2,1)} %bitcast.64), channel_id=1, source_target_pairs={{0,12},{4,8},{8,4},{12,0},{16,28},{20,24},{24,20},{28,16},{1,13},{... | collective-permute-start | bytes 1572872 | tf_op jit(solution)/shard_map/ppermute | solution.py:317
  20.4 4.9 %all-to-all-start = ((bf16[8,8,128,128]{3,2,1,0:T(8,128)(2,1)}), bf16[8,8,128,128]{3,2,1,0:T(8,128)(2,1)}, u32[]{:S(2)}, u32[]{:S(2)}) async-start(bf16[8,8,128,128]{3,2,1,0:T(8,128)(2,1)} %touch.3), calls=%async_computation | async-start | bytes 4194304 | tf_op jit(solution)/shard_map/all_to_all | solution.py:342
  27.2 33.2 %collective-permute-done.3 = bf16[4,400,128]{2,1,0:T(8,128)(2,1)S(1)} collective-permute-done((bf16[4,400,128]{2,1,0:T(8,128)(2,1)S(1)}, bf16[4,400,128]{2,1,0:T(8,128)(2,1)S(1)}, u32[]{:S(2)}, u32[]{:S(2)}) %collective-permute-start.3) | collective-permute-done | bytes 409632 | tf_op jit(solution)/shard_map/ppermute | solution.py:317
  62.5 2.2 %plan.1.refs_3_.refs_1_.refs_0_ = s32[456]{0:T(512)} custom-call(s32[48,3]{1,0:T(8,128)} %reshape.45.refs_0_), custom_call_target="tpu_custom_call" | custom-call | flops 9999999827968 | tf_op jit(solution)/shard_map/plan/pallas_call | solution.py:80
  65.4 4.2 %contract.1 = (f32[8,64,256]{2,1,0:T(8,128)S(1)}, bf16[8,64,256]{2,1,0:T(8,128)(2,1)}, bf16[8,64,256]{2,1,0:T(8,128)(2,1)S(1)}, bf16[8,64,256]{2,1,0:T(8,128)(2,1)S(1)}, bf16[32,256,128]{2,1,0:T(8,128)(2,1)S(1)}) custom-call(s32[2]{0:T(128)S(1)} %copy-done.3, s32[456]{0:T(512)S(1)} %copy-done.1, ...), custom_call_target="tpu_custom_call" | custom-call | flops 9999999827968 | tf_op jit(solution)/shard_map/contract/pallas_call | solution.py:185
  72.4 1.7 %all-to-all-done = bf16[8,8,128,128]{3,2,1,0:T(8,128)(2,1)} async-done(((bf16[8,8,128,128]{3,2,1,0:T(8,128)(2,1)}), bf16[8,8,128,128]{3,2,1,0:T(8,128)(2,1)}, u32[]{:S(2)}, u32[]{:S(2)}) %all-to-all-start) | async-done | bytes 2097184 | tf_op jit(solution)/shard_map/all_to_all | solution.py:342
  74.6 3.4 %collective-permute-start.10 = (bf16[8,64,256]{2,1,0:T(8,128)(2,1)}, bf16[8,64,256]{2,1,0:T(8,128)(2,1)}, u32[]{:S(2)}, u32[]{:S(2)}) collective-permute-start(bf16[8,64,256]{2,1,0:T(8,128)(2,1)} %get-tuple-element.27), channel_id=1, source_target_pairs={{0,16},{4,20},{8,24},{12,28},{16,0},{20,4},{24,8},{28,12},{1,17},{... | collective-permute-start | bytes 786440 | tf_op jit(solution)/shard_map/ppermute | solution.py:317
  78.1 6.0 %whole.2.refs_3_ = f32[49,64,128]{2,1,0:T(8,128)S(1)} custom-call(s32[456]{0:T(512)S(1)} %copy-done.1, bf16[8,400,128]{2,1,0:T(8,128)(2,1)} %constant_dynamic-update-slice_fusion.refs_2_.refs_1_, bf16[64,128,128]{2,1,0:T(8,128)(2,1)} %bitcast.17.refs_2_), custom_call_target="tpu_custom_call" | custom-call | tf_op jit(solution)/shard_map/whole/pallas_call | solution.py:215
  84.1 6.0 %whole.3.refs_4_ = f32[49,64,128]{2,1,0:T(8,128)S(1)} custom-call(s32[456]{0:T(512)S(1)} %copy-done.1, bf16[8,400,128]{2,1,0:T(8,128)(2,1)} %constant_dynamic-update-slice_fusion.refs_2_.refs_1_, bf16[64,128,128]{2,1,0:T(8,128)(2,1)} %collective-permute-done.11.refs_2_, f32[49,64,128]{2,1,0:T(8,128)S(1)} %whole.2.refs_3_), custom_call_target="tpu_custom_call" | custom-call | tf_op jit(solution)/shard_map/whole/pallas_call | solution.py:215
  90.2 6.5 %collective-permute-done.10.refs_3_ = bf16[8,64,256]{2,1,0:T(8,128)(2,1)} collective-permute-done((bf16[8,64,256]{2,1,0:T(8,128)(2,1)}, bf16[8,64,256]{2,1,0:T(8,128)(2,1)}, u32[]{:S(2)}, u32[]{:S(2)}) %collective-permute-start.10) | collective-permute-done | bytes 262176 | tf_op jit(solution)/shard_map/ppermute | solution.py:317
  96.6 2.5 %project.2.refs_4_ = f32[49,64,128]{2,1,0:T(8,128)S(1)} custom-call(s32[2]{0:T(128)S(1)} %copy-done.3, s32[456]{0:T(512)S(1)} %copy-done.1, f32[8,64,256]{2,1,0:T(8,128)S(1)} %get-tuple-element.26.refs_2_, bf16[8,64,256]{2,1,0:T(8,128)(2,1)} %collective-permute-done.10.refs_3_, f32[49,64,128]{2,1,0:T(8,128)S(1)} %whole.3.refs_4_, ...), custom_call_target="tpu_custom_call" | custom-call | tf_op jit(solution)/shard_map/project/pallas_call | solution.py:246
  99.2 1.8 %collective-permute-done.9.refs_3_ = bf16[8,64,256]{2,1,0:T(8,128)(2,1)} collective-permute-done((bf16[8,64,256]{2,1,0:T(8,128)(2,1)}, bf16[8,64,256]{2,1,0:T(8,128)(2,1)}, u32[]{:S(2)}, u32[]{:S(2)}) %collective-permute-start.9) | collective-permute-done | bytes 262176 | tf_op jit(solution)/shard_map/ppermute | solution.py:328
  101.0 2.1 %project.3 = f32[49,64,128]{2,1,0:T(8,128)S(1)} custom-call(s32[2]{0:T(128)S(1)} %copy-done.3, s32[456]{0:T(512)S(1)} %copy-done.1, bf16[8,64,256]{2,1,0:T(8,128)(2,1)S(1)} %collective-permute-done.8.refs_2_, bf16[8,64,256]{2,1,0:T(8,128)(2,1)} %collective-permute-done.9.refs_3_, f32[49,64,128]{2,1,0:T(8,128)S(1)} %project.2.refs_4_, ...), custom_call_target="tpu_custom_call" | custom-call | tf_op jit(solution)/shard_map/project/pallas_call | solution.py:246
  107.0 5.1 %collective-permute-done.15 = bf16[4,6,32,128]{3,2,1,0:T(8,128)(2,1)S(1)} collective-permute-done((bf16[4,6,32,128]{3,2,1,0:T(8,128)(2,1)S(1)}, bf16[4,6,32,128]{3,2,1,0:T(8,128)(2,1)S(1)}, u32[]{:S(2)}, u32[]{:S(2)}) %collective-permute-start.15) | collective-permute-done | bytes 196640 | tf_op jit(solution)/shard_map/ppermute | solution.py:328
  112.1 2.6 %collective-permute-done.14 = bf16[4,6,32,128]{3,2,1,0:T(8,128)(2,1)S(1)} collective-permute-done((bf16[4,6,32,128]{3,2,1,0:T(8,128)(2,1)S(1)}, bf16[4,6,32,128]{3,2,1,0:T(8,128)(2,1)S(1)}, u32[]{:S(2)}, u32[]{:S(2)}) %collective-permute-start.14) | collective-permute-done | bytes 196640 | tf_op jit(solution)/shard_map/ppermute | solution.py:328
  115.9 2.5 %collective-permute-start.18 = (bf16[6,32,128]{2,1,0:T(8,128)(2,1)S(1)}, bf16[6,32,128]{2,1,0:T(8,128)(2,1)S(1)}, u32[]{:S(2)}, u32[]{:S(2)}) collective-permute-start(bf16[6,32,128]{2,1,0:T(8,128)(2,1)S(1)} %get-tuple-element.38), channel_id=1, source_target_pairs={{0,24},{4,28},{8,16},{12,20},{16,8},{20,12},{24,0},{28,4},{1,25},{... | collective-permute-start | bytes 147464 | tf_op jit(solution)/shard_map/ppermute | solution.py:317
  118.4 2.0 %collective-permute-start.16 = (bf16[6,32,128]{2,1,0:T(8,128)(2,1)S(1)}, bf16[6,32,128]{2,1,0:T(8,128)(2,1)S(1)}, u32[]{:S(2)}, u32[]{:S(2)}) collective-permute-start(bf16[6,32,128]{2,1,0:T(8,128)(2,1)S(1)} %get-tuple-element.37), channel_id=1, source_target_pairs={{0,8},{4,12},{8,0},{12,4},{16,24},{20,28},{24,16},{28,20},{1,9},{5... | collective-permute-start | bytes 147464 | tf_op jit(solution)/shard_map/ppermute | solution.py:317
  120.4 1.6 %collective-permute-done.18 = bf16[6,32,128]{2,1,0:T(8,128)(2,1)S(1)} collective-permute-done((bf16[6,32,128]{2,1,0:T(8,128)(2,1)S(1)}, bf16[6,32,128]{2,1,0:T(8,128)(2,1)S(1)}, u32[]{:S(2)}, u32[]{:S(2)}) %collective-permute-start.18) | collective-permute-done | bytes 49184 | tf_op jit(solution)/shard_map/ppermute | solution.py:317
  125.5 2.3 %collective-permute-done.20.refs_2_ = bf16[6,32,128]{2,1,0:T(8,128)(2,1)S(1)} collective-permute-done((bf16[6,32,128]{2,1,0:T(8,128)(2,1)S(1)}, bf16[6,32,128]{2,1,0:T(8,128)(2,1)S(1)}, u32[]{:S(2)}, u32[]{:S(2)}) %collective-permute-start.20) | collective-permute-done | bytes 49184 | tf_op jit(solution)/shard_map/ppermute | solution.py:320
  (76 shorter events, 25.5 us)
Async XLA Ops:
  2.3 15.1 %collective-permute-start = (bf16[400,128]{1,0:T(8,128)(2,1)S(1)}, bf16[400,128]{1,0:T(8,128)(2,1)S(1)}, u32[]{:S(2)}, u32[]{:S(2)}) collective-permute-start(bf16[400,128]{1,0:T(8,128)(2,1)S(1)} %pack.1), channel_id=1, source_target_pairs={{0,8},{4,12},{8,0},{12,4},{16,24},{20,28},{24,16},{28,20},{1,9},{5... | collective-permute-start | bytes 307208 | tf_op jit(solution)/shard_map/ppermute | solution.py:317
  5.4 12.0 %collective-permute-start.1 = (bf16[400,128]{1,0:T(8,128)(2,1)S(1)}, bf16[400,128]{1,0:T(8,128)(2,1)S(1)}, u32[]{:S(2)}, u32[]{:S(2)}) collective-permute-start(bf16[400,128]{1,0:T(8,128)(2,1)S(1)} %pack.1), channel_id=1, source_target_pairs={{0,16},{4,20},{8,24},{12,28},{16,0},{20,4},{24,8},{28,12},{1,17},{... | collective-permute-start | bytes 307208 | tf_op jit(solution)/shard_map/ppermute | solution.py:317
  8.0 9.4 %collective-permute-start.2 = (bf16[400,128]{1,0:T(8,128)(2,1)S(1)}, bf16[400,128]{1,0:T(8,128)(2,1)S(1)}, u32[]{:S(2)}, u32[]{:S(2)}) collective-permute-start(bf16[400,128]{1,0:T(8,128)(2,1)S(1)} %pack.1), channel_id=1, source_target_pairs={{0,24},{4,28},{8,16},{12,20},{16,8},{20,12},{24,0},{28,4},{1,25},{... | collective-permute-start | bytes 307208 | tf_op jit(solution)/shard_map/ppermute | solution.py:317
  9.7 5.8 %slice-start = ((bf16[1,2048,8,128]{3,2,1,0:T(8,128)(2,1)}), bf16[1,1024,8,128]{3,2,1,0:T(8,128)(2,1)S(1)}, s32[]{:S(2)}) async-start(bf16[1,2048,8,128]{3,2,1,0:T(8,128)(2,1)} %param.4), calls=%async_computation.1 | async-start | bytes 4194304 | tf_op jit(solution)/shard_map/slice | solution.py:330
  10.6 54.2 %collective-permute-start.5 = (bf16[8,256,128]{2,1,0:T(8,128)(2,1)}, bf16[8,256,128]{2,1,0:T(8,128)(2,1)}, u32[]{:S(2)}, u32[]{:S(2)}) collective-permute-start(bf16[8,256,128]{2,1,0:T(8,128)(2,1)} %bitcast.66), channel_id=1, source_target_pairs={{0,4},{4,0},{8,12},{12,8},{16,20},{20,16},{24,28},{28,24},{1,5},{5... | collective-permute-start | bytes 1572872 | tf_op jit(solution)/shard_map/ppermute | solution.py:317
  13.2 51.6 %collective-permute-start.6 = (bf16[8,256,128]{2,1,0:T(8,128)(2,1)}, bf16[8,256,128]{2,1,0:T(8,128)(2,1)}, u32[]{:S(2)}, u32[]{:S(2)}) collective-permute-start(bf16[8,256,128]{2,1,0:T(8,128)(2,1)} %bitcast.65), channel_id=1, source_target_pairs={{0,8},{4,12},{8,0},{12,4},{16,24},{20,28},{24,16},{28,20},{1,9},{5... | collective-permute-start | bytes 1572872 | tf_op jit(solution)/shard_map/ppermute | solution.py:317
  17.5 42.9 %collective-permute-start.3 = (bf16[4,400,128]{2,1,0:T(8,128)(2,1)S(1)}, bf16[4,400,128]{2,1,0:T(8,128)(2,1)S(1)}, u32[]{:S(2)}, u32[]{:S(2)}) collective-permute-start(bf16[4,400,128]{2,1,0:T(8,128)(2,1)S(1)} %pad_maximum_fusion.refs_1_), channel_id=1, source_target_pairs={{0,4},{4,0},{8,12},{12,8},{16,20},{20,16},{24,28},{28,24},{1,5},{5... | collective-permute-start | bytes 1228808 | tf_op jit(solution)/shard_map/ppermute | solution.py:317
  18.1 46.7 %collective-permute-start.7 = (bf16[8,256,128]{2,1,0:T(8,128)(2,1)}, bf16[8,256,128]{2,1,0:T(8,128)(2,1)}, u32[]{:S(2)}, u32[]{:S(2)}) collective-permute-start(bf16[8,256,128]{2,1,0:T(8,128)(2,1)} %bitcast.64), channel_id=1, source_target_pairs={{0,12},{4,8},{8,4},{12,0},{16,28},{20,24},{24,20},{28,16},{1,13},{... | collective-permute-start | bytes 1572872 | tf_op jit(solution)/shard_map/ppermute | solution.py:317
  20.4 53.7 %all-to-all-start = ((bf16[8,8,128,128]{3,2,1,0:T(8,128)(2,1)}), bf16[8,8,128,128]{3,2,1,0:T(8,128)(2,1)}, u32[]{:S(2)}, u32[]{:S(2)}) async-start(bf16[8,8,128,128]{3,2,1,0:T(8,128)(2,1)} %touch.3), calls=%async_computation | async-start | bytes 4194304 | tf_op jit(solution)/shard_map/all_to_all | solution.py:342
  61.9 2.9 %collective-permute-start.4 = (bf16[8,400,128]{2,1,0:T(8,128)(2,1)}, bf16[8,400,128]{2,1,0:T(8,128)(2,1)}, u32[]{:S(2)}, u32[]{:S(2)}) collective-permute-start(bf16[8,400,128]{2,1,0:T(8,128)(2,1)} %constant_dynamic-update-slice_fusion.refs_2_.refs_1_), channel_id=1, source_target_pairs={{0,1},{1,0},{2,3},{3,2},{4,5},{5,4},{6,7},{7,6},{8,9},{9,8},{10,11... | collective-permute-start | bytes 2457608 | tf_op jit(solution)/shard_map/ppermute | solution.py:320
  74.1 10.0 %collective-permute-start.11 = (bf16[64,128,128]{2,1,0:T(8,128)(2,1)}, bf16[64,128,128]{2,1,0:T(8,128)(2,1)}, u32[]{:S(2)}, u32[]{:S(2)}) collective-permute-start(bf16[64,128,128]{2,1,0:T(8,128)(2,1)} %bitcast.17.refs_2_), channel_id=1, source_target_pairs={{0,1},{1,0},{2,3},{3,2},{4,5},{5,4},{6,7},{7,6},{8,9},{9,8},{10,11... | collective-permute-start | bytes 6291464 | tf_op jit(solution)/shard_map/ppermute | solution.py:320
  74.1 26.9 %collective-permute-start.12 = (bf16[32,256,128]{2,1,0:T(8,128)(2,1)}, bf16[32,256,128]{2,1,0:T(8,128)(2,1)S(1)}, u32[]{:S(2)}, u32[]{:S(2)}) collective-permute-start(bf16[32,256,128]{2,1,0:T(8,128)(2,1)} %copy-done.5), channel_id=1, source_target_pairs={{0,1},{1,0},{2,3},{3,2},{4,5},{5,4},{6,7},{7,6},{8,9},{9,8},{10,11... | collective-permute-start | bytes 6291464 | tf_op jit(solution)/shard_map/ppermute | solution.py:320
  74.6 22.0 %collective-permute-start.10 = (bf16[8,64,256]{2,1,0:T(8,128)(2,1)}, bf16[8,64,256]{2,1,0:T(8,128)(2,1)}, u32[]{:S(2)}, u32[]{:S(2)}) collective-permute-start(bf16[8,64,256]{2,1,0:T(8,128)(2,1)} %get-tuple-element.27), channel_id=1, source_target_pairs={{0,16},{4,20},{8,24},{12,28},{16,0},{20,4},{24,8},{28,12},{1,17},{... | collective-permute-start | bytes 786440 | tf_op jit(solution)/shard_map/ppermute | solution.py:317
  78.0 21.2 %collective-permute-start.8 = (bf16[8,64,256]{2,1,0:T(8,128)(2,1)}, bf16[8,64,256]{2,1,0:T(8,128)(2,1)S(1)}, u32[]{:S(2)}, u32[]{:S(2)}) collective-permute-start(bf16[8,64,256]{2,1,0:T(8,128)(2,1)} %copy-done.7), channel_id=1, source_target_pairs={{0,1},{1,0},{2,3},{3,2},{4,5},{5,4},{6,7},{7,6},{8,9},{9,8},{10,11... | collective-permute-start | bytes 786440 | tf_op jit(solution)/shard_map/ppermute | solution.py:320
  78.0 23.0 %collective-permute-start.9 = (bf16[8,64,256]{2,1,0:T(8,128)(2,1)}, bf16[8,64,256]{2,1,0:T(8,128)(2,1)}, u32[]{:S(2)}, u32[]{:S(2)}) collective-permute-start(bf16[8,64,256]{2,1,0:T(8,128)(2,1)} %copy-done.6), channel_id=1, source_target_pairs={{0,17},{1,16},{2,19},{3,18},{4,21},{5,20},{6,23},{7,22},{8,25},{9,... | collective-permute-start | bytes 786440 | tf_op jit(solution)/shard_map/ppermute | solution.py:328
  103.4 8.7 %collective-permute-start.15 = (bf16[4,6,32,128]{3,2,1,0:T(8,128)(2,1)S(1)}, bf16[4,6,32,128]{3,2,1,0:T(8,128)(2,1)S(1)}, u32[]{:S(2)}, u32[]{:S(2)}) collective-permute-start(bf16[4,6,32,128]{3,2,1,0:T(8,128)(2,1)S(1)} %get-tuple-element.36), channel_id=1, source_target_pairs={{0,6},{1,7},{2,4},{3,5},{4,2},{5,3},{6,0},{7,1},{8,14},{9,15},{10,... | collective-permute-start | bytes 589832 | tf_op jit(solution)/shard_map/ppermute | solution.py:328
  105.0 9.7 %collective-permute-start.14 = (bf16[4,6,32,128]{3,2,1,0:T(8,128)(2,1)S(1)}, bf16[4,6,32,128]{3,2,1,0:T(8,128)(2,1)S(1)}, u32[]{:S(2)}, u32[]{:S(2)}) collective-permute-start(bf16[4,6,32,128]{3,2,1,0:T(8,128)(2,1)S(1)} %get-tuple-element.35), channel_id=1, source_target_pairs={{0,2},{1,3},{2,0},{3,1},{4,6},{5,7},{6,4},{7,5},{8,10},{9,11},{10,... | collective-permute-start | bytes 589832 | tf_op jit(solution)/shard_map/ppermute | solution.py:328
  105.6 10.3 %collective-permute-start.13 = (bf16[4,6,32,128]{3,2,1,0:T(8,128)(2,1)S(1)}, bf16[4,6,32,128]{3,2,1,0:T(8,128)(2,1)S(1)}, u32[]{:S(2)}, u32[]{:S(2)}) collective-permute-start(bf16[4,6,32,128]{3,2,1,0:T(8,128)(2,1)S(1)} %fusion.4), channel_id=1, source_target_pairs={{0,4},{1,5},{2,6},{3,7},{4,0},{5,1},{6,2},{7,3},{8,12},{9,13},{10,... | collective-permute-start | bytes 589832 | tf_op jit(solution)/shard_map/ppermute | solution.py:328
  115.9 6.1 %collective-permute-start.18 = (bf16[6,32,128]{2,1,0:T(8,128)(2,1)S(1)}, bf16[6,32,128]{2,1,0:T(8,128)(2,1)S(1)}, u32[]{:S(2)}, u32[]{:S(2)}) collective-permute-start(bf16[6,32,128]{2,1,0:T(8,128)(2,1)S(1)} %get-tuple-element.38), channel_id=1, source_target_pairs={{0,24},{4,28},{8,16},{12,20},{16,8},{20,12},{24,0},{28,4},{1,25},{... | collective-permute-start | bytes 147464 | tf_op jit(solution)/shard_map/ppermute | solution.py:317
  118.4 5.1 %collective-permute-start.17 = (bf16[6,32,128]{2,1,0:T(8,128)(2,1)S(1)}, bf16[6,32,128]{2,1,0:T(8,128)(2,1)S(1)}, u32[]{:S(2)}, u32[]{:S(2)}) collective-permute-start(bf16[6,32,128]{2,1,0:T(8,128)(2,1)S(1)} %get-tuple-element.39), channel_id=1, source_target_pairs={{0,16},{4,20},{8,24},{12,28},{16,0},{20,4},{24,8},{28,12},{1,17},{... | collective-permute-start | bytes 147464 | tf_op jit(solution)/shard_map/ppermute | solution.py:317
  118.4 5.1 %collective-permute-start.16 = (bf16[6,32,128]{2,1,0:T(8,128)(2,1)S(1)}, bf16[6,32,128]{2,1,0:T(8,128)(2,1)S(1)}, u32[]{:S(2)}, u32[]{:S(2)}) collective-permute-start(bf16[6,32,128]{2,1,0:T(8,128)(2,1)S(1)} %get-tuple-element.37), channel_id=1, source_target_pairs={{0,8},{4,12},{8,0},{12,4},{16,24},{20,28},{24,16},{28,20},{1,9},{5... | collective-permute-start | bytes 147464 | tf_op jit(solution)/shard_map/ppermute | solution.py:317
  123.6 1.9 %collective-permute-start.19 = (bf16[6,32,128]{2,1,0:T(8,128)(2,1)S(1)}, bf16[6,32,128]{2,1,0:T(8,128)(2,1)S(1)}, u32[]{:S(2)}, u32[]{:S(2)}) collective-permute-start(bf16[6,32,128]{2,1,0:T(8,128)(2,1)S(1)} %fusion.7.refs_0_), channel_id=1, source_target_pairs={{0,1},{1,0},{2,3},{3,2},{4,5},{5,4},{6,7},{7,6},{8,9},{9,8},{10,11... | collective-permute-start | bytes 147464 | tf_op jit(solution)/shard_map/ppermute | solution.py:320
  123.7 4.2 %collective-permute-start.20 = (bf16[6,32,128]{2,1,0:T(8,128)(2,1)S(1)}, bf16[6,32,128]{2,1,0:T(8,128)(2,1)S(1)}, u32[]{:S(2)}, u32[]{:S(2)}) collective-permute-start(bf16[6,32,128]{2,1,0:T(8,128)(2,1)S(1)} %fusion.7.refs_0_), channel_id=1, source_target_pairs={{0,2},{1,3},{2,0},{3,1},{4,6},{5,7},{6,4},{7,5},{8,10},{9,11},{10,... | collective-permute-start | bytes 147464 | tf_op jit(solution)/shard_map/ppermute | solution.py:320
  125.2 3.7 %collective-permute-start.21 = (bf16[6,32,128]{2,1,0:T(8,128)(2,1)S(1)}, bf16[6,32,128]{2,1,0:T(8,128)(2,1)S(1)}, u32[]{:S(2)}, u32[]{:S(2)}) collective-permute-start(bf16[6,32,128]{2,1,0:T(8,128)(2,1)S(1)} %fusion.7.refs_0_), channel_id=1, source_target_pairs={{0,3},{1,2},{2,1},{3,0},{4,7},{5,6},{6,5},{7,4},{8,11},{9,10},{10,... | collective-permute-start | bytes 147464 | tf_op jit(solution)/shard_map/ppermute | solution.py:320
  (9 other events, 12.5 us)

commit v5 on v4

--- a/solution.py
+++ b/solution.py
@@ -6,7 +6,7 @@
 from jax.sharding import PartitionSpec as P
 
 CAP = 2
-BATCH = 8
+BATCH = 6
 META = 16
 MEMBERS = 4
 FULL = 2
@@ -340,7 +340,7 @@
     listed = plan(meta.reshape(total, 3), slots, pairs, virt)
 
     full = lax.all_to_all(touch([jnp.transpose(full, (0, 2, 1, 3))], near)[0], "pair", 0, 0, tiled=True)
-    for d in (3,):
+    for d in (2,):
         pieces[d] = after(pieces[d], near)
 
     others = over_aux(blocks, 1)

time: 130 us -> 129 us (level)
    ppermute x11, waiting for transfers between devices: 42.8 us -> 40.4 us  [over_pair(): lax.ppermute(value, 'pair', [(i, i ^ distance) for i in range(pairs)])]
    all_to_all x1, waiting for transfers between devices: 1.72 us -> 3.99 us  [near_plan(): lax.all_to_all(touch([jnp.transpose(full, (0, 2, 1, 3))], near)[0], 'pair...]
    ppermute x11, starting transfers between devices: 18.8 us -> 16.9 us  [over_pair(): lax.ppermute(value, 'pair', [(i, i ^ distance) for i in range(pairs)])]
  transfers between devices with their start and end apart: 23 -> 23, of which waited for: 11 -> 11; matrix products, arithmetic and copies ran while one was open for 9% -> 9% of each run, Pallas kernels for 16% -> 15%
where the time goes in v5:
time: 129 us; the launch traced here: 128 us
  waiting for transfers between devices  58.8 us (46%)
  starting transfers between devices  29.4 us (23%)
  Pallas kernels  23.1 us (18%)
  local copies, waits for them, and re-layouts  15.6 us (12%)
    ppermute x11, waiting for transfers between devices, over_pair(): lax.ppermute(value, 'pair', [(i, i ^ distance) for i in range(pairs)])  40.4 us
    ppermute x11, starting transfers between devices, over_pair(): lax.ppermute(value, 'pair', [(i, i ^ distance) for i in range(pairs)])  16.9 us
    pallas_call x2, Pallas kernels, whole(): pl.pallas_call(lambda *refs: whole_kernel(owners, rows, virt, *refs), out...  11.1 us
    ppermute x4, waiting for transfers between devices, over_both(): return lax.ppermute(value, ('pair', 'aux'), route)  11 us
    unnamed x24, local copies, waits for them, and re-layouts  7.61 us
    ppermute x4, starting transfers between devices, over_both(): return lax.ppermute(value, ('pair', 'aux'), route)  4.96 us
    all_to_all x1, starting transfers between devices, near_plan(): lax.all_to_all(touch([jnp.transpose(full, (0, 2, 1, 3))], near)[0], 'pair...  4.88 us
    pallas_call x2, Pallas kernels, project(): pl.pallas_call(lambda *refs: project_kernel(owners, *refs), out_shape=jax...  4.42 us
  transfers between devices with their start and end apart: 23, of which 11 were waited for; matrix products, arithmetic and copies ran while one was open for 9% of the time, Pallas kernels for 15%

profile of v5, /device:TPU:0, one launch (start us, length us, event | category | flops | bytes accessed | tf_op | source)
XLA Modules:
  0.0 128.1 jit_solution(16260420321590906748)
XLA Ops:
  2.3 3.1 %collective-permute-start = (bf16[400,128]{1,0:T(8,128)(2,1)S(1)}, bf16[400,128]{1,0:T(8,128)(2,1)S(1)}, u32[]{:S(2)}, u32[]{:S(2)}) collective-permute-start(bf16[400,128]{1,0:T(8,128)(2,1)S(1)} %pack.1), channel_id=1, source_target_pairs={{0,8},{4,12},{8,0},{12,4},{16,24},{20,28},{24,16},{28,20},{1,9},{5... | collective-permute-start | bytes 307208 | tf_op jit(solution)/shard_map/ppermute | solution.py:317
  5.4 2.6 %collective-permute-start.1 = (bf16[400,128]{1,0:T(8,128)(2,1)S(1)}, bf16[400,128]{1,0:T(8,128)(2,1)S(1)}, u32[]{:S(2)}, u32[]{:S(2)}) collective-permute-start(bf16[400,128]{1,0:T(8,128)(2,1)S(1)} %pack.1), channel_id=1, source_target_pairs={{0,16},{4,20},{8,24},{12,28},{16,0},{20,4},{24,8},{28,12},{1,17},{... | collective-permute-start | bytes 307208 | tf_op jit(solution)/shard_map/ppermute | solution.py:317
  8.0 1.7 %constant_dynamic-slice_fusion = (bf16[1,256,8,128]{3,2,1,0:T(8,128)(2,1)S(1)}, bf16[1,256,8,128]{3,2,1,0:T(8,128)(2,1)S(1)}, bf16[1,256,8,128]{3,2,1,0:T(8,128)(2,1)S(1)}, bf16[1,256,8,128]{3,2,1,0:T(8,128)(2,1)S(1)}) fusion(bf16[1,2048,8,128]{3,2,1,0:T(8,128)(2,1)} %param.4, s32[]{:T(128)S(6)} %select_n.22, s32[]{:T(128)S(6)} %select_n.20, ...), kind=kLoop, calls=%fused_computation.31 | loop fusion | bytes 4194320 | tf_op jit(solution)/shard_map/dynamic_slice | solution.py:333
  10.6 1.7 %collective-permute-start.5 = (bf16[8,256,128]{2,1,0:T(8,128)(2,1)}, bf16[8,256,128]{2,1,0:T(8,128)(2,1)}, u32[]{:S(2)}, u32[]{:S(2)}) collective-permute-start(bf16[8,256,128]{2,1,0:T(8,128)(2,1)} %bitcast.66), channel_id=1, source_target_pairs={{0,4},{4,0},{8,12},{12,8},{16,20},{20,16},{24,28},{28,24},{1,5},{5... | collective-permute-start | bytes 1572872 | tf_op jit(solution)/shard_map/ppermute | solution.py:317
  15.4 2.0 %copy.41 = bf16[8,128,8,128]{3,1,2,0:T(8,128)(2,1)} copy(bf16[8,128,8,128]{3,2,1,0:T(8,128)(2,1)S(1)} %bitcast.72) | data formatting | bytes 4194304 | tf_op jit(solution)/shard_map/optimization_barrier | solution.py:331
  17.5 1.6 %collective-permute-start.3 = (bf16[4,400,128]{2,1,0:T(8,128)(2,1)S(1)}, bf16[4,400,128]{2,1,0:T(8,128)(2,1)S(1)}, u32[]{:S(2)}, u32[]{:S(2)}) collective-permute-start(bf16[4,400,128]{2,1,0:T(8,128)(2,1)S(1)} %pad_maximum_fusion.refs_1_), channel_id=1, source_target_pairs={{0,4},{4,0},{8,12},{12,8},{16,20},{20,16},{24,28},{28,24},{1,5},{5... | collective-permute-start | bytes 1228808 | tf_op jit(solution)/shard_map/ppermute | solution.py:317
  20.4 4.9 %all-to-all-start = ((bf16[8,8,128,128]{3,2,1,0:T(8,128)(2,1)}), bf16[8,8,128,128]{3,2,1,0:T(8,128)(2,1)}, u32[]{:S(2)}, u32[]{:S(2)}) async-start(bf16[8,8,128,128]{3,2,1,0:T(8,128)(2,1)} %touch.3), calls=%async_computation | async-start | bytes 4194304 | tf_op jit(solution)/shard_map/all_to_all | solution.py:342
  27.2 29.9 %collective-permute-done.3 = bf16[4,400,128]{2,1,0:T(8,128)(2,1)S(1)} collective-permute-done((bf16[4,400,128]{2,1,0:T(8,128)(2,1)S(1)}, bf16[4,400,128]{2,1,0:T(8,128)(2,1)S(1)}, u32[]{:S(2)}, u32[]{:S(2)}) %collective-permute-start.3) | collective-permute-done | bytes 409632 | tf_op jit(solution)/shard_map/ppermute | solution.py:317
  59.2 2.2 %plan.1.refs_3_.refs_1_.refs_0_ = s32[440]{0:T(512)} custom-call(s32[48,3]{1,0:T(8,128)} %reshape.45.refs_0_), custom_call_target="tpu_custom_call" | custom-call | flops 9999999827968 | tf_op jit(solution)/shard_map/plan/pallas_call | solution.py:80
  62.1 4.1 %contract.1 = (f32[8,64,256]{2,1,0:T(8,128)S(1)}, bf16[8,64,256]{2,1,0:T(8,128)(2,1)}, bf16[8,64,256]{2,1,0:T(8,128)(2,1)S(1)}, bf16[8,64,256]{2,1,0:T(8,128)(2,1)S(1)}, bf16[32,256,128]{2,1,0:T(8,128)(2,1)S(1)}) custom-call(s32[2]{0:T(128)S(1)} %copy-done.3, s32[440]{0:T(512)S(1)} %copy-done.1, ...), custom_call_target="tpu_custom_call" | custom-call | flops 9999999827968 | tf_op jit(solution)/shard_map/contract/pallas_call | solution.py:185
  68.9 4.0 %all-to-all-done = bf16[8,8,128,128]{3,2,1,0:T(8,128)(2,1)} async-done(((bf16[8,8,128,128]{3,2,1,0:T(8,128)(2,1)}), bf16[8,8,128,128]{3,2,1,0:T(8,128)(2,1)}, u32[]{:S(2)}, u32[]{:S(2)}) %all-to-all-start) | async-done | bytes 2097184 | tf_op jit(solution)/shard_map/all_to_all | solution.py:342
  76.4 5.5 %whole.2.refs_3_ = f32[49,64,128]{2,1,0:T(8,128)S(1)} custom-call(s32[440]{0:T(512)S(1)} %copy-done.1, bf16[8,400,128]{2,1,0:T(8,128)(2,1)} %constant_dynamic-update-slice_fusion.refs_2_.refs_1_, bf16[64,128,128]{2,1,0:T(8,128)(2,1)} %bitcast.17.refs_2_), custom_call_target="tpu_custom_call" | custom-call | tf_op jit(solution)/shard_map/whole/pallas_call | solution.py:215
  82.0 5.5 %whole.3.refs_4_ = f32[49,64,128]{2,1,0:T(8,128)S(1)} custom-call(s32[440]{0:T(512)S(1)} %copy-done.1, bf16[8,400,128]{2,1,0:T(8,128)(2,1)} %constant_dynamic-update-slice_fusion.refs_2_.refs_1_, bf16[64,128,128]{2,1,0:T(8,128)(2,1)} %collective-permute-done.11.refs_2_, f32[49,64,128]{2,1,0:T(8,128)S(1)} %whole.2.refs_3_), custom_call_target="tpu_custom_call" | custom-call | tf_op jit(solution)/shard_map/whole/pallas_call | solution.py:215
  87.5 6.9 %collective-permute-done.10.refs_3_ = bf16[8,64,256]{2,1,0:T(8,128)(2,1)} collective-permute-done((bf16[8,64,256]{2,1,0:T(8,128)(2,1)}, bf16[8,64,256]{2,1,0:T(8,128)(2,1)}, u32[]{:S(2)}, u32[]{:S(2)}) %collective-permute-start.10) | collective-permute-done | bytes 262176 | tf_op jit(solution)/shard_map/ppermute | solution.py:317
  94.4 2.4 %project.2.refs_4_ = f32[49,64,128]{2,1,0:T(8,128)S(1)} custom-call(s32[2]{0:T(128)S(1)} %copy-done.3, s32[440]{0:T(512)S(1)} %copy-done.1, f32[8,64,256]{2,1,0:T(8,128)S(1)} %get-tuple-element.26.refs_2_, bf16[8,64,256]{2,1,0:T(8,128)(2,1)} %collective-permute-done.10.refs_3_, f32[49,64,128]{2,1,0:T(8,128)S(1)} %whole.3.refs_4_, ...), custom_call_target="tpu_custom_call" | custom-call | tf_op jit(solution)/shard_map/project/pallas_call | solution.py:246
  96.8 2.5 %collective-permute-done.9.refs_3_ = bf16[8,64,256]{2,1,0:T(8,128)(2,1)} collective-permute-done((bf16[8,64,256]{2,1,0:T(8,128)(2,1)}, bf16[8,64,256]{2,1,0:T(8,128)(2,1)}, u32[]{:S(2)}, u32[]{:S(2)}) %collective-permute-start.9) | collective-permute-done | bytes 262176 | tf_op jit(solution)/shard_map/ppermute | solution.py:328
  99.3 2.0 %project.3 = f32[49,64,128]{2,1,0:T(8,128)S(1)} custom-call(s32[2]{0:T(128)S(1)} %copy-done.3, s32[440]{0:T(512)S(1)} %copy-done.1, bf16[8,64,256]{2,1,0:T(8,128)(2,1)S(1)} %collective-permute-done.8.refs_2_, bf16[8,64,256]{2,1,0:T(8,128)(2,1)} %collective-permute-done.9.refs_3_, f32[49,64,128]{2,1,0:T(8,128)S(1)} %project.2.refs_4_, ...), custom_call_target="tpu_custom_call" | custom-call | tf_op jit(solution)/shard_map/project/pallas_call | solution.py:246
  103.3 2.0 %collective-permute-start.13 = (bf16[4,6,32,128]{3,2,1,0:T(8,128)(2,1)S(1)}, bf16[4,6,32,128]{3,2,1,0:T(8,128)(2,1)S(1)}, u32[]{:S(2)}, u32[]{:S(2)}) collective-permute-start(bf16[4,6,32,128]{3,2,1,0:T(8,128)(2,1)S(1)} %fusion.4), channel_id=1, source_target_pairs={{0,4},{1,5},{2,6},{3,7},{4,0},{5,1},{6,2},{7,3},{8,12},{9,13},{10,... | collective-permute-start | bytes 589832 | tf_op jit(solution)/shard_map/ppermute | solution.py:328
  105.3 5.1 %collective-permute-done.15 = bf16[4,6,32,128]{3,2,1,0:T(8,128)(2,1)S(1)} collective-permute-done((bf16[4,6,32,128]{3,2,1,0:T(8,128)(2,1)S(1)}, bf16[4,6,32,128]{3,2,1,0:T(8,128)(2,1)S(1)}, u32[]{:S(2)}, u32[]{:S(2)}) %collective-permute-start.15) | collective-permute-done | bytes 196640 | tf_op jit(solution)/shard_map/ppermute | solution.py:328
  110.4 2.3 %collective-permute-done.14 = bf16[4,6,32,128]{3,2,1,0:T(8,128)(2,1)S(1)} collective-permute-done((bf16[4,6,32,128]{3,2,1,0:T(8,128)(2,1)S(1)}, bf16[4,6,32,128]{3,2,1,0:T(8,128)(2,1)S(1)}, u32[]{:S(2)}, u32[]{:S(2)}) %collective-permute-start.14) | collective-permute-done | bytes 196640 | tf_op jit(solution)/shard_map/ppermute | solution.py:328
  113.9 3.1 %collective-permute-start.18 = (bf16[6,32,128]{2,1,0:T(8,128)(2,1)S(1)}, bf16[6,32,128]{2,1,0:T(8,128)(2,1)S(1)}, u32[]{:S(2)}, u32[]{:S(2)}) collective-permute-start(bf16[6,32,128]{2,1,0:T(8,128)(2,1)S(1)} %get-tuple-element.38), channel_id=1, source_target_pairs={{0,24},{4,28},{8,16},{12,20},{16,8},{20,12},{24,0},{28,4},{1,25},{... | collective-permute-start | bytes 147464 | tf_op jit(solution)/shard_map/ppermute | solution.py:317
  118.3 1.7 %collective-permute-done.18 = bf16[6,32,128]{2,1,0:T(8,128)(2,1)S(1)} collective-permute-done((bf16[6,32,128]{2,1,0:T(8,128)(2,1)S(1)}, bf16[6,32,128]{2,1,0:T(8,128)(2,1)S(1)}, u32[]{:S(2)}, u32[]{:S(2)}) %collective-permute-start.18) | collective-permute-done | bytes 49184 | tf_op jit(solution)/shard_map/ppermute | solution.py:317
  120.1 2.0 %collective-permute-done.17 = bf16[6,32,128]{2,1,0:T(8,128)(2,1)S(1)} collective-permute-done((bf16[6,32,128]{2,1,0:T(8,128)(2,1)S(1)}, bf16[6,32,128]{2,1,0:T(8,128)(2,1)S(1)}, u32[]{:S(2)}, u32[]{:S(2)}) %collective-permute-start.17) | collective-permute-done | bytes 49184 | tf_op jit(solution)/shard_map/ppermute | solution.py:317
  124.0 2.3 %collective-permute-done.20.refs_2_ = bf16[6,32,128]{2,1,0:T(8,128)(2,1)S(1)} collective-permute-done((bf16[6,32,128]{2,1,0:T(8,128)(2,1)S(1)}, bf16[6,32,128]{2,1,0:T(8,128)(2,1)S(1)}, u32[]{:S(2)}, u32[]{:S(2)}) %collective-permute-start.20) | collective-permute-done | bytes 49184 | tf_op jit(solution)/shard_map/ppermute | solution.py:320
  (76 shorter events, 26.9 us)
Async XLA Ops:
  2.3 15.0 %collective-permute-start = (bf16[400,128]{1,0:T(8,128)(2,1)S(1)}, bf16[400,128]{1,0:T(8,128)(2,1)S(1)}, u32[]{:S(2)}, u32[]{:S(2)}) collective-permute-start(bf16[400,128]{1,0:T(8,128)(2,1)S(1)} %pack.1), channel_id=1, source_target_pairs={{0,8},{4,12},{8,0},{12,4},{16,24},{20,28},{24,16},{28,20},{1,9},{5... | collective-permute-start | bytes 307208 | tf_op jit(solution)/shard_map/ppermute | solution.py:317
  5.4 11.9 %collective-permute-start.1 = (bf16[400,128]{1,0:T(8,128)(2,1)S(1)}, bf16[400,128]{1,0:T(8,128)(2,1)S(1)}, u32[]{:S(2)}, u32[]{:S(2)}) collective-permute-start(bf16[400,128]{1,0:T(8,128)(2,1)S(1)} %pack.1), channel_id=1, source_target_pairs={{0,16},{4,20},{8,24},{12,28},{16,0},{20,4},{24,8},{28,12},{1,17},{... | collective-permute-start | bytes 307208 | tf_op jit(solution)/shard_map/ppermute | solution.py:317
  8.0 9.4 %collective-permute-start.2 = (bf16[400,128]{1,0:T(8,128)(2,1)S(1)}, bf16[400,128]{1,0:T(8,128)(2,1)S(1)}, u32[]{:S(2)}, u32[]{:S(2)}) collective-permute-start(bf16[400,128]{1,0:T(8,128)(2,1)S(1)} %pack.1), channel_id=1, source_target_pairs={{0,24},{4,28},{8,16},{12,20},{16,8},{20,12},{24,0},{28,4},{1,25},{... | collective-permute-start | bytes 307208 | tf_op jit(solution)/shard_map/ppermute | solution.py:317
  9.7 5.7 %slice-start = ((bf16[1,2048,8,128]{3,2,1,0:T(8,128)(2,1)}), bf16[1,1024,8,128]{3,2,1,0:T(8,128)(2,1)S(1)}, s32[]{:S(2)}) async-start(bf16[1,2048,8,128]{3,2,1,0:T(8,128)(2,1)} %param.4), calls=%async_computation.1 | async-start | bytes 4194304 | tf_op jit(solution)/shard_map/slice | solution.py:330
  10.6 50.9 %collective-permute-start.5 = (bf16[8,256,128]{2,1,0:T(8,128)(2,1)}, bf16[8,256,128]{2,1,0:T(8,128)(2,1)}, u32[]{:S(2)}, u32[]{:S(2)}) collective-permute-start(bf16[8,256,128]{2,1,0:T(8,128)(2,1)} %bitcast.66), channel_id=1, source_target_pairs={{0,4},{4,0},{8,12},{12,8},{16,20},{20,16},{24,28},{28,24},{1,5},{5... | collective-permute-start | bytes 1572872 | tf_op jit(solution)/shard_map/ppermute | solution.py:317
  13.2 48.3 %collective-permute-start.7 = (bf16[8,256,128]{2,1,0:T(8,128)(2,1)}, bf16[8,256,128]{2,1,0:T(8,128)(2,1)}, u32[]{:S(2)}, u32[]{:S(2)}) collective-permute-start(bf16[8,256,128]{2,1,0:T(8,128)(2,1)} %bitcast.64), channel_id=1, source_target_pairs={{0,12},{4,8},{8,4},{12,0},{16,28},{20,24},{24,20},{28,16},{1,13},{... | collective-permute-start | bytes 1572872 | tf_op jit(solution)/shard_map/ppermute | solution.py:317
  17.5 39.6 %collective-permute-start.3 = (bf16[4,400,128]{2,1,0:T(8,128)(2,1)S(1)}, bf16[4,400,128]{2,1,0:T(8,128)(2,1)S(1)}, u32[]{:S(2)}, u32[]{:S(2)}) collective-permute-start(bf16[4,400,128]{2,1,0:T(8,128)(2,1)S(1)} %pad_maximum_fusion.refs_1_), channel_id=1, source_target_pairs={{0,4},{4,0},{8,12},{12,8},{16,20},{20,16},{24,28},{28,24},{1,5},{5... | collective-permute-start | bytes 1228808 | tf_op jit(solution)/shard_map/ppermute | solution.py:317
  19.1 42.4 %collective-permute-start.6 = (bf16[8,256,128]{2,1,0:T(8,128)(2,1)}, bf16[8,256,128]{2,1,0:T(8,128)(2,1)}, u32[]{:S(2)}, u32[]{:S(2)}) collective-permute-start(bf16[8,256,128]{2,1,0:T(8,128)(2,1)} %bitcast.65), channel_id=1, source_target_pairs={{0,8},{4,12},{8,0},{12,4},{16,24},{20,28},{24,16},{28,20},{1,9},{5... | collective-permute-start | bytes 1572872 | tf_op jit(solution)/shard_map/ppermute | solution.py:317
  20.4 52.5 %all-to-all-start = ((bf16[8,8,128,128]{3,2,1,0:T(8,128)(2,1)}), bf16[8,8,128,128]{3,2,1,0:T(8,128)(2,1)}, u32[]{:S(2)}, u32[]{:S(2)}) async-start(bf16[8,8,128,128]{3,2,1,0:T(8,128)(2,1)} %touch.3), calls=%async_computation | async-start | bytes 4194304 | tf_op jit(solution)/shard_map/all_to_all | solution.py:342
  58.6 2.9 %collective-permute-start.4 = (bf16[8,400,128]{2,1,0:T(8,128)(2,1)}, bf16[8,400,128]{2,1,0:T(8,128)(2,1)}, u32[]{:S(2)}, u32[]{:S(2)}) collective-permute-start(bf16[8,400,128]{2,1,0:T(8,128)(2,1)} %constant_dynamic-update-slice_fusion.refs_2_.refs_1_), channel_id=1, source_target_pairs={{0,1},{1,0},{2,3},{3,2},{4,5},{5,4},{6,7},{7,6},{8,9},{9,8},{10,11... | collective-permute-start | bytes 2457608 | tf_op jit(solution)/shard_map/ppermute | solution.py:320
  72.9 9.1 %collective-permute-start.11 = (bf16[64,128,128]{2,1,0:T(8,128)(2,1)}, bf16[64,128,128]{2,1,0:T(8,128)(2,1)}, u32[]{:S(2)}, u32[]{:S(2)}) collective-permute-start(bf16[64,128,128]{2,1,0:T(8,128)(2,1)} %bitcast.17.refs_2_), channel_id=1, source_target_pairs={{0,1},{1,0},{2,3},{3,2},{4,5},{5,4},{6,7},{7,6},{8,9},{9,8},{10,11... | collective-permute-start | bytes 6291464 | tf_op jit(solution)/shard_map/ppermute | solution.py:320
  72.9 26.4 %collective-permute-start.12 = (bf16[32,256,128]{2,1,0:T(8,128)(2,1)}, bf16[32,256,128]{2,1,0:T(8,128)(2,1)S(1)}, u32[]{:S(2)}, u32[]{:S(2)}) collective-permute-start(bf16[32,256,128]{2,1,0:T(8,128)(2,1)} %copy-done.5), channel_id=1, source_target_pairs={{0,1},{1,0},{2,3},{3,2},{4,5},{5,4},{6,7},{7,6},{8,9},{9,8},{10,11... | collective-permute-start | bytes 6291464 | tf_op jit(solution)/shard_map/ppermute | solution.py:320
  73.4 21.0 %collective-permute-start.10 = (bf16[8,64,256]{2,1,0:T(8,128)(2,1)}, bf16[8,64,256]{2,1,0:T(8,128)(2,1)}, u32[]{:S(2)}, u32[]{:S(2)}) collective-permute-start(bf16[8,64,256]{2,1,0:T(8,128)(2,1)} %get-tuple-element.27), channel_id=1, source_target_pairs={{0,16},{4,20},{8,24},{12,28},{16,0},{20,4},{24,8},{28,12},{1,17},{... | collective-permute-start | bytes 786440 | tf_op jit(solution)/shard_map/ppermute | solution.py:317
  74.8 22.0 %collective-permute-start.8 = (bf16[8,64,256]{2,1,0:T(8,128)(2,1)}, bf16[8,64,256]{2,1,0:T(8,128)(2,1)S(1)}, u32[]{:S(2)}, u32[]{:S(2)}) collective-permute-start(bf16[8,64,256]{2,1,0:T(8,128)(2,1)} %copy-done.7), channel_id=1, source_target_pairs={{0,1},{1,0},{2,3},{3,2},{4,5},{5,4},{6,7},{7,6},{8,9},{9,8},{10,11... | collective-permute-start | bytes 786440 | tf_op jit(solution)/shard_map/ppermute | solution.py:320
  75.1 24.2 %collective-permute-start.9 = (bf16[8,64,256]{2,1,0:T(8,128)(2,1)}, bf16[8,64,256]{2,1,0:T(8,128)(2,1)}, u32[]{:S(2)}, u32[]{:S(2)}) collective-permute-start(bf16[8,64,256]{2,1,0:T(8,128)(2,1)} %copy-done.6), channel_id=1, source_target_pairs={{0,17},{1,16},{2,19},{3,18},{4,21},{5,20},{6,23},{7,22},{8,25},{9,... | collective-permute-start | bytes 786440 | tf_op jit(solution)/shard_map/ppermute | solution.py:328
  101.6 8.8 %collective-permute-start.15 = (bf16[4,6,32,128]{3,2,1,0:T(8,128)(2,1)S(1)}, bf16[4,6,32,128]{3,2,1,0:T(8,128)(2,1)S(1)}, u32[]{:S(2)}, u32[]{:S(2)}) collective-permute-start(bf16[4,6,32,128]{3,2,1,0:T(8,128)(2,1)S(1)} %get-tuple-element.36), channel_id=1, source_target_pairs={{0,6},{1,7},{2,4},{3,5},{4,2},{5,3},{6,0},{7,1},{8,14},{9,15},{10,... | collective-permute-start | bytes 589832 | tf_op jit(solution)/shard_map/ppermute | solution.py:328
  101.8 10.8 %collective-permute-start.14 = (bf16[4,6,32,128]{3,2,1,0:T(8,128)(2,1)S(1)}, bf16[4,6,32,128]{3,2,1,0:T(8,128)(2,1)S(1)}, u32[]{:S(2)}, u32[]{:S(2)}) collective-permute-start(bf16[4,6,32,128]{3,2,1,0:T(8,128)(2,1)S(1)} %get-tuple-element.35), channel_id=1, source_target_pairs={{0,2},{1,3},{2,0},{3,1},{4,6},{5,7},{6,4},{7,5},{8,10},{9,11},{10,... | collective-permute-start | bytes 589832 | tf_op jit(solution)/shard_map/ppermute | solution.py:328
  103.3 10.5 %collective-permute-start.13 = (bf16[4,6,32,128]{3,2,1,0:T(8,128)(2,1)S(1)}, bf16[4,6,32,128]{3,2,1,0:T(8,128)(2,1)S(1)}, u32[]{:S(2)}, u32[]{:S(2)}) collective-permute-start(bf16[4,6,32,128]{3,2,1,0:T(8,128)(2,1)S(1)} %fusion.4), channel_id=1, source_target_pairs={{0,4},{1,5},{2,6},{3,7},{4,0},{5,1},{6,2},{7,3},{8,12},{9,13},{10,... | collective-permute-start | bytes 589832 | tf_op jit(solution)/shard_map/ppermute | solution.py:328
  113.9 6.2 %collective-permute-start.18 = (bf16[6,32,128]{2,1,0:T(8,128)(2,1)S(1)}, bf16[6,32,128]{2,1,0:T(8,128)(2,1)S(1)}, u32[]{:S(2)}, u32[]{:S(2)}) collective-permute-start(bf16[6,32,128]{2,1,0:T(8,128)(2,1)S(1)} %get-tuple-element.38), channel_id=1, source_target_pairs={{0,24},{4,28},{8,16},{12,20},{16,8},{20,12},{24,0},{28,4},{1,25},{... | collective-permute-start | bytes 147464 | tf_op jit(solution)/shard_map/ppermute | solution.py:317
  117.0 5.0 %collective-permute-start.17 = (bf16[6,32,128]{2,1,0:T(8,128)(2,1)S(1)}, bf16[6,32,128]{2,1,0:T(8,128)(2,1)S(1)}, u32[]{:S(2)}, u32[]{:S(2)}) collective-permute-start(bf16[6,32,128]{2,1,0:T(8,128)(2,1)S(1)} %get-tuple-element.39), channel_id=1, source_target_pairs={{0,16},{4,20},{8,24},{12,28},{16,0},{20,4},{24,8},{28,12},{1,17},{... | collective-permute-start | bytes 147464 | tf_op jit(solution)/shard_map/ppermute | solution.py:317
  117.0 5.0 %collective-permute-start.16 = (bf16[6,32,128]{2,1,0:T(8,128)(2,1)S(1)}, bf16[6,32,128]{2,1,0:T(8,128)(2,1)S(1)}, u32[]{:S(2)}, u32[]{:S(2)}) collective-permute-start(bf16[6,32,128]{2,1,0:T(8,128)(2,1)S(1)} %get-tuple-element.37), channel_id=1, source_target_pairs={{0,8},{4,12},{8,0},{12,4},{16,24},{20,28},{24,16},{28,20},{1,9},{5... | collective-permute-start | bytes 147464 | tf_op jit(solution)/shard_map/ppermute | solution.py:317
  122.1 1.9 %collective-permute-start.19 = (bf16[6,32,128]{2,1,0:T(8,128)(2,1)S(1)}, bf16[6,32,128]{2,1,0:T(8,128)(2,1)S(1)}, u32[]{:S(2)}, u32[]{:S(2)}) collective-permute-start(bf16[6,32,128]{2,1,0:T(8,128)(2,1)S(1)} %fusion.7.refs_0_), channel_id=1, source_target_pairs={{0,1},{1,0},{2,3},{3,2},{4,5},{5,4},{6,7},{7,6},{8,9},{9,8},{10,11... | collective-permute-start | bytes 147464 | tf_op jit(solution)/shard_map/ppermute | solution.py:320
  122.2 4.2 %collective-permute-start.20 = (bf16[6,32,128]{2,1,0:T(8,128)(2,1)S(1)}, bf16[6,32,128]{2,1,0:T(8,128)(2,1)S(1)}, u32[]{:S(2)}, u32[]{:S(2)}) collective-permute-start(bf16[6,32,128]{2,1,0:T(8,128)(2,1)S(1)} %fusion.7.refs_0_), channel_id=1, source_target_pairs={{0,2},{1,3},{2,0},{3,1},{4,6},{5,7},{6,4},{7,5},{8,10},{9,11},{10,... | collective-permute-start | bytes 147464 | tf_op jit(solution)/shard_map/ppermute | solution.py:320
  123.7 3.7 %collective-permute-start.21 = (bf16[6,32,128]{2,1,0:T(8,128)(2,1)S(1)}, bf16[6,32,128]{2,1,0:T(8,128)(2,1)S(1)}, u32[]{:S(2)}, u32[]{:S(2)}) collective-permute-start(bf16[6,32,128]{2,1,0:T(8,128)(2,1)S(1)} %fusion.7.refs_0_), channel_id=1, source_target_pairs={{0,3},{1,2},{2,1},{3,0},{4,7},{5,6},{6,5},{7,4},{8,11},{9,10},{10,... | collective-permute-start | bytes 147464 | tf_op jit(solution)/shard_map/ppermute | solution.py:320
  (9 other events, 12.6 us)

commit v6 on v5

--- a/solution.py
+++ b/solution.py
@@ -340,7 +340,7 @@
     listed = plan(meta.reshape(total, 3), slots, pairs, virt)
 
     full = lax.all_to_all(touch([jnp.transpose(full, (0, 2, 1, 3))], near)[0], "pair", 0, 0, tiled=True)
-    for d in (2,):
+    for d in (1, 2):
         pieces[d] = after(pieces[d], near)
 
     others = over_aux(blocks, 1)

time: 129 us -> 128 us (level)
    ppermute x11, waiting for transfers between devices: 40.4 us -> 38.4 us  [over_pair(): lax.ppermute(value, 'pair', [(i, i ^ distance) for i in range(pairs)])]
    all_to_all x1, waiting for transfers between devices: 3.99 us -> 5.99 us  [near_plan(): lax.all_to_all(touch([jnp.transpose(full, (0, 2, 1, 3))], near)[0], 'pair...]
    dynamic_slice x5 -> x3, local copies, waits for them, and re-layouts: 4.35 us -> 2.61 us  [near_plan(): lax.dynamic_slice_in_dim(factors, start, chunk, 0)]
    ppermute x4, starting transfers between devices: 4.96 us -> 6.58 us  [over_both(): return lax.ppermute(value, ('pair', 'aux'), route)]
  transfers between devices with their start and end apart: 23 -> 23, of which waited for: 11 -> 13; matrix products, arithmetic and copies ran while one was open for 9% -> 8% of each run, Pallas kernels for 15% -> 16%
where the time goes in v6:
time: 128 us; the launch traced here: 127 us
  waiting for transfers between devices  59 us (46%)
  starting transfers between devices  29.4 us (23%)
  Pallas kernels  23.1 us (18%)
  local copies, waits for them, and re-layouts  14.4 us (11%)
    ppermute x11, waiting for transfers between devices, over_pair(): lax.ppermute(value, 'pair', [(i, i ^ distance) for i in range(pairs)])  38.4 us
    ppermute x11, starting transfers between devices, over_pair(): lax.ppermute(value, 'pair', [(i, i ^ distance) for i in range(pairs)])  15.7 us
    ppermute x4, waiting for transfers between devices, over_both(): return lax.ppermute(value, ('pair', 'aux'), route)  11.2 us
    pallas_call x2, Pallas kernels, whole(): pl.pallas_call(lambda *refs: whole_kernel(owners, rows, virt, *refs), out...  11.1 us
    unnamed x24, local copies, waits for them, and re-layouts  7.03 us
    ppermute x4, starting transfers between devices, over_both(): return lax.ppermute(value, ('pair', 'aux'), route)  6.58 us
    all_to_all x1, waiting for transfers between devices, near_plan(): lax.all_to_all(touch([jnp.transpose(full, (0, 2, 1, 3))], near)[0], 'pair...  5.99 us
    all_to_all x1, starting transfers between devices, near_plan(): lax.all_to_all(touch([jnp.transpose(full, (0, 2, 1, 3))], near)[0], 'pair...  4.67 us
  transfers between devices with their start and end apart: 23, of which 13 were waited for; matrix products, arithmetic and copies ran while one was open for 8% of the time, Pallas kernels for 16%

profile of v6, /device:TPU:0, one launch (start us, length us, event | category | flops | bytes accessed | tf_op | source)
XLA Modules:
  0.0 127.1 jit_solution(8831566364225421056)
XLA Ops:
  2.3 3.1 %collective-permute-start = (bf16[400,128]{1,0:T(8,128)(2,1)S(1)}, bf16[400,128]{1,0:T(8,128)(2,1)S(1)}, u32[]{:S(2)}, u32[]{:S(2)}) collective-permute-start(bf16[400,128]{1,0:T(8,128)(2,1)S(1)} %pack.1), channel_id=1, source_target_pairs={{0,8},{4,12},{8,0},{12,4},{16,24},{20,28},{24,16},{28,20},{1,9},{5... | collective-permute-start | bytes 307208 | tf_op jit(solution)/shard_map/ppermute | solution.py:317
  5.4 2.6 %collective-permute-start.1 = (bf16[400,128]{1,0:T(8,128)(2,1)S(1)}, bf16[400,128]{1,0:T(8,128)(2,1)S(1)}, u32[]{:S(2)}, u32[]{:S(2)}) collective-permute-start(bf16[400,128]{1,0:T(8,128)(2,1)S(1)} %pack.1), channel_id=1, source_target_pairs={{0,16},{4,20},{8,24},{12,28},{16,0},{20,4},{24,8},{28,12},{1,17},{... | collective-permute-start | bytes 307208 | tf_op jit(solution)/shard_map/ppermute | solution.py:317
  10.6 1.9 %collective-permute-start.7 = (bf16[8,256,128]{2,1,0:T(8,128)(2,1)}, bf16[8,256,128]{2,1,0:T(8,128)(2,1)}, u32[]{:S(2)}, u32[]{:S(2)}) collective-permute-start(bf16[8,256,128]{2,1,0:T(8,128)(2,1)} %bitcast.64), channel_id=1, source_target_pairs={{0,12},{4,8},{8,4},{12,0},{16,28},{20,24},{24,20},{28,16},{1,13},{... | collective-permute-start | bytes 1572872 | tf_op jit(solution)/shard_map/ppermute | solution.py:317
  14.3 2.0 %copy.41 = bf16[8,128,8,128]{3,1,2,0:T(8,128)(2,1)} copy(bf16[8,128,8,128]{3,2,1,0:T(8,128)(2,1)S(1)} %bitcast.70) | data formatting | bytes 4194304 | tf_op jit(solution)/shard_map/optimization_barrier | solution.py:331
  20.0 4.7 %all-to-all-start = ((bf16[8,8,128,128]{3,2,1,0:T(8,128)(2,1)}), bf16[8,8,128,128]{3,2,1,0:T(8,128)(2,1)}, u32[]{:S(2)}, u32[]{:S(2)}) async-start(bf16[8,8,128,128]{3,2,1,0:T(8,128)(2,1)} %touch.3), calls=%async_computation | async-start | bytes 4194304 | tf_op jit(solution)/shard_map/all_to_all | solution.py:342
  26.6 15.1 %collective-permute-done.3 = bf16[4,400,128]{2,1,0:T(8,128)(2,1)S(1)} collective-permute-done((bf16[4,400,128]{2,1,0:T(8,128)(2,1)S(1)}, bf16[4,400,128]{2,1,0:T(8,128)(2,1)S(1)}, u32[]{:S(2)}, u32[]{:S(2)}) %collective-permute-start.3) | collective-permute-done | bytes 409632 | tf_op jit(solution)/shard_map/ppermute | solution.py:317
  43.9 2.2 %plan.1.refs_3_.refs_1_.refs_0_ = s32[440]{0:T(512)} custom-call(s32[48,3]{1,0:T(8,128)} %reshape.45.refs_0_), custom_call_target="tpu_custom_call" | custom-call | flops 9999999827968 | tf_op jit(solution)/shard_map/plan/pallas_call | solution.py:80
  46.1 11.3 %collective-permute-done.5.refs_0_ = bf16[8,256,128]{2,1,0:T(8,128)(2,1)} collective-permute-done((bf16[8,256,128]{2,1,0:T(8,128)(2,1)}, bf16[8,256,128]{2,1,0:T(8,128)(2,1)}, u32[]{:S(2)}, u32[]{:S(2)}) %collective-permute-start.5) | collective-permute-done | bytes 524320 | tf_op jit(solution)/shard_map/ppermute | solution.py:317
  57.4 2.1 %collective-permute-done.6.refs_1_ = bf16[8,256,128]{2,1,0:T(8,128)(2,1)} collective-permute-done((bf16[8,256,128]{2,1,0:T(8,128)(2,1)}, bf16[8,256,128]{2,1,0:T(8,128)(2,1)}, u32[]{:S(2)}, u32[]{:S(2)}) %collective-permute-start.6) | collective-permute-done | bytes 524320 | tf_op jit(solution)/shard_map/ppermute | solution.py:317
  59.5 4.1 %contract.1 = (f32[8,64,256]{2,1,0:T(8,128)S(1)}, bf16[8,64,256]{2,1,0:T(8,128)(2,1)}, bf16[8,64,256]{2,1,0:T(8,128)(2,1)S(1)}, bf16[8,64,256]{2,1,0:T(8,128)(2,1)S(1)}, bf16[32,256,128]{2,1,0:T(8,128)(2,1)S(1)}) custom-call(s32[2]{0:T(128)S(1)} %copy-done.3, s32[440]{0:T(512)S(1)} %copy-done.1, ...), custom_call_target="tpu_custom_call" | custom-call | flops 9999999827968 | tf_op jit(solution)/shard_map/contract/pallas_call | solution.py:185
  66.3 6.0 %all-to-all-done = bf16[8,8,128,128]{3,2,1,0:T(8,128)(2,1)} async-done(((bf16[8,8,128,128]{3,2,1,0:T(8,128)(2,1)}), bf16[8,8,128,128]{3,2,1,0:T(8,128)(2,1)}, u32[]{:S(2)}, u32[]{:S(2)}) %all-to-all-start) | async-done | bytes 2097184 | tf_op jit(solution)/shard_map/all_to_all | solution.py:342
  72.9 3.0 %collective-permute-start.9 = (bf16[8,64,256]{2,1,0:T(8,128)(2,1)}, bf16[8,64,256]{2,1,0:T(8,128)(2,1)}, u32[]{:S(2)}, u32[]{:S(2)}) collective-permute-start(bf16[8,64,256]{2,1,0:T(8,128)(2,1)} %copy-done.6), channel_id=1, source_target_pairs={{0,17},{1,16},{2,19},{3,18},{4,21},{5,20},{6,23},{7,22},{8,25},{9,... | collective-permute-start | bytes 786440 | tf_op jit(solution)/shard_map/ppermute | solution.py:328
  75.9 5.5 %whole.2.refs_3_ = f32[49,64,128]{2,1,0:T(8,128)S(1)} custom-call(s32[440]{0:T(512)S(1)} %copy-done.1, bf16[8,400,128]{2,1,0:T(8,128)(2,1)} %constant_dynamic-update-slice_fusion.refs_2_.refs_1_, bf16[64,128,128]{2,1,0:T(8,128)(2,1)} %bitcast.17.refs_2_), custom_call_target="tpu_custom_call" | custom-call | tf_op jit(solution)/shard_map/whole/pallas_call | solution.py:215
  81.4 5.5 %whole.3.refs_4_ = f32[49,64,128]{2,1,0:T(8,128)S(1)} custom-call(s32[440]{0:T(512)S(1)} %copy-done.1, bf16[8,400,128]{2,1,0:T(8,128)(2,1)} %constant_dynamic-update-slice_fusion.refs_2_.refs_1_, bf16[64,128,128]{2,1,0:T(8,128)(2,1)} %collective-permute-done.11.refs_2_, f32[49,64,128]{2,1,0:T(8,128)S(1)} %whole.2.refs_3_), custom_call_target="tpu_custom_call" | custom-call | tf_op jit(solution)/shard_map/whole/pallas_call | solution.py:215
  87.0 6.8 %collective-permute-done.10.refs_3_ = bf16[8,64,256]{2,1,0:T(8,128)(2,1)} collective-permute-done((bf16[8,64,256]{2,1,0:T(8,128)(2,1)}, bf16[8,64,256]{2,1,0:T(8,128)(2,1)}, u32[]{:S(2)}, u32[]{:S(2)}) %collective-permute-start.10) | collective-permute-done | bytes 262176 | tf_op jit(solution)/shard_map/ppermute | solution.py:317
  93.7 2.4 %project.2.refs_4_ = f32[49,64,128]{2,1,0:T(8,128)S(1)} custom-call(s32[2]{0:T(128)S(1)} %copy-done.3, s32[440]{0:T(512)S(1)} %copy-done.1, f32[8,64,256]{2,1,0:T(8,128)S(1)} %get-tuple-element.28.refs_2_, bf16[8,64,256]{2,1,0:T(8,128)(2,1)} %collective-permute-done.10.refs_3_, f32[49,64,128]{2,1,0:T(8,128)S(1)} %whole.3.refs_4_, ...), custom_call_target="tpu_custom_call" | custom-call | tf_op jit(solution)/shard_map/project/pallas_call | solution.py:246
  96.2 2.7 %collective-permute-done.9.refs_3_ = bf16[8,64,256]{2,1,0:T(8,128)(2,1)} collective-permute-done((bf16[8,64,256]{2,1,0:T(8,128)(2,1)}, bf16[8,64,256]{2,1,0:T(8,128)(2,1)}, u32[]{:S(2)}, u32[]{:S(2)}) %collective-permute-start.9) | collective-permute-done | bytes 262176 | tf_op jit(solution)/shard_map/ppermute | solution.py:328
  98.9 2.0 %project.3 = f32[49,64,128]{2,1,0:T(8,128)S(1)} custom-call(s32[2]{0:T(128)S(1)} %copy-done.3, s32[440]{0:T(512)S(1)} %copy-done.1, bf16[8,64,256]{2,1,0:T(8,128)(2,1)S(1)} %collective-permute-done.8.refs_2_, bf16[8,64,256]{2,1,0:T(8,128)(2,1)} %collective-permute-done.9.refs_3_, f32[49,64,128]{2,1,0:T(8,128)S(1)} %project.2.refs_4_, ...), custom_call_target="tpu_custom_call" | custom-call | tf_op jit(solution)/shard_map/project/pallas_call | solution.py:246
  102.9 2.0 %collective-permute-start.13 = (bf16[4,6,32,128]{3,2,1,0:T(8,128)(2,1)S(1)}, bf16[4,6,32,128]{3,2,1,0:T(8,128)(2,1)S(1)}, u32[]{:S(2)}, u32[]{:S(2)}) collective-permute-start(bf16[4,6,32,128]{3,2,1,0:T(8,128)(2,1)S(1)} %fusion.4), channel_id=1, source_target_pairs={{0,4},{1,5},{2,6},{3,7},{4,0},{5,1},{6,2},{7,3},{8,12},{9,13},{10,... | collective-permute-start | bytes 589832 | tf_op jit(solution)/shard_map/ppermute | solution.py:328
  104.9 5.1 %collective-permute-done.15 = bf16[4,6,32,128]{3,2,1,0:T(8,128)(2,1)S(1)} collective-permute-done((bf16[4,6,32,128]{3,2,1,0:T(8,128)(2,1)S(1)}, bf16[4,6,32,128]{3,2,1,0:T(8,128)(2,1)S(1)}, u32[]{:S(2)}, u32[]{:S(2)}) %collective-permute-start.15) | collective-permute-done | bytes 196640 | tf_op jit(solution)/shard_map/ppermute | solution.py:328
  110.0 2.2 %collective-permute-done.14 = bf16[4,6,32,128]{3,2,1,0:T(8,128)(2,1)S(1)} collective-permute-done((bf16[4,6,32,128]{3,2,1,0:T(8,128)(2,1)S(1)}, bf16[4,6,32,128]{3,2,1,0:T(8,128)(2,1)S(1)}, u32[]{:S(2)}, u32[]{:S(2)}) %collective-permute-start.14) | collective-permute-done | bytes 196640 | tf_op jit(solution)/shard_map/ppermute | solution.py:328
  114.8 3.1 %collective-permute-start.16 = (bf16[6,32,128]{2,1,0:T(8,128)(2,1)S(1)}, bf16[6,32,128]{2,1,0:T(8,128)(2,1)S(1)}, u32[]{:S(2)}, u32[]{:S(2)}) collective-permute-start(bf16[6,32,128]{2,1,0:T(8,128)(2,1)S(1)} %get-tuple-element.39), channel_id=1, source_target_pairs={{0,8},{4,12},{8,0},{12,4},{16,24},{20,28},{24,16},{28,20},{1,9},{5... | collective-permute-start | bytes 147464 | tf_op jit(solution)/shard_map/ppermute | solution.py:317
  117.9 1.9 %collective-permute-done.18 = bf16[6,32,128]{2,1,0:T(8,128)(2,1)S(1)} collective-permute-done((bf16[6,32,128]{2,1,0:T(8,128)(2,1)S(1)}, bf16[6,32,128]{2,1,0:T(8,128)(2,1)S(1)}, u32[]{:S(2)}, u32[]{:S(2)}) %collective-permute-start.18) | collective-permute-done | bytes 49184 | tf_op jit(solution)/shard_map/ppermute | solution.py:317
  123.1 2.3 %collective-permute-done.20.refs_2_ = bf16[6,32,128]{2,1,0:T(8,128)(2,1)S(1)} collective-permute-done((bf16[6,32,128]{2,1,0:T(8,128)(2,1)S(1)}, bf16[6,32,128]{2,1,0:T(8,128)(2,1)S(1)}, u32[]{:S(2)}, u32[]{:S(2)}) %collective-permute-start.20) | collective-permute-done | bytes 49184 | tf_op jit(solution)/shard_map/ppermute | solution.py:320
  (75 shorter events, 27.5 us)
Async XLA Ops:
  2.3 14.0 %collective-permute-start = (bf16[400,128]{1,0:T(8,128)(2,1)S(1)}, bf16[400,128]{1,0:T(8,128)(2,1)S(1)}, u32[]{:S(2)}, u32[]{:S(2)}) collective-permute-start(bf16[400,128]{1,0:T(8,128)(2,1)S(1)} %pack.1), channel_id=1, source_target_pairs={{0,8},{4,12},{8,0},{12,4},{16,24},{20,28},{24,16},{28,20},{1,9},{5... | collective-permute-start | bytes 307208 | tf_op jit(solution)/shard_map/ppermute | solution.py:317
  5.4 10.9 %collective-permute-start.1 = (bf16[400,128]{1,0:T(8,128)(2,1)S(1)}, bf16[400,128]{1,0:T(8,128)(2,1)S(1)}, u32[]{:S(2)}, u32[]{:S(2)}) collective-permute-start(bf16[400,128]{1,0:T(8,128)(2,1)S(1)} %pack.1), channel_id=1, source_target_pairs={{0,16},{4,20},{8,24},{12,28},{16,0},{20,4},{24,8},{28,12},{1,17},{... | collective-permute-start | bytes 307208 | tf_op jit(solution)/shard_map/ppermute | solution.py:317
  8.0 8.3 %collective-permute-start.2 = (bf16[400,128]{1,0:T(8,128)(2,1)S(1)}, bf16[400,128]{1,0:T(8,128)(2,1)S(1)}, u32[]{:S(2)}, u32[]{:S(2)}) collective-permute-start(bf16[400,128]{1,0:T(8,128)(2,1)S(1)} %pack.1), channel_id=1, source_target_pairs={{0,24},{4,28},{8,16},{12,20},{16,8},{20,12},{24,0},{28,4},{1,25},{... | collective-permute-start | bytes 307208 | tf_op jit(solution)/shard_map/ppermute | solution.py:317
  10.6 35.5 %collective-permute-start.7 = (bf16[8,256,128]{2,1,0:T(8,128)(2,1)}, bf16[8,256,128]{2,1,0:T(8,128)(2,1)}, u32[]{:S(2)}, u32[]{:S(2)}) collective-permute-start(bf16[8,256,128]{2,1,0:T(8,128)(2,1)} %bitcast.64), channel_id=1, source_target_pairs={{0,12},{4,8},{8,4},{12,0},{16,28},{20,24},{24,20},{28,16},{1,13},{... | collective-permute-start | bytes 1572872 | tf_op jit(solution)/shard_map/ppermute | solution.py:317
  16.4 25.4 %collective-permute-start.3 = (bf16[4,400,128]{2,1,0:T(8,128)(2,1)S(1)}, bf16[4,400,128]{2,1,0:T(8,128)(2,1)S(1)}, u32[]{:S(2)}, u32[]{:S(2)}) collective-permute-start(bf16[4,400,128]{2,1,0:T(8,128)(2,1)S(1)} %pad_maximum_fusion.refs_1_), channel_id=1, source_target_pairs={{0,4},{4,0},{8,12},{12,8},{16,20},{20,16},{24,28},{28,24},{1,5},{5... | collective-permute-start | bytes 1228808 | tf_op jit(solution)/shard_map/ppermute | solution.py:317
  17.8 39.5 %collective-permute-start.5 = (bf16[8,256,128]{2,1,0:T(8,128)(2,1)}, bf16[8,256,128]{2,1,0:T(8,128)(2,1)}, u32[]{:S(2)}, u32[]{:S(2)}) collective-permute-start(bf16[8,256,128]{2,1,0:T(8,128)(2,1)} %get-tuple-element.21), channel_id=1, source_target_pairs={{0,4},{4,0},{8,12},{12,8},{16,20},{20,16},{24,28},{28,24},{1,5},{5... | collective-permute-start | bytes 1572872 | tf_op jit(solution)/shard_map/ppermute | solution.py:317
  18.5 41.0 %collective-permute-start.6 = (bf16[8,256,128]{2,1,0:T(8,128)(2,1)}, bf16[8,256,128]{2,1,0:T(8,128)(2,1)}, u32[]{:S(2)}, u32[]{:S(2)}) collective-permute-start(bf16[8,256,128]{2,1,0:T(8,128)(2,1)} %get-tuple-element.22), channel_id=1, source_target_pairs={{0,8},{4,12},{8,0},{12,4},{16,24},{20,28},{24,16},{28,20},{1,9},{5... | collective-permute-start | bytes 1572872 | tf_op jit(solution)/shard_map/ppermute | solution.py:317
  20.0 52.3 %all-to-all-start = ((bf16[8,8,128,128]{3,2,1,0:T(8,128)(2,1)}), bf16[8,8,128,128]{3,2,1,0:T(8,128)(2,1)}, u32[]{:S(2)}, u32[]{:S(2)}) async-start(bf16[8,8,128,128]{3,2,1,0:T(8,128)(2,1)} %touch.3), calls=%async_computation | async-start | bytes 4194304 | tf_op jit(solution)/shard_map/all_to_all | solution.py:342
  43.2 16.3 %collective-permute-start.4 = (bf16[8,400,128]{2,1,0:T(8,128)(2,1)}, bf16[8,400,128]{2,1,0:T(8,128)(2,1)}, u32[]{:S(2)}, u32[]{:S(2)}) collective-permute-start(bf16[8,400,128]{2,1,0:T(8,128)(2,1)} %constant_dynamic-update-slice_fusion.refs_2_.refs_1_), channel_id=1, source_target_pairs={{0,1},{1,0},{2,3},{3,2},{4,5},{5,4},{6,7},{7,6},{8,9},{9,8},{10,11... | collective-permute-start | bytes 2457608 | tf_op jit(solution)/shard_map/ppermute | solution.py:320
  46.1 13.4 %copy-start.1 = (s32[440]{0:T(512)S(1)}, s32[440]{0:T(512)}, u32[]{:S(2)}) copy-start(s32[440]{0:T(512)} %plan.1.refs_3_.refs_1_.refs_0_) | copy-start | bytes 5284
  72.3 9.1 %collective-permute-start.11 = (bf16[64,128,128]{2,1,0:T(8,128)(2,1)}, bf16[64,128,128]{2,1,0:T(8,128)(2,1)}, u32[]{:S(2)}, u32[]{:S(2)}) collective-permute-start(bf16[64,128,128]{2,1,0:T(8,128)(2,1)} %bitcast.17.refs_2_), channel_id=1, source_target_pairs={{0,1},{1,0},{2,3},{3,2},{4,5},{5,4},{6,7},{7,6},{8,9},{9,8},{10,11... | collective-permute-start | bytes 6291464 | tf_op jit(solution)/shard_map/ppermute | solution.py:320
  72.3 26.6 %collective-permute-start.12 = (bf16[32,256,128]{2,1,0:T(8,128)(2,1)}, bf16[32,256,128]{2,1,0:T(8,128)(2,1)S(1)}, u32[]{:S(2)}, u32[]{:S(2)}) collective-permute-start(bf16[32,256,128]{2,1,0:T(8,128)(2,1)} %copy-done.5), channel_id=1, source_target_pairs={{0,1},{1,0},{2,3},{3,2},{4,5},{5,4},{6,7},{7,6},{8,9},{9,8},{10,11... | collective-permute-start | bytes 6291464 | tf_op jit(solution)/shard_map/ppermute | solution.py:320
  72.9 20.9 %collective-permute-start.10 = (bf16[8,64,256]{2,1,0:T(8,128)(2,1)}, bf16[8,64,256]{2,1,0:T(8,128)(2,1)}, u32[]{:S(2)}, u32[]{:S(2)}) collective-permute-start(bf16[8,64,256]{2,1,0:T(8,128)(2,1)} %get-tuple-element.29), channel_id=1, source_target_pairs={{0,16},{4,20},{8,24},{12,28},{16,0},{20,4},{24,8},{28,12},{1,17},{... | collective-permute-start | bytes 786440 | tf_op jit(solution)/shard_map/ppermute | solution.py:317
  72.9 23.3 %collective-permute-start.8 = (bf16[8,64,256]{2,1,0:T(8,128)(2,1)}, bf16[8,64,256]{2,1,0:T(8,128)(2,1)S(1)}, u32[]{:S(2)}, u32[]{:S(2)}) collective-permute-start(bf16[8,64,256]{2,1,0:T(8,128)(2,1)} %copy-done.7), channel_id=1, source_target_pairs={{0,1},{1,0},{2,3},{3,2},{4,5},{5,4},{6,7},{7,6},{8,9},{9,8},{10,11... | collective-permute-start | bytes 786440 | tf_op jit(solution)/shard_map/ppermute | solution.py:320
  72.9 26.0 %collective-permute-start.9 = (bf16[8,64,256]{2,1,0:T(8,128)(2,1)}, bf16[8,64,256]{2,1,0:T(8,128)(2,1)}, u32[]{:S(2)}, u32[]{:S(2)}) collective-permute-start(bf16[8,64,256]{2,1,0:T(8,128)(2,1)} %copy-done.6), channel_id=1, source_target_pairs={{0,17},{1,16},{2,19},{3,18},{4,21},{5,20},{6,23},{7,22},{8,25},{9,... | collective-permute-start | bytes 786440 | tf_op jit(solution)/shard_map/ppermute | solution.py:328
  101.2 8.8 %collective-permute-start.15 = (bf16[4,6,32,128]{3,2,1,0:T(8,128)(2,1)S(1)}, bf16[4,6,32,128]{3,2,1,0:T(8,128)(2,1)S(1)}, u32[]{:S(2)}, u32[]{:S(2)}) collective-permute-start(bf16[4,6,32,128]{3,2,1,0:T(8,128)(2,1)S(1)} %get-tuple-element.38), channel_id=1, source_target_pairs={{0,6},{1,7},{2,4},{3,5},{4,2},{5,3},{6,0},{7,1},{8,14},{9,15},{10,... | collective-permute-start | bytes 589832 | tf_op jit(solution)/shard_map/ppermute | solution.py:328
  101.3 10.9 %collective-permute-start.14 = (bf16[4,6,32,128]{3,2,1,0:T(8,128)(2,1)S(1)}, bf16[4,6,32,128]{3,2,1,0:T(8,128)(2,1)S(1)}, u32[]{:S(2)}, u32[]{:S(2)}) collective-permute-start(bf16[4,6,32,128]{3,2,1,0:T(8,128)(2,1)S(1)} %get-tuple-element.37), channel_id=1, source_target_pairs={{0,2},{1,3},{2,0},{3,1},{4,6},{5,7},{6,4},{7,5},{8,10},{9,11},{10,... | collective-permute-start | bytes 589832 | tf_op jit(solution)/shard_map/ppermute | solution.py:328
  102.9 10.4 %collective-permute-start.13 = (bf16[4,6,32,128]{3,2,1,0:T(8,128)(2,1)S(1)}, bf16[4,6,32,128]{3,2,1,0:T(8,128)(2,1)S(1)}, u32[]{:S(2)}, u32[]{:S(2)}) collective-permute-start(bf16[4,6,32,128]{3,2,1,0:T(8,128)(2,1)S(1)} %fusion.4), channel_id=1, source_target_pairs={{0,4},{1,5},{2,6},{3,7},{4,0},{5,1},{6,2},{7,3},{8,12},{9,13},{10,... | collective-permute-start | bytes 589832 | tf_op jit(solution)/shard_map/ppermute | solution.py:328
  113.4 6.4 %collective-permute-start.18 = (bf16[6,32,128]{2,1,0:T(8,128)(2,1)S(1)}, bf16[6,32,128]{2,1,0:T(8,128)(2,1)S(1)}, u32[]{:S(2)}, u32[]{:S(2)}) collective-permute-start(bf16[6,32,128]{2,1,0:T(8,128)(2,1)S(1)} %get-tuple-element.40), channel_id=1, source_target_pairs={{0,24},{4,28},{8,16},{12,20},{16,8},{20,12},{24,0},{28,4},{1,25},{... | collective-permute-start | bytes 147464 | tf_op jit(solution)/shard_map/ppermute | solution.py:317
  114.8 6.3 %collective-permute-start.17 = (bf16[6,32,128]{2,1,0:T(8,128)(2,1)S(1)}, bf16[6,32,128]{2,1,0:T(8,128)(2,1)S(1)}, u32[]{:S(2)}, u32[]{:S(2)}) collective-permute-start(bf16[6,32,128]{2,1,0:T(8,128)(2,1)S(1)} %get-tuple-element.41), channel_id=1, source_target_pairs={{0,16},{4,20},{8,24},{12,28},{16,0},{20,4},{24,8},{28,12},{1,17},{... | collective-permute-start | bytes 147464 | tf_op jit(solution)/shard_map/ppermute | solution.py:317
  114.8 6.3 %collective-permute-start.16 = (bf16[6,32,128]{2,1,0:T(8,128)(2,1)S(1)}, bf16[6,32,128]{2,1,0:T(8,128)(2,1)S(1)}, u32[]{:S(2)}, u32[]{:S(2)}) collective-permute-start(bf16[6,32,128]{2,1,0:T(8,128)(2,1)S(1)} %get-tuple-element.39), channel_id=1, source_target_pairs={{0,8},{4,12},{8,0},{12,4},{16,24},{20,28},{24,16},{28,20},{1,9},{5... | collective-permute-start | bytes 147464 | tf_op jit(solution)/shard_map/ppermute | solution.py:317
  121.1 1.9 %collective-permute-start.19 = (bf16[6,32,128]{2,1,0:T(8,128)(2,1)S(1)}, bf16[6,32,128]{2,1,0:T(8,128)(2,1)S(1)}, u32[]{:S(2)}, u32[]{:S(2)}) collective-permute-start(bf16[6,32,128]{2,1,0:T(8,128)(2,1)S(1)} %fusion.7.refs_0_), channel_id=1, source_target_pairs={{0,1},{1,0},{2,3},{3,2},{4,5},{5,4},{6,7},{7,6},{8,9},{9,8},{10,11... | collective-permute-start | bytes 147464 | tf_op jit(solution)/shard_map/ppermute | solution.py:320
  121.2 4.2 %collective-permute-start.20 = (bf16[6,32,128]{2,1,0:T(8,128)(2,1)S(1)}, bf16[6,32,128]{2,1,0:T(8,128)(2,1)S(1)}, u32[]{:S(2)}, u32[]{:S(2)}) collective-permute-start(bf16[6,32,128]{2,1,0:T(8,128)(2,1)S(1)} %fusion.7.refs_0_), channel_id=1, source_target_pairs={{0,2},{1,3},{2,0},{3,1},{4,6},{5,7},{6,4},{7,5},{8,10},{9,11},{10,... | collective-permute-start | bytes 147464 | tf_op jit(solution)/shard_map/ppermute | solution.py:320
  122.7 3.7 %collective-permute-start.21 = (bf16[6,32,128]{2,1,0:T(8,128)(2,1)S(1)}, bf16[6,32,128]{2,1,0:T(8,128)(2,1)S(1)}, u32[]{:S(2)}, u32[]{:S(2)}) collective-permute-start(bf16[6,32,128]{2,1,0:T(8,128)(2,1)S(1)} %fusion.7.refs_0_), channel_id=1, source_target_pairs={{0,3},{1,2},{2,1},{3,0},{4,7},{5,6},{6,5},{7,4},{8,11},{9,10},{10,... | collective-permute-start | bytes 147464 | tf_op jit(solution)/shard_map/ppermute | solution.py:320
  (9 other events, 30.1 us)

commit v7 on v6

--- a/solution.py
+++ b/solution.py
@@ -345,7 +345,7 @@
 
     others = over_aux(blocks, 1)
     mine = [over_pair(pieces[d], d) for d in range(1, MEMBERS)]
-    mine = [pieces[0], *touch(mine, listed, others)]
+    mine = [pieces[0], *touch(mine, listed)]
     own, same, cross, again, stack = contract(place, listed, blocks, others, mine, pairs, virt, rows)
     got = over_pair(same, MEMBERS), over_both(cross, MEMBERS, 1)
     own = own, over_aux(again, 1)

time: 128 us -> 128 us (level)
    unnamed x24 -> x26, local copies, waits for them, and re-layouts: 7.03 us -> 7.66 us
where the time goes in v7:
time: 128 us; the launch traced here: 127 us
  waiting for transfers between devices  58.2 us (45%)
  starting transfers between devices  29.4 us (23%)
  Pallas kernels  23.2 us (18%)
  local copies, waits for them, and re-layouts  15 us (12%)
    ppermute x11, waiting for transfers between devices, over_pair(): lax.ppermute(value, 'pair', [(i, i ^ distance) for i in range(pairs)])  38.3 us
    ppermute x11, starting transfers between devices, over_pair(): lax.ppermute(value, 'pair', [(i, i ^ distance) for i in range(pairs)])  15.7 us
    ppermute x4, waiting for transfers between devices, over_both(): return lax.ppermute(value, ('pair', 'aux'), route)  11.2 us
    pallas_call x2, Pallas kernels, whole(): pl.pallas_call(lambda *refs: whole_kernel(owners, rows, virt, *refs), out...  11.1 us
    unnamed x26, local copies, waits for them, and re-layouts  7.66 us
    ppermute x4, starting transfers between devices, over_both(): return lax.ppermute(value, ('pair', 'aux'), route)  6.57 us
    all_to_all x1, waiting for transfers between devices, near_plan(): lax.all_to_all(touch([jnp.transpose(full, (0, 2, 1, 3))], near)[0], 'pair...  5.39 us
    all_to_all x1, starting transfers between devices, near_plan(): lax.all_to_all(touch([jnp.transpose(full, (0, 2, 1, 3))], near)[0], 'pair...  4.66 us
  transfers between devices with their start and end apart: 23, of which 13 were waited for; matrix products, arithmetic and copies ran while one was open for 8% of the time, Pallas kernels for 16%

profile of v7, /device:TPU:0, one launch (start us, length us, event | category | flops | bytes accessed | tf_op | source)
XLA Modules:
  0.0 127.1 jit_solution(2605600463510715663)
XLA Ops:
  2.3 3.1 %collective-permute-start = (bf16[400,128]{1,0:T(8,128)(2,1)S(1)}, bf16[400,128]{1,0:T(8,128)(2,1)S(1)}, u32[]{:S(2)}, u32[]{:S(2)}) collective-permute-start(bf16[400,128]{1,0:T(8,128)(2,1)S(1)} %pack.1), channel_id=1, source_target_pairs={{0,8},{4,12},{8,0},{12,4},{16,24},{20,28},{24,16},{28,20},{1,9},{5... | collective-permute-start | bytes 307208 | tf_op jit(solution)/shard_map/ppermute | solution.py:317
  5.4 2.6 %collective-permute-start.1 = (bf16[400,128]{1,0:T(8,128)(2,1)S(1)}, bf16[400,128]{1,0:T(8,128)(2,1)S(1)}, u32[]{:S(2)}, u32[]{:S(2)}) collective-permute-start(bf16[400,128]{1,0:T(8,128)(2,1)S(1)} %pack.1), channel_id=1, source_target_pairs={{0,16},{4,20},{8,24},{12,28},{16,0},{20,4},{24,8},{28,12},{1,17},{... | collective-permute-start | bytes 307208 | tf_op jit(solution)/shard_map/ppermute | solution.py:317
  10.6 1.9 %collective-permute-start.7 = (bf16[8,256,128]{2,1,0:T(8,128)(2,1)}, bf16[8,256,128]{2,1,0:T(8,128)(2,1)}, u32[]{:S(2)}, u32[]{:S(2)}) collective-permute-start(bf16[8,256,128]{2,1,0:T(8,128)(2,1)} %bitcast.64), channel_id=1, source_target_pairs={{0,12},{4,8},{8,4},{12,0},{16,28},{20,24},{24,20},{28,16},{1,13},{... | collective-permute-start | bytes 1572872 | tf_op jit(solution)/shard_map/ppermute | solution.py:317
  14.3 2.0 %copy.41 = bf16[8,128,8,128]{3,1,2,0:T(8,128)(2,1)} copy(bf16[8,128,8,128]{3,2,1,0:T(8,128)(2,1)S(1)} %bitcast.70) | data formatting | bytes 4194304 | tf_op jit(solution)/shard_map/optimization_barrier | solution.py:331
  20.0 4.7 %all-to-all-start = ((bf16[8,8,128,128]{3,2,1,0:T(8,128)(2,1)}), bf16[8,8,128,128]{3,2,1,0:T(8,128)(2,1)}, u32[]{:S(2)}, u32[]{:S(2)}) async-start(bf16[8,8,128,128]{3,2,1,0:T(8,128)(2,1)} %touch.3), calls=%async_computation | async-start | bytes 4194304 | tf_op jit(solution)/shard_map/all_to_all | solution.py:342
  26.6 15.1 %collective-permute-done.3 = bf16[4,400,128]{2,1,0:T(8,128)(2,1)S(1)} collective-permute-done((bf16[4,400,128]{2,1,0:T(8,128)(2,1)S(1)}, bf16[4,400,128]{2,1,0:T(8,128)(2,1)S(1)}, u32[]{:S(2)}, u32[]{:S(2)}) %collective-permute-start.3) | collective-permute-done | bytes 409632 | tf_op jit(solution)/shard_map/ppermute | solution.py:317
  43.9 2.3 %plan.1.refs_3_.refs_1_.refs_0_ = s32[440]{0:T(512)} custom-call(s32[48,3]{1,0:T(8,128)} %reshape.45.refs_0_), custom_call_target="tpu_custom_call" | custom-call | flops 9999999827968 | tf_op jit(solution)/shard_map/plan/pallas_call | solution.py:80
  46.3 11.1 %collective-permute-done.5.refs_0_ = bf16[8,256,128]{2,1,0:T(8,128)(2,1)} collective-permute-done((bf16[8,256,128]{2,1,0:T(8,128)(2,1)}, bf16[8,256,128]{2,1,0:T(8,128)(2,1)}, u32[]{:S(2)}, u32[]{:S(2)}) %collective-permute-start.5) | collective-permute-done | bytes 524320 | tf_op jit(solution)/shard_map/ppermute | solution.py:317
  57.4 2.1 %collective-permute-done.6.refs_1_ = bf16[8,256,128]{2,1,0:T(8,128)(2,1)} collective-permute-done((bf16[8,256,128]{2,1,0:T(8,128)(2,1)}, bf16[8,256,128]{2,1,0:T(8,128)(2,1)}, u32[]{:S(2)}, u32[]{:S(2)}) %collective-permute-start.6) | collective-permute-done | bytes 524320 | tf_op jit(solution)/shard_map/ppermute | solution.py:317
  60.1 4.1 %contract.1 = (f32[8,64,256]{2,1,0:T(8,128)S(1)}, bf16[8,64,256]{2,1,0:T(8,128)(2,1)}, bf16[8,64,256]{2,1,0:T(8,128)(2,1)S(1)}, bf16[8,64,256]{2,1,0:T(8,128)(2,1)S(1)}, bf16[32,256,128]{2,1,0:T(8,128)(2,1)S(1)}) custom-call(s32[2]{0:T(128)S(1)} %copy-done.4, s32[440]{0:T(512)S(1)} %copy-done.1, ...), custom_call_target="tpu_custom_call" | custom-call | flops 9999999827968 | tf_op jit(solution)/shard_map/contract/pallas_call | solution.py:185
  67.0 5.4 %all-to-all-done = bf16[8,8,128,128]{3,2,1,0:T(8,128)(2,1)} async-done(((bf16[8,8,128,128]{3,2,1,0:T(8,128)(2,1)}), bf16[8,8,128,128]{3,2,1,0:T(8,128)(2,1)}, u32[]{:S(2)}, u32[]{:S(2)}) %all-to-all-start) | async-done | bytes 2097184 | tf_op jit(solution)/shard_map/all_to_all | solution.py:342
  72.9 3.0 %collective-permute-start.9 = (bf16[8,64,256]{2,1,0:T(8,128)(2,1)}, bf16[8,64,256]{2,1,0:T(8,128)(2,1)}, u32[]{:S(2)}, u32[]{:S(2)}) collective-permute-start(bf16[8,64,256]{2,1,0:T(8,128)(2,1)} %copy-done.7), channel_id=1, source_target_pairs={{0,17},{1,16},{2,19},{3,18},{4,21},{5,20},{6,23},{7,22},{8,25},{9,... | collective-permute-start | bytes 786440 | tf_op jit(solution)/shard_map/ppermute | solution.py:328
  75.9 5.5 %whole.2.refs_3_ = f32[49,64,128]{2,1,0:T(8,128)S(1)} custom-call(s32[440]{0:T(512)S(1)} %copy-done.2, bf16[8,400,128]{2,1,0:T(8,128)(2,1)} %constant_dynamic-update-slice_fusion.refs_2_.refs_1_, bf16[64,128,128]{2,1,0:T(8,128)(2,1)} %bitcast.17.refs_2_), custom_call_target="tpu_custom_call" | custom-call | tf_op jit(solution)/shard_map/whole/pallas_call | solution.py:215
  81.4 5.5 %whole.3.refs_4_ = f32[49,64,128]{2,1,0:T(8,128)S(1)} custom-call(s32[440]{0:T(512)S(1)} %copy-done.2, bf16[8,400,128]{2,1,0:T(8,128)(2,1)} %constant_dynamic-update-slice_fusion.refs_2_.refs_1_, bf16[64,128,128]{2,1,0:T(8,128)(2,1)} %collective-permute-done.11.refs_2_, f32[49,64,128]{2,1,0:T(8,128)S(1)} %whole.2.refs_3_), custom_call_target="tpu_custom_call" | custom-call | tf_op jit(solution)/shard_map/whole/pallas_call | solution.py:215
  87.0 6.7 %collective-permute-done.10.refs_3_ = bf16[8,64,256]{2,1,0:T(8,128)(2,1)} collective-permute-done((bf16[8,64,256]{2,1,0:T(8,128)(2,1)}, bf16[8,64,256]{2,1,0:T(8,128)(2,1)}, u32[]{:S(2)}, u32[]{:S(2)}) %collective-permute-start.10) | collective-permute-done | bytes 262176 | tf_op jit(solution)/shard_map/ppermute | solution.py:317
  93.7 2.5 %project.2.refs_4_ = f32[49,64,128]{2,1,0:T(8,128)S(1)} custom-call(s32[2]{0:T(128)S(1)} %copy-done.4, s32[440]{0:T(512)S(1)} %copy-done.2, f32[8,64,256]{2,1,0:T(8,128)S(1)} %get-tuple-element.28.refs_2_, bf16[8,64,256]{2,1,0:T(8,128)(2,1)} %collective-permute-done.10.refs_3_, f32[49,64,128]{2,1,0:T(8,128)S(1)} %whole.3.refs_4_, ...), custom_call_target="tpu_custom_call" | custom-call | tf_op jit(solution)/shard_map/project/pallas_call | solution.py:246
  96.2 2.7 %collective-permute-done.9.refs_3_ = bf16[8,64,256]{2,1,0:T(8,128)(2,1)} collective-permute-done((bf16[8,64,256]{2,1,0:T(8,128)(2,1)}, bf16[8,64,256]{2,1,0:T(8,128)(2,1)}, u32[]{:S(2)}, u32[]{:S(2)}) %collective-permute-start.9) | collective-permute-done | bytes 262176 | tf_op jit(solution)/shard_map/ppermute | solution.py:328
  98.9 2.0 %project.3 = f32[49,64,128]{2,1,0:T(8,128)S(1)} custom-call(s32[2]{0:T(128)S(1)} %copy-done.4, s32[440]{0:T(512)S(1)} %copy-done.2, bf16[8,64,256]{2,1,0:T(8,128)(2,1)S(1)} %collective-permute-done.8.refs_2_, bf16[8,64,256]{2,1,0:T(8,128)(2,1)} %collective-permute-done.9.refs_3_, f32[49,64,128]{2,1,0:T(8,128)S(1)} %project.2.refs_4_, ...), custom_call_target="tpu_custom_call" | custom-call | tf_op jit(solution)/shard_map/project/pallas_call | solution.py:246
  102.9 2.0 %collective-permute-start.13 = (bf16[4,6,32,128]{3,2,1,0:T(8,128)(2,1)S(1)}, bf16[4,6,32,128]{3,2,1,0:T(8,128)(2,1)S(1)}, u32[]{:S(2)}, u32[]{:S(2)}) collective-permute-start(bf16[4,6,32,128]{3,2,1,0:T(8,128)(2,1)S(1)} %fusion.4), channel_id=1, source_target_pairs={{0,4},{1,5},{2,6},{3,7},{4,0},{5,1},{6,2},{7,3},{8,12},{9,13},{10,... | collective-permute-start | bytes 589832 | tf_op jit(solution)/shard_map/ppermute | solution.py:328
  104.9 5.1 %collective-permute-done.15 = bf16[4,6,32,128]{3,2,1,0:T(8,128)(2,1)S(1)} collective-permute-done((bf16[4,6,32,128]{3,2,1,0:T(8,128)(2,1)S(1)}, bf16[4,6,32,128]{3,2,1,0:T(8,128)(2,1)S(1)}, u32[]{:S(2)}, u32[]{:S(2)}) %collective-permute-start.15) | collective-permute-done | bytes 196640 | tf_op jit(solution)/shard_map/ppermute | solution.py:328
  110.0 2.2 %collective-permute-done.14 = bf16[4,6,32,128]{3,2,1,0:T(8,128)(2,1)S(1)} collective-permute-done((bf16[4,6,32,128]{3,2,1,0:T(8,128)(2,1)S(1)}, bf16[4,6,32,128]{3,2,1,0:T(8,128)(2,1)S(1)}, u32[]{:S(2)}, u32[]{:S(2)}) %collective-permute-start.14) | collective-permute-done | bytes 196640 | tf_op jit(solution)/shard_map/ppermute | solution.py:328
  114.8 3.1 %collective-permute-start.16 = (bf16[6,32,128]{2,1,0:T(8,128)(2,1)S(1)}, bf16[6,32,128]{2,1,0:T(8,128)(2,1)S(1)}, u32[]{:S(2)}, u32[]{:S(2)}) collective-permute-start(bf16[6,32,128]{2,1,0:T(8,128)(2,1)S(1)} %get-tuple-element.39), channel_id=1, source_target_pairs={{0,8},{4,12},{8,0},{12,4},{16,24},{20,28},{24,16},{28,20},{1,9},{5... | collective-permute-start | bytes 147464 | tf_op jit(solution)/shard_map/ppermute | solution.py:317
  117.9 1.9 %collective-permute-done.18 = bf16[6,32,128]{2,1,0:T(8,128)(2,1)S(1)} collective-permute-done((bf16[6,32,128]{2,1,0:T(8,128)(2,1)S(1)}, bf16[6,32,128]{2,1,0:T(8,128)(2,1)S(1)}, u32[]{:S(2)}, u32[]{:S(2)}) %collective-permute-start.18) | collective-permute-done | bytes 49184 | tf_op jit(solution)/shard_map/ppermute | solution.py:317
  123.1 2.3 %collective-permute-done.20.refs_2_ = bf16[6,32,128]{2,1,0:T(8,128)(2,1)S(1)} collective-permute-done((bf16[6,32,128]{2,1,0:T(8,128)(2,1)S(1)}, bf16[6,32,128]{2,1,0:T(8,128)(2,1)S(1)}, u32[]{:S(2)}, u32[]{:S(2)}) %collective-permute-start.20) | collective-permute-done | bytes 49184 | tf_op jit(solution)/shard_map/ppermute | solution.py:320
  (77 shorter events, 28.1 us)
Async XLA Ops:
  2.3 13.9 %collective-permute-start = (bf16[400,128]{1,0:T(8,128)(2,1)S(1)}, bf16[400,128]{1,0:T(8,128)(2,1)S(1)}, u32[]{:S(2)}, u32[]{:S(2)}) collective-permute-start(bf16[400,128]{1,0:T(8,128)(2,1)S(1)} %pack.1), channel_id=1, source_target_pairs={{0,8},{4,12},{8,0},{12,4},{16,24},{20,28},{24,16},{28,20},{1,9},{5... | collective-permute-start | bytes 307208 | tf_op jit(solution)/shard_map/ppermute | solution.py:317
  5.4 10.8 %collective-permute-start.1 = (bf16[400,128]{1,0:T(8,128)(2,1)S(1)}, bf16[400,128]{1,0:T(8,128)(2,1)S(1)}, u32[]{:S(2)}, u32[]{:S(2)}) collective-permute-start(bf16[400,128]{1,0:T(8,128)(2,1)S(1)} %pack.1), channel_id=1, source_target_pairs={{0,16},{4,20},{8,24},{12,28},{16,0},{20,4},{24,8},{28,12},{1,17},{... | collective-permute-start | bytes 307208 | tf_op jit(solution)/shard_map/ppermute | solution.py:317
  8.0 8.3 %collective-permute-start.2 = (bf16[400,128]{1,0:T(8,128)(2,1)S(1)}, bf16[400,128]{1,0:T(8,128)(2,1)S(1)}, u32[]{:S(2)}, u32[]{:S(2)}) collective-permute-start(bf16[400,128]{1,0:T(8,128)(2,1)S(1)} %pack.1), channel_id=1, source_target_pairs={{0,24},{4,28},{8,16},{12,20},{16,8},{20,12},{24,0},{28,4},{1,25},{... | collective-permute-start | bytes 307208 | tf_op jit(solution)/shard_map/ppermute | solution.py:317
  10.6 35.7 %collective-permute-start.7 = (bf16[8,256,128]{2,1,0:T(8,128)(2,1)}, bf16[8,256,128]{2,1,0:T(8,128)(2,1)}, u32[]{:S(2)}, u32[]{:S(2)}) collective-permute-start(bf16[8,256,128]{2,1,0:T(8,128)(2,1)} %bitcast.64), channel_id=1, source_target_pairs={{0,12},{4,8},{8,4},{12,0},{16,28},{20,24},{24,20},{28,16},{1,13},{... | collective-permute-start | bytes 1572872 | tf_op jit(solution)/shard_map/ppermute | solution.py:317
  16.4 25.4 %collective-permute-start.3 = (bf16[4,400,128]{2,1,0:T(8,128)(2,1)S(1)}, bf16[4,400,128]{2,1,0:T(8,128)(2,1)S(1)}, u32[]{:S(2)}, u32[]{:S(2)}) collective-permute-start(bf16[4,400,128]{2,1,0:T(8,128)(2,1)S(1)} %pad_maximum_fusion.refs_1_), channel_id=1, source_target_pairs={{0,4},{4,0},{8,12},{12,8},{16,20},{20,16},{24,28},{28,24},{1,5},{5... | collective-permute-start | bytes 1228808 | tf_op jit(solution)/shard_map/ppermute | solution.py:317
  17.8 39.5 %collective-permute-start.5 = (bf16[8,256,128]{2,1,0:T(8,128)(2,1)}, bf16[8,256,128]{2,1,0:T(8,128)(2,1)}, u32[]{:S(2)}, u32[]{:S(2)}) collective-permute-start(bf16[8,256,128]{2,1,0:T(8,128)(2,1)} %get-tuple-element.21), channel_id=1, source_target_pairs={{0,4},{4,0},{8,12},{12,8},{16,20},{20,16},{24,28},{28,24},{1,5},{5... | collective-permute-start | bytes 1572872 | tf_op jit(solution)/shard_map/ppermute | solution.py:317
  18.5 41.1 %collective-permute-start.6 = (bf16[8,256,128]{2,1,0:T(8,128)(2,1)}, bf16[8,256,128]{2,1,0:T(8,128)(2,1)}, u32[]{:S(2)}, u32[]{:S(2)}) collective-permute-start(bf16[8,256,128]{2,1,0:T(8,128)(2,1)} %get-tuple-element.22), channel_id=1, source_target_pairs={{0,8},{4,12},{8,0},{12,4},{16,24},{20,28},{24,16},{28,20},{1,9},{5... | collective-permute-start | bytes 1572872 | tf_op jit(solution)/shard_map/ppermute | solution.py:317
  20.0 52.3 %all-to-all-start = ((bf16[8,8,128,128]{3,2,1,0:T(8,128)(2,1)}), bf16[8,8,128,128]{3,2,1,0:T(8,128)(2,1)}, u32[]{:S(2)}, u32[]{:S(2)}) async-start(bf16[8,8,128,128]{3,2,1,0:T(8,128)(2,1)} %touch.3), calls=%async_computation | async-start | bytes 4194304 | tf_op jit(solution)/shard_map/all_to_all | solution.py:342
  43.3 16.2 %collective-permute-start.4 = (bf16[8,400,128]{2,1,0:T(8,128)(2,1)}, bf16[8,400,128]{2,1,0:T(8,128)(2,1)}, u32[]{:S(2)}, u32[]{:S(2)}) collective-permute-start(bf16[8,400,128]{2,1,0:T(8,128)(2,1)} %constant_dynamic-update-slice_fusion.refs_2_.refs_1_), channel_id=1, source_target_pairs={{0,1},{1,0},{2,3},{3,2},{4,5},{5,4},{6,7},{7,6},{8,9},{9,8},{10,11... | collective-permute-start | bytes 2457608 | tf_op jit(solution)/shard_map/ppermute | solution.py:320
  60.1 15.8 %copy-start.2 = (s32[440]{0:T(512)S(1)}, s32[440]{0:T(512)}, u32[]{:S(2)}) copy-start(s32[440]{0:T(512)} %plan.1.refs_3_.refs_1_.refs_0_) | copy-start | bytes 5284
  72.3 9.1 %collective-permute-start.11 = (bf16[64,128,128]{2,1,0:T(8,128)(2,1)}, bf16[64,128,128]{2,1,0:T(8,128)(2,1)}, u32[]{:S(2)}, u32[]{:S(2)}) collective-permute-start(bf16[64,128,128]{2,1,0:T(8,128)(2,1)} %bitcast.17.refs_2_), channel_id=1, source_target_pairs={{0,1},{1,0},{2,3},{3,2},{4,5},{5,4},{6,7},{7,6},{8,9},{9,8},{10,11... | collective-permute-start | bytes 6291464 | tf_op jit(solution)/shard_map/ppermute | solution.py:320
  72.3 26.6 %collective-permute-start.12 = (bf16[32,256,128]{2,1,0:T(8,128)(2,1)}, bf16[32,256,128]{2,1,0:T(8,128)(2,1)S(1)}, u32[]{:S(2)}, u32[]{:S(2)}) collective-permute-start(bf16[32,256,128]{2,1,0:T(8,128)(2,1)} %copy-done.6), channel_id=1, source_target_pairs={{0,1},{1,0},{2,3},{3,2},{4,5},{5,4},{6,7},{7,6},{8,9},{9,8},{10,11... | collective-permute-start | bytes 6291464 | tf_op jit(solution)/shard_map/ppermute | solution.py:320
  72.9 20.9 %collective-permute-start.10 = (bf16[8,64,256]{2,1,0:T(8,128)(2,1)}, bf16[8,64,256]{2,1,0:T(8,128)(2,1)}, u32[]{:S(2)}, u32[]{:S(2)}) collective-permute-start(bf16[8,64,256]{2,1,0:T(8,128)(2,1)} %get-tuple-element.29), channel_id=1, source_target_pairs={{0,16},{4,20},{8,24},{12,28},{16,0},{20,4},{24,8},{28,12},{1,17},{... | collective-permute-start | bytes 786440 | tf_op jit(solution)/shard_map/ppermute | solution.py:317
  72.9 23.3 %collective-permute-start.8 = (bf16[8,64,256]{2,1,0:T(8,128)(2,1)}, bf16[8,64,256]{2,1,0:T(8,128)(2,1)S(1)}, u32[]{:S(2)}, u32[]{:S(2)}) collective-permute-start(bf16[8,64,256]{2,1,0:T(8,128)(2,1)} %copy-done.8), channel_id=1, source_target_pairs={{0,1},{1,0},{2,3},{3,2},{4,5},{5,4},{6,7},{7,6},{8,9},{9,8},{10,11... | collective-permute-start | bytes 786440 | tf_op jit(solution)/shard_map/ppermute | solution.py:320
  72.9 26.0 %collective-permute-start.9 = (bf16[8,64,256]{2,1,0:T(8,128)(2,1)}, bf16[8,64,256]{2,1,0:T(8,128)(2,1)}, u32[]{:S(2)}, u32[]{:S(2)}) collective-permute-start(bf16[8,64,256]{2,1,0:T(8,128)(2,1)} %copy-done.7), channel_id=1, source_target_pairs={{0,17},{1,16},{2,19},{3,18},{4,21},{5,20},{6,23},{7,22},{8,25},{9,... | collective-permute-start | bytes 786440 | tf_op jit(solution)/shard_map/ppermute | solution.py:328
  101.2 8.8 %collective-permute-start.15 = (bf16[4,6,32,128]{3,2,1,0:T(8,128)(2,1)S(1)}, bf16[4,6,32,128]{3,2,1,0:T(8,128)(2,1)S(1)}, u32[]{:S(2)}, u32[]{:S(2)}) collective-permute-start(bf16[4,6,32,128]{3,2,1,0:T(8,128)(2,1)S(1)} %get-tuple-element.38), channel_id=1, source_target_pairs={{0,6},{1,7},{2,4},{3,5},{4,2},{5,3},{6,0},{7,1},{8,14},{9,15},{10,... | collective-permute-start | bytes 589832 | tf_op jit(solution)/shard_map/ppermute | solution.py:328
  101.3 10.9 %collective-permute-start.14 = (bf16[4,6,32,128]{3,2,1,0:T(8,128)(2,1)S(1)}, bf16[4,6,32,128]{3,2,1,0:T(8,128)(2,1)S(1)}, u32[]{:S(2)}, u32[]{:S(2)}) collective-permute-start(bf16[4,6,32,128]{3,2,1,0:T(8,128)(2,1)S(1)} %get-tuple-element.37), channel_id=1, source_target_pairs={{0,2},{1,3},{2,0},{3,1},{4,6},{5,7},{6,4},{7,5},{8,10},{9,11},{10,... | collective-permute-start | bytes 589832 | tf_op jit(solution)/shard_map/ppermute | solution.py:328
  102.9 10.4 %collective-permute-start.13 = (bf16[4,6,32,128]{3,2,1,0:T(8,128)(2,1)S(1)}, bf16[4,6,32,128]{3,2,1,0:T(8,128)(2,1)S(1)}, u32[]{:S(2)}, u32[]{:S(2)}) collective-permute-start(bf16[4,6,32,128]{3,2,1,0:T(8,128)(2,1)S(1)} %fusion.4), channel_id=1, source_target_pairs={{0,4},{1,5},{2,6},{3,7},{4,0},{5,1},{6,2},{7,3},{8,12},{9,13},{10,... | collective-permute-start | bytes 589832 | tf_op jit(solution)/shard_map/ppermute | solution.py:328
  113.4 6.3 %collective-permute-start.18 = (bf16[6,32,128]{2,1,0:T(8,128)(2,1)S(1)}, bf16[6,32,128]{2,1,0:T(8,128)(2,1)S(1)}, u32[]{:S(2)}, u32[]{:S(2)}) collective-permute-start(bf16[6,32,128]{2,1,0:T(8,128)(2,1)S(1)} %get-tuple-element.40), channel_id=1, source_target_pairs={{0,24},{4,28},{8,16},{12,20},{16,8},{20,12},{24,0},{28,4},{1,25},{... | collective-permute-start | bytes 147464 | tf_op jit(solution)/shard_map/ppermute | solution.py:317
  114.8 6.3 %collective-permute-start.17 = (bf16[6,32,128]{2,1,0:T(8,128)(2,1)S(1)}, bf16[6,32,128]{2,1,0:T(8,128)(2,1)S(1)}, u32[]{:S(2)}, u32[]{:S(2)}) collective-permute-start(bf16[6,32,128]{2,1,0:T(8,128)(2,1)S(1)} %get-tuple-element.41), channel_id=1, source_target_pairs={{0,16},{4,20},{8,24},{12,28},{16,0},{20,4},{24,8},{28,12},{1,17},{... | collective-permute-start | bytes 147464 | tf_op jit(solution)/shard_map/ppermute | solution.py:317
  114.8 6.3 %collective-permute-start.16 = (bf16[6,32,128]{2,1,0:T(8,128)(2,1)S(1)}, bf16[6,32,128]{2,1,0:T(8,128)(2,1)S(1)}, u32[]{:S(2)}, u32[]{:S(2)}) collective-permute-start(bf16[6,32,128]{2,1,0:T(8,128)(2,1)S(1)} %get-tuple-element.39), channel_id=1, source_target_pairs={{0,8},{4,12},{8,0},{12,4},{16,24},{20,28},{24,16},{28,20},{1,9},{5... | collective-permute-start | bytes 147464 | tf_op jit(solution)/shard_map/ppermute | solution.py:317
  121.1 1.9 %collective-permute-start.19 = (bf16[6,32,128]{2,1,0:T(8,128)(2,1)S(1)}, bf16[6,32,128]{2,1,0:T(8,128)(2,1)S(1)}, u32[]{:S(2)}, u32[]{:S(2)}) collective-permute-start(bf16[6,32,128]{2,1,0:T(8,128)(2,1)S(1)} %fusion.7.refs_0_), channel_id=1, source_target_pairs={{0,1},{1,0},{2,3},{3,2},{4,5},{5,4},{6,7},{7,6},{8,9},{9,8},{10,11... | collective-permute-start | bytes 147464 | tf_op jit(solution)/shard_map/ppermute | solution.py:320
  121.2 4.2 %collective-permute-start.20 = (bf16[6,32,128]{2,1,0:T(8,128)(2,1)S(1)}, bf16[6,32,128]{2,1,0:T(8,128)(2,1)S(1)}, u32[]{:S(2)}, u32[]{:S(2)}) collective-permute-start(bf16[6,32,128]{2,1,0:T(8,128)(2,1)S(1)} %fusion.7.refs_0_), channel_id=1, source_target_pairs={{0,2},{1,3},{2,0},{3,1},{4,6},{5,7},{6,4},{7,5},{8,10},{9,11},{10,... | collective-permute-start | bytes 147464 | tf_op jit(solution)/shard_map/ppermute | solution.py:320
  122.7 3.7 %collective-permute-start.21 = (bf16[6,32,128]{2,1,0:T(8,128)(2,1)S(1)}, bf16[6,32,128]{2,1,0:T(8,128)(2,1)S(1)}, u32[]{:S(2)}, u32[]{:S(2)}) collective-permute-start(bf16[6,32,128]{2,1,0:T(8,128)(2,1)S(1)} %fusion.7.refs_0_), channel_id=1, source_target_pairs={{0,3},{1,2},{2,1},{3,0},{4,7},{5,6},{6,5},{7,4},{8,11},{9,10},{10,... | collective-permute-start | bytes 147464 | tf_op jit(solution)/shard_map/ppermute | solution.py:320
  (10 other events, 32.9 us)
